TPU v7x, 256 devices: a whole 4x4x8 slice. The times are simulated.
256 devices in a mesh: noise: 16 (over z_lo, x), qi: 2 (over core), kj: 8 (over z_hi, y).
Axes of the slice: x: 4, y: 4, z: 8 (z_hi: 2, z_lo: 4; z = z_hi * 4 + z_lo), core: 2. Of those that a mesh axis runs over, the one named last changes fastest.
Arguments:
- pair_rep: bfloat16 [512, 2, 256, 128], P('qi', None, 'kj'), may hold values from -6 to 6
- query_rows: bfloat16 [16, 512, 768], P('noise', 'qi'), may hold values from -10 to 10
- key_rows: bfloat16 [16, 2, 256, 768], P('noise', None, 'kj'), may hold values from -10 to 10
- value_rows: bfloat16 [16, 2, 256, 768], P('noise', None, 'kj'), may hold values from -6 to 6
- output_grad: bfloat16 [16, 512, 768], P('noise', 'qi'), may hold values from -96 to 96
- gain_first: float32 [128], replicated, may hold values from 0.5 to 1.5
- gate_weight: bfloat16 [128, 512], replicated, may hold values from -0.5 to 0.5
- up_weight: bfloat16 [128, 512], replicated, may hold values from -0.5 to 0.5
- down_weight: bfloat16 [512, 128], replicated, may hold values from -0.25 to 0.25
- gain_second: float32 [128], replicated, may hold values from 0.5 to 1.5
- head_weight: bfloat16 [128, 16], replicated, may hold values from -0.5 to 0.5
Outputs:
- query_grad: bfloat16 [16, 512, 768], P('noise', ('qi', 'kj'))
- key_grad: bfloat16 [16, 512, 768], P('noise', ('qi', 'kj'))
- value_grad: bfloat16 [16, 512, 768], P('noise', ('qi', 'kj'))
- pair_grad: bfloat16 [2, 16, 16, 2, 256, 128], P('qi', 'noise', None, None, 'kj')
- gate_grad: float32 [128, 512], replicated
- up_grad: float32 [128, 512], replicated
- down_grad: float32 [512, 128], replicated
- head_grad: float32 [128, 16], replicated
- first_grad: float32 [128], replicated
- second_grad: float32 [128], replicated
All inputs are finite; a program needn't handle non-finite values.
Results may differ from a plain program's by a relative error of at most 0.011.
Values may be sent and summed in bfloat16 or wider, within the bound.
No kernel may reach another device: no remote copies, remote signals or barrier semaphores. Data moves between devices by JAX's collectives and lax.ppermute only.
A program may use at most 64 MiB of HBM per device.

v0:
```python
import jax
import jax.numpy as jnp
from jax import lax
from jax.sharding import PartitionSpec as P

HEADS = 16
HEAD_DIM = 48


epsilon = 1e-05


def merged(value, axis, combine):
    everything = jax.tree.map(lambda part: lax.all_gather(part, axis), value)
    initial = jax.tree.map(lambda part: part[0], everything)

    def hop(k, so_far):
        return combine(so_far, jax.tree.map(lambda part: part[k], everything))

    return lax.fori_loop(1, lax.axis_size(axis), hop, initial)


def layer_norm(values, gain_vec):
    center = values - jnp.mean(values, axis=1, keepdims=True)
    inverse = lax.rsqrt(jnp.mean(center * center, axis=1, keepdims=True) + epsilon)
    normed = center * inverse
    return (normed, inverse, normed * gain_vec)


def norm_backward(normed_grad, normed, inverse):
    first_mean = jnp.mean(normed_grad, axis=1, keepdims=True)
    second_mean = jnp.mean(normed_grad * normed, axis=1, keepdims=True)
    return inverse * (normed_grad - first_mean - normed * second_mean)


def transition_forward(cells, params):
    gain_first, gate_weight, up_weight, down_weight, gain_second, head_weight = params
    inputs = cells.astype(jnp.float32)
    pre_normed, pre_inverse, pre_scaled = layer_norm(inputs, gain_first)
    pre_lowered = pre_scaled.astype(jnp.bfloat16)
    gate_pre = jnp.dot(pre_lowered, gate_weight, preferred_element_type=jnp.float32)
    up_pre = jnp.dot(pre_lowered, up_weight, preferred_element_type=jnp.float32)
    gate_sigmoid = jax.nn.sigmoid(gate_pre)
    hidden = (gate_pre * gate_sigmoid * up_pre).astype(jnp.bfloat16)
    updated = inputs + jnp.dot(hidden, down_weight, preferred_element_type=jnp.float32)
    post_normed, post_inverse, post_scaled = layer_norm(updated, gain_second)
    post_lowered = post_scaled.astype(jnp.bfloat16)
    bias_heads = jnp.einsum(
        "mc,ch->hm", post_lowered, head_weight, preferred_element_type=jnp.float32
    ).astype(jnp.bfloat16)
    saved_state = (
        pre_normed,
        pre_inverse,
        pre_lowered,
        gate_pre,
        up_pre,
        gate_sigmoid,
        hidden,
        post_normed,
        post_inverse,
        post_lowered,
    )
    return (bias_heads, saved_state)


def transition_backward(saved_state, grad_heads, params):
    gain_first, gate_weight, up_weight, down_weight, gain_second, head_weight = params
    (
        pre_normed,
        pre_inverse,
        pre_lowered,
        gate_pre,
        up_pre,
        gate_sigmoid,
        hidden,
        post_normed,
        post_inverse,
        post_lowered,
    ) = saved_state
    grad_low = grad_heads.astype(jnp.bfloat16)
    post_scaled = jnp.einsum("hm,ch->mc", grad_low, head_weight, preferred_element_type=jnp.float32)
    head_part = jnp.einsum("mc,hm->ch", post_lowered, grad_low, preferred_element_type=jnp.float32)
    second_part = jnp.sum(post_scaled * post_normed, axis=0)
    updated_grad = norm_backward(post_scaled * gain_second, post_normed, post_inverse)
    updated_low = updated_grad.astype(jnp.bfloat16)
    down_part = jnp.einsum("mf,mc->fc", hidden, updated_low, preferred_element_type=jnp.float32)
    hidden_grad = jnp.einsum(
        "mc,fc->mf", updated_low, down_weight, preferred_element_type=jnp.float32
    )
    gate_low = (
        hidden_grad * up_pre * gate_sigmoid * (1.0 + gate_pre * (1.0 - gate_sigmoid))
    ).astype(jnp.bfloat16)
    up_low = (hidden_grad * gate_pre * gate_sigmoid).astype(jnp.bfloat16)
    gate_part = jnp.einsum("mc,mf->cf", pre_lowered, gate_low, preferred_element_type=jnp.float32)
    up_part = jnp.einsum("mc,mf->cf", pre_lowered, up_low, preferred_element_type=jnp.float32)
    pre_scaled = jnp.einsum(
        "mf,cf->mc", gate_low, gate_weight, preferred_element_type=jnp.float32
    ) + jnp.einsum("mf,cf->mc", up_low, up_weight, preferred_element_type=jnp.float32)
    first_part = jnp.sum(pre_scaled * pre_normed, axis=0)
    inputs_grad = norm_backward(pre_scaled * gain_first, pre_normed, pre_inverse)
    pair_low = (updated_grad + inputs_grad).astype(jnp.bfloat16)
    return (pair_low, (gate_part, up_part, down_part, head_part, first_part, second_part))


def combine_stats(earlier, later):
    early_max, early_sum, early_dot = earlier
    late_max, late_sum, late_dot = later
    largest = jnp.maximum(early_max, late_max)
    early_scale = jnp.exp(early_max - largest)
    late_scale = jnp.exp(late_max - largest)
    return (
        largest,
        early_sum * early_scale + late_sum * late_scale,
        early_dot * early_scale + late_dot * late_scale,
    )


def local(
    pair_rep,
    query_rows,
    key_rows,
    value_rows,
    output_grad,
    gain_first,
    gate_weight,
    up_weight,
    down_weight,
    gain_second,
    head_weight,
):
    params = (gain_first, gate_weight, up_weight, down_weight, gain_second, head_weight)
    tile_rows, block_count, block_rows, channels = pair_rep.shape
    key_count = block_count * block_rows
    feature_width = query_rows.shape[2]
    score_scale = HEAD_DIM ** (-0.5)
    noise_count = lax.axis_size("noise")
    share_rows = tile_rows // noise_count
    own_start = lax.axis_index("noise") * share_rows
    pair_tile = pair_rep.reshape(tile_rows, key_count, channels)
    own_cells = lax.dynamic_slice_in_dim(pair_tile, own_start, share_rows, 0).reshape(
        share_rows * key_count, channels
    )

    def block_bias(cells):
        return transition_forward(cells, params)[0]

    row_blocks = pair_tile.reshape(noise_count, share_rows * key_count, channels)
    bias_blocks = lax.map(block_bias, row_blocks)
    bias_tile = (
        bias_blocks.reshape(noise_count, HEADS, share_rows, key_count)
        .transpose(1, 3, 0, 2)
        .reshape(HEADS, key_count, tile_rows)
    )
    saved_state = transition_forward(own_cells, params)[1]
    query_tile = query_rows[0].reshape(tile_rows, HEADS, HEAD_DIM)
    keys_tile = key_rows[0].reshape(key_count, HEADS, HEAD_DIM)
    values_tile = value_rows[0].reshape(key_count, HEADS, HEAD_DIM)
    grad_tile = output_grad[0].reshape(tile_rows, HEADS, HEAD_DIM)
    scores = jnp.einsum(
        "qhd,khd->hkq", query_tile, keys_tile, preferred_element_type=jnp.float32
    ) * score_scale + bias_tile.astype(jnp.float32)
    local_max = jnp.max(scores, axis=1)
    local_expo = jnp.exp(scores - local_max[:, None, :])
    attend_grad = jnp.einsum(
        "qhd,khd->hkq", grad_tile, values_tile, preferred_element_type=jnp.float32
    )
    local_sum = jnp.sum(local_expo, axis=1)
    local_dot = jnp.sum(local_expo * attend_grad, axis=1)
    row_max, row_sum, row_dot = merged((local_max, local_sum, local_dot), "kj", combine_stats)
    attend = jnp.exp(scores - row_max[:, None, :]) / row_sum[:, None, :]
    score_grad = attend * (attend_grad - (row_dot / row_sum)[:, None, :])
    score_low = score_grad.astype(jnp.bfloat16)
    attend_low = attend.astype(jnp.bfloat16)
    product = (
        jnp.einsum("hkq,khd->qhd", score_low, keys_tile, preferred_element_type=jnp.float32)
        * score_scale
    )
    query_sum = lax.psum_scatter(
        product.reshape(block_rows * lax.axis_size("kj"), feature_width),
        "kj",
        scatter_dimension=0,
        tiled=True,
    )
    row_count = block_rows * lax.axis_size("qi")
    key_part = (
        jnp.einsum("hkq,qhd->khd", score_low, query_tile, preferred_element_type=jnp.float32)
        * score_scale
    )
    value_part = jnp.einsum(
        "hkq,qhd->khd", attend_low, grad_tile, preferred_element_type=jnp.float32
    )
    key_sum = lax.psum_scatter(
        jnp.concatenate(
            (
                key_part.reshape(row_count, feature_width),
                value_part.reshape(row_count, feature_width),
            ),
            1,
        ),
        "qi",
        scatter_dimension=0,
        tiled=True,
    )
    query_grad = query_sum.astype(jnp.bfloat16)[None]
    key_grad = key_sum[:, :feature_width].astype(jnp.bfloat16)[None]
    value_grad = key_sum[:, feature_width:].astype(jnp.bfloat16)[None]
    summed = lax.psum(score_grad, "noise")
    share_grad = lax.dynamic_slice_in_dim(summed, own_start, share_rows, 2)
    grad_heads = share_grad.transpose(0, 2, 1).reshape(HEADS, share_rows * key_count)
    pair_low, weight_parts = transition_backward(saved_state, grad_heads, params)
    reduced = lax.psum(
        (
            weight_parts[0],
            weight_parts[1],
            weight_parts[2],
            weight_parts[3],
            weight_parts[4],
            weight_parts[5],
        ),
        ("noise", "qi", "kj"),
    )
    tokens = tile_rows * lax.axis_size("qi")
    factor = 1.0 / tokens
    pair_grad = pair_low.reshape(1, 1, share_rows, block_count, block_rows, channels)
    return (
        query_grad,
        key_grad,
        value_grad,
        pair_grad,
        reduced[0] * factor,
        reduced[1] * factor,
        reduced[2] * factor,
        reduced[3] * factor,
        reduced[4] * factor,
        reduced[5] * factor,
    )


def solution(mesh):
    return jax.shard_map(
        local,
        mesh=mesh,
        in_specs=(
            P("qi", None, "kj", None),
            P("noise", "qi", None),
            P("noise", None, "kj", None),
            P("noise", None, "kj", None),
            P("noise", "qi", None),
            P(),
            P(),
            P(),
            P(),
            P(),
            P(),
        ),
        out_specs=(
            P("noise", ("qi", "kj"), None),
            P("noise", ("qi", "kj"), None),
            P("noise", ("qi", "kj"), None),
            P("qi", "noise", None, None, "kj", None),
            P(),
            P(),
            P(),
            P(),
            P(),
            P(),
        ),
        check_vma=False,
    )
```

profile of v0, /device:TPU:1, one launch (start us, length us, event | category | flops | bytes accessed | tf_op | source)
XLA Modules:
  0.0 629.5 jit_solution(5931415006050077510)
XLA Ops:
  8.1 1.2 convert_reduce_fusion.1
  10.0 1.9 multiply_reduce_fusion.7
  12.0 1.8 dynamic-slice_convert_fusion.1
  13.8 1.2 reshape_squeeze.12
  18.0 96.8 %while.29 = (s32[]{:T(128)}, bf16[16,16,1024]{2,1,0:T(8,128)(2,1)}, bf16[16,1024,128]{2,1,0:T(8,128)(2,1)}, f32[128]{0:T(128)}, bf16[128,512]{1,0:T(8,128)(2,1)S...) while((s32[]{:T(128)}, bf16[16,16,1024]{2,1,0:T(8,128)(2,1)}, ...), condition=%wide.region_5.6_spmd, body=%wide.region_0.5_spmd.sunk | while | flops 413419520 | bytes 8377973 | solution.py:148
  20.5 2.0 fusion.104
  22.6 1.5 fusion.105
  25.4 1.2 fusion.103
  26.6 2.0 fusion.104
  28.7 1.5 fusion.105
  32.6 2.0 fusion.104
  34.7 1.5 fusion.105
  37.5 1.2 fusion.103
  38.7 2.0 fusion.104
  40.8 1.5 fusion.105
  44.7 2.0 fusion.104
  46.8 1.5 fusion.105
  50.8 2.0 fusion.104
  52.9 1.5 fusion.105
  56.8 2.0 fusion.104
  58.9 1.5 fusion.105
  61.7 1.2 fusion.103
  62.9 2.0 fusion.104
  65.0 1.5 fusion.105
  68.9 2.0 fusion.104
  71.0 1.5 fusion.105
  73.8 1.2 fusion.103
  75.0 2.0 fusion.104
  77.1 1.5 fusion.105
  79.8 1.2 fusion.103
  81.0 2.0 fusion.104
  83.1 1.5 fusion.105
  87.1 2.0 fusion.104
  89.1 1.5 fusion.105
  93.1 2.0 fusion.104
  95.2 1.5 fusion.105
  99.1 2.0 fusion.104
  101.2 1.5 fusion.105
  105.2 2.0 fusion.104
  107.3 1.5 fusion.105
  111.2 2.0 fusion.104
  113.3 1.5 fusion.105
  114.8 1.6 reshape.146
  116.5 1.5 copy.35
  118.0 2.2 copy.36
  120.6 40.7 %all-gather = f32[128,256]{1,0:T(8,128)S(1)} all-gather(f32[16,256]{1,0:T(8,128)S(1)} %get-tuple-element.302), channel_id=2, replica_groups=mesh['noise'=16,'qi'=2,'kj'=8] {'kj'}, dimensions={0}, use_global_device_ids=true | all-gather | bytes 147456 | tf_op jit(solution)/shard_map/all_gather | solution.py:14
  161.7 37.5 %all-gather.2 = f32[128,256]{1,0:T(8,128)S(1)} all-gather(f32[16,256]{1,0:T(8,128)S(1)} %get-tuple-element.250), channel_id=4, replica_groups=mesh['noise'=16,'qi'=2,'kj'=8] {'kj'}, dimensions={0}, use_global_device_ids=true | all-gather | bytes 147456 | tf_op jit(solution)/shard_map/all_gather | solution.py:14
  199.2 37.4 %all-gather.1 = f32[128,256]{1,0:T(8,128)S(1)} all-gather(f32[16,256]{1,0:T(8,128)S(1)} %get-tuple-element.251), channel_id=3, replica_groups=mesh['noise'=16,'qi'=2,'kj'=8] {'kj'}, dimensions={0}, use_global_device_ids=true | all-gather | bytes 147456 | tf_op jit(solution)/shard_map/all_gather | solution.py:14
  240.6 78.2 %all-reduce.6 = bf16[16,64,256]{2,1,0:T(8,128)(2,1)S(1)} all-reduce(f32[16,64,256]{2,1,0:T(8,128)S(1)} %subtract_multiply_fusion), channel_id=1, replica_groups=mesh['noise'=16,'qi'=2,'kj'=8] {'noise'}, use_global_device_ids=true, to_apply=%region_17.18 | all-reduce | flops 262144 | bytes 1572864 | tf_op jit(solution)/shard_map/psum | solution.py:207
  319.3 1.3 multiply_convert_fusion.7
  323.0 1.6 multiply_reduce_fusion.2
  326.4 1.2 multiply_convert_fusion.3
  331.0 2.1 fusion.34
  333.1 1.8 copy.42
  334.9 1.8 pad_maximum_fusion
  336.7 2.3 copy.40
  340.6 1.6 multiply_reduce_fusion.3
  342.3 106.4 %all-reduce = (f32[128,16]{0,1:T(8,128)S(1)}, f32[128]{0:T(128)S(1)}, f32[128]{0:T(128)S(1)}) all-reduce(f32[128,16]{0,1:T(8,128)S(1)} %fusion.41, f32[128]{0:T(128)S(1)} %get-tuple-element.248, f32[128]{0:T(128)S(1)} %copy-done.24), channel_id=1, replica_groups=mesh['noise'=16,'qi'=2,'kj'=8] {'noise','qi','kj'}, use_global_device_ids=true, to_apply=%region_25.26 | all-reduce | flops 2304 | bytes 18432 | tf_op jit(solution)/shard_map/psum | solution.py:211
  450.3 2.3 add_convert_fusion
  452.6 161.4 %all-reduce.5.cloned.1.call-done = (f32[128,512]{1,0:T(8,128)}, f32[128,512]{1,0:T(8,128)}, f32[512,128]{1,0:T(8,128)}) async-done(((f32[128,512]{1,0:T(8,128)}, f32[128,512]{1,0:T(8,128)}, f32[512,128]{1,0:T(8,128)}), (f32[128,512]{1,0:T(8,128)}, f32[128,512]{1,0:T(8,128)}, f32[512,128]{1,0:T(8,128)})) %all-reduce.5.cloned.1.call-update) | async-done | bytes 786448 | tf_op jit(solution)/shard_map/psum | solution.py:211
  614.0 1.7 broadcast_multiply_fusion.4
  615.7 1.7 broadcast_multiply_fusion.3
  617.3 1.7 broadcast_multiply_fusion.2
  620.6 1.5 convert_bitcast_fusion.1
  (277 shorter events, 55.8 us)
Async XLA Ops:
  8.0 7.9 %copy-start.18 = (bf16[1,2,32,768]{3,2,1,0:T(8,128)(2,1)S(1)}, bf16[1,2,32,768]{3,2,1,0:T(8,128)(2,1)}, u32[]{:S(2)}) copy-start(bf16[1,2,32,768]{3,2,1,0:T(8,128)(2,1)} %param.18) | copy-start | bytes 294916
  8.0 8.9 %copy-start.12 = (bf16[1,256,768]{2,1,0:T(8,128)(2,1)S(1)}, bf16[1,256,768]{2,1,0:T(8,128)(2,1)}, u32[]{:S(2)}) copy-start(bf16[1,256,768]{2,1,0:T(8,128)(2,1)} %param.16) | copy-start | bytes 1179652
  8.0 9.1 %copy-start.13 = (bf16[1,256,768]{2,1,0:T(8,128)(2,1)S(1)}, bf16[1,256,768]{2,1,0:T(8,128)(2,1)}, u32[]{:S(2)}) copy-start(bf16[1,256,768]{2,1,0:T(8,128)(2,1)} %param.19) | copy-start | bytes 1179652
  8.0 10.0 %copy-start = (bf16[128,512]{1,0:T(8,128)(2,1)S(1)}, bf16[128,512]{1,0:T(8,128)(2,1)}, u32[]{:S(2)}) copy-start(bf16[128,512]{1,0:T(8,128)(2,1)} %param.22) | copy-start | bytes 393220
  8.1 10.0 %copy-start.10 = (bf16[128,512]{1,0:T(8,128)(2,1)S(1)}, bf16[128,512]{1,0:T(8,128)(2,1)}, u32[]{:S(2)}) copy-start(bf16[128,512]{1,0:T(8,128)(2,1)} %param.21) | copy-start | bytes 393220
  8.1 10.0 %copy-start.16 = (bf16[128,16]{0,1:T(8,128)(2,1)S(1)}, bf16[128,16]{0,1:T(8,128)(2,1)}, u32[]{:S(2)}) copy-start(bf16[128,16]{0,1:T(8,128)(2,1)} %param.25) | copy-start | bytes 12292
  8.1 605.9 %all-reduce.5.cloned.1.call-start = ((), (), s32[]{:S(2)}) async-start(), calls=%async_computation.4 | async-start | bytes 1572864 | tf_op jit(solution)/shard_map/psum | solution.py:211
  17.1 103.1 %copy-start.3 = (bf16[1,256,768]{1,2,0:T(8,128)(2,1)}, bf16[1,256,768]{1,2,0:T(8,128)(2,1)S(1)}, u32[]{:S(2)}) copy-start(bf16[1,256,768]{1,2,0:T(8,128)(2,1)S(1)} %copy.32) | copy-start | bytes 1179652
  118.0 2.3 copy-start.6
  120.2 41.1 %copy-start.8 = (bf16[1,256,768]{1,2,0:T(8,128)(2,1)S(1)}, bf16[1,256,768]{1,2,0:T(8,128)(2,1)}, u32[]{:S(2)}) copy-start(bf16[1,256,768]{1,2,0:T(8,128)(2,1)} %copy.37) | copy-start | bytes 1179652
  120.2 41.1 %copy-start.9 = (bf16[64,16,48]{2,1,0:T(8,128)(2,1)S(1)}, bf16[64,16,48]{2,1,0:T(8,128)(2,1)}, u32[]{:S(2)}) copy-start(bf16[64,16,48]{2,1,0:T(8,128)(2,1)} %reshape_squeeze.14) | copy-start | bytes 294916
  237.3 1.0 copy-start.4
  237.3 2.0 copy-start.7
  238.3 2.3 copy-start.23
  239.4 79.9 %copy-start.19 = (f32[1024]{0:T(1024)S(1)}, f32[1024]{0:T(1024)}, u32[]{:S(2)}) copy-start(f32[1024]{0:T(1024)} %div.59) | copy-start | bytes 12292
  319.3 3.7 copy-start.14
  321.0 1.0 copy-start.5
  321.0 1.1 copy-start.17
  321.7 1.3 copy-start.22
  323.0 3.4 copy-start.20
  327.6 1.1 copy-start.1
  329.8 289.2 %reduce-scatter.5.cloned.1.call-start = ((), (), s32[]{:S(2)}) async-start(), calls=%async_computation.3 | async-start | bytes 589824 | tf_op jit(solution)/shard_map/reduce_scatter | solution.py:192
  333.1 6.0 copy-start.15
  333.1 6.0 copy-start.21
  334.9 5.3 copy-start.2
  336.7 3.5 copy-start.11
  336.7 283.9 %reduce-scatter.3.cloned.1.call-start = ((), (), s32[]{:S(2)}) async-start(), calls=%async_computation.2 | async-start | bytes 884736 | tf_op jit(solution)/shard_map/reduce_scatter | solution.py:178
  340.2 2.1 copy-start.24
Sparse Core Ops, SparseCore 0:
  329.9 284.0 all-reduce.4
Sparse Core Ops, SparseCore 1:
  336.8 43.1 reduce-scatter.4
  384.3 84.1 reduce-scatter.2
where the time goes:
time: 632 us; the launch traced here: 630 us
  blocking collectives  300 us (47%)
  waiting for transfers between devices  161 us (25%)
  matrix products  90.3 us (14%)
  local copies, waits for them, and re-layouts  35.6 us (6%)
  other arithmetic  24.7 us (4%)
  between operations  15.9 us (3%)
    psum x1, waiting for transfers between devices, local(): lax.psum((weight_parts[0], weight_parts[1], weight_parts[2], weight_parts...  161 us
    all_gather x3, blocking collectives, merged(): everything = jax.tree.map(lambda part: lax.all_gather(part, axis), value)  116 us
    psum x1, blocking collectives, local(): lax.psum((weight_parts[0], weight_parts[1], weight_parts[2], weight_parts...  106 us
    psum x1, blocking collectives, local(): summed = lax.psum(score_grad, 'noise')  78.2 us
    dot_general x17, matrix products, transition_forward(): jnp.dot(hidden, down_weight, preferred_element_type=jnp.float32)  32.3 us
    dot_general x16, matrix products, transition_forward(): jnp.einsum('mc,ch->hm', post_lowered, head_weight, preferred_element_type...  23.8 us
    dot_general x17, matrix products, transition_forward(): up_pre = jnp.dot(pre_lowered, up_weight, preferred_element_type=jnp.float32)  19.6 us
    dynamic_slice x32, local copies, waits for them, and re-layouts, local(): bias_blocks = lax.map(block_bias, row_blocks)  17.8 us
  transfers between devices with their start and end apart: 3, of which 1 were waited for; matrix products, arithmetic and copies ran while one was open for 4% of the time, Pallas kernels for 0%

commit v1 on v0

v1 whole, which is shorter than its diff:
```python
import functools

import jax
import jax.numpy as jnp
from jax import lax
from jax.experimental import pallas as pl
from jax.experimental.pallas import tpu as pltpu
from jax.sharding import Mesh, PartitionSpec as P

HEADS = 16
HEAD_DIM = 48
WIDTH = HEADS * HEAD_DIM
PAIR = 128
FF = 512
KEYS = 64
ROWS = 256
SUB = 16
EPSILON = 1e-05
SCALE = HEAD_DIM**-0.5
CHUNK_ROWS = 56
CHUNKS = 32
F32 = jnp.float32
BF16 = jnp.bfloat16
NOISE = ("zl", "x")
PLANE = ("x", "qi", "y")
COLUMN = ("zh", "zl")

VMEM = pl.BlockSpec(memory_space=pltpu.VMEM)
SMEM = pl.BlockSpec(memory_space=pltpu.SMEM)
PARAMS = pltpu.CompilerParams(vmem_limit_bytes=48 * 1024 * 1024)


def dot(left, right, dims):
    return lax.dot_general(left, right, (dims, ((), ())), preferred_element_type=F32)


NN = ((1,), (0,))
NT = ((1,), (1,))
TN = ((0,), (0,))


def layer_norm(values):
    center = values - jnp.mean(values, axis=1, keepdims=True)
    inverse = lax.rsqrt(jnp.mean(center * center, axis=1, keepdims=True) + EPSILON)
    return center * inverse, inverse


def norm_backward(grad, normed, inverse):
    first = jnp.mean(grad, axis=1, keepdims=True)
    second = jnp.mean(grad * normed, axis=1, keepdims=True)
    return inverse * (grad - first - normed * second)


def chunk_cells(read_row, chunk):
    slabs = [
        read_row(half * 8 + 2 * chunk + step) for step in range(2) for half in range(2)
    ]
    return jnp.concatenate(slabs, axis=0)


def bias_kernel(place, pair, gain1, gate_w, up_w, down_w, gain2, head_t, out, rows):
    for chunk in range(4):
        cells = chunk_cells(lambda r: pair[r].reshape(KEYS, PAIR), chunk).astype(F32)
        normed, _ = layer_norm(cells)
        lowered = (normed * gain1[...]).astype(BF16)
        gate = dot(lowered, gate_w[...], NN)
        up = dot(lowered, up_w[...], NN)
        hidden = (gate * jax.nn.sigmoid(gate) * up).astype(BF16)
        updated = cells + dot(hidden, down_w[...], NN)
        post, _ = layer_norm(updated)
        post_low = (post * gain2[...]).astype(BF16)
        bias = dot(head_t[...], post_low, NT)
        rows[pl.ds(2 * chunk, HEADS, stride=8), :] = bias[:, :128]
        rows[pl.ds(2 * chunk + 1, HEADS, stride=8), :] = bias[:, 128:]
    out[0] = rows[...].astype(BF16)


def head_mask(shape, head):
    column = lax.broadcasted_iota(jnp.int32, shape, 1)
    return (column >= head * HEAD_DIM) & (column < (head + 1) * HEAD_DIM)


def spread_heads(tile):
    wide = tile.astype(F32)
    parts = [
        jnp.where(head_mask(wide.shape, h), wide, 0.0).astype(BF16) for h in range(HEADS)
    ]
    return jnp.concatenate(parts, axis=0)


def permute_rows(tile):
    width = tile.shape[1]
    wide = tile.astype(F32).reshape(16, 2, 8, width)
    parts = [wide[:, half].reshape(128, width) for half in range(2)]
    return jnp.concatenate(parts, axis=0).astype(BF16)


def product_kernel(query, grad, keys, values, scores, attend, query_out, grad_out, keys_out):
    query_p = permute_rows(query[...])
    grad_p = permute_rows(grad[...])
    query_out[...] = query_p
    grad_out[...] = grad_p
    wide_keys = spread_heads(keys[...].reshape(KEYS, WIDTH))
    keys_out[...] = wide_keys
    scores[...] = dot(wide_keys, query_p, NT) * SCALE
    wide_values = spread_heads(values[...].reshape(KEYS, WIDTH))
    attend[...] = dot(wide_values, grad_p, NT)


def stats_kernel(place, scores, attend, own, first, second, third, expo, stats, wide):
    x = place[1]
    for shift, piece in enumerate((own, first, second, third)):
        origin = lax.rem(x + 4 - shift, 4)
        for zl in range(4):
            wide[zl, origin] = piece[zl].astype(F32)
    for h in range(HEADS):
        block = wide[:, :, 8 * h : 8 * h + 8, :].reshape(128, 128).T
        bias = jnp.concatenate([block[:KEYS], block[KEYS:]], axis=1)
        rows = slice(h * KEYS, (h + 1) * KEYS)
        total = scores[rows, :] + bias
        largest = jnp.max(total, axis=0, keepdims=True)
        powers = jnp.exp(total - largest)
        expo[rows, :] = powers
        stats[h : h + 1, :] = largest
        stats[HEADS + h : HEADS + h + 1, :] = jnp.sum(powers, axis=0, keepdims=True)
        stats[2 * HEADS + h : 2 * HEADS + h + 1, :] = jnp.sum(
            powers * attend[rows, :], axis=0, keepdims=True
        )


def grad_kernel(stats, gathered, expo, attend, send, score_low, attend_low):
    peers = [gathered[j] for j in range(8)]
    largest = functools.reduce(jnp.maximum, [p[:HEADS] for p in peers])
    total = jnp.zeros((HEADS, ROWS), F32)
    weighted = jnp.zeros((HEADS, ROWS), F32)
    for p in peers:
        factor = jnp.exp(p[:HEADS] - largest)
        total = total + p[HEADS : 2 * HEADS] * factor
        weighted = weighted + p[2 * HEADS :] * factor
    factor = jnp.exp(stats[:HEADS, :] - largest) / total
    delta = weighted / total
    for pair in range(HEADS // 2):
        blocks = []
        for h in (2 * pair, 2 * pair + 1):
            rows = slice(h * KEYS, (h + 1) * KEYS)
            weights = expo[rows, :] * factor[h : h + 1]
            score = weights * (attend[rows, :] - delta[h : h + 1])
            score_low[rows, :] = score.astype(BF16)
            attend_low[rows, :] = weights.astype(BF16)
            block = jnp.concatenate([score[:, :128], score[:, 128:]], axis=0).T
            blocks.append(block.reshape(16, 8, 128))
        send[:, 16 * pair : 16 * pair + 16, :] = jnp.concatenate(blocks, axis=1).astype(BF16)


def rows_kernel(place, score_low, attend_low, query, grad, keys, query_send, kv_send):
    y, zh, qi = place[2], place[3], place[4]
    product = dot(score_low[...], keys[...], TN) * SCALE
    for target in range(8):
        rel_z = lax.rem(target // 4 + zh, 2)
        rel_y = lax.rem(target % 4 + 4 - y, 4)
        parts = []
        for block in (2 * target, 2 * target + 1):
            for half in range(2):
                start = half * 128 + block * 8
                parts.append(product[start : start + 8])
        query_send[rel_z, rel_y] = jnp.concatenate(parts, axis=0).astype(BF16)
    for which, (low, rows) in enumerate(((score_low, query), (attend_low, grad))):
        result = jnp.zeros((KEYS, WIDTH), F32)
        for quad in range(4):
            part = dot(low[quad * 256 : quad * 256 + 256, :], rows[...], NN)
            for step in range(4):
                piece = part[step * KEYS : (step + 1) * KEYS]
                mask = head_mask(piece.shape, quad * 4 + step)
                result = result + jnp.where(mask, piece, 0.0)
        if which == 0:
            result = result * SCALE
        for a in range(2):
            rel = lax.rem(a + qi, 2)
            kv_send[rel, :, which * WIDTH : (which + 1) * WIDTH] = result[a * 32 : a * 32 + 32]


def pair_kernel(
    place, pair, received, gain1, gate_w, up_w, down_w, gain2, head_t, pair_out, weights,
    rows, pre_s, gate_s, up_s, hidden_s, updated_s, post_s, low_s,
):
    rows[...] = jnp.sum(received[...].astype(F32), axis=0)
    first_sum = jnp.zeros((1, PAIR), F32)
    second_sum = jnp.zeros((1, PAIR), F32)
    for chunk in range(4):
        span = slice(chunk * 256, (chunk + 1) * 256)
        cells = chunk_cells(lambda r: pair[r].reshape(KEYS, PAIR), chunk).astype(F32)
        pre_normed, pre_inverse = layer_norm(cells)
        lowered = (pre_normed * gain1[...]).astype(BF16)
        pre_s[span, :] = lowered
        gate = dot(lowered, gate_w[...], NN)
        up = dot(lowered, up_w[...], NN)
        sigmoid = jax.nn.sigmoid(gate)
        silu = gate * sigmoid
        hidden = (silu * up).astype(BF16)
        hidden_s[span, :] = hidden
        updated = cells + dot(hidden, down_w[...], NN)
        post_normed, post_inverse = layer_norm(updated)
        post_s[span, :] = (post_normed * gain2[...]).astype(BF16)
        low = jnp.concatenate(
            [rows[pl.ds(2 * chunk + step, HEADS, stride=8), :] for step in range(2)], axis=1
        ).astype(BF16)
        low_s[:, span] = low
        post_scaled = dot(low, head_t[...], TN)
        second_sum = second_sum + jnp.sum(post_scaled * post_normed, axis=0, keepdims=True)
        updated_grad = norm_backward(post_scaled * gain2[...], post_normed, post_inverse)
        updated_low = updated_grad.astype(BF16)
        updated_s[span, :] = updated_low
        hidden_grad = dot(updated_low, down_w[...], NT)
        gate_low = (hidden_grad * up * sigmoid * (1.0 + gate * (1.0 - sigmoid))).astype(BF16)
        up_low = (hidden_grad * silu).astype(BF16)
        gate_s[span, :] = gate_low
        up_s[span, :] = up_low
        pre_scaled = dot(gate_low, gate_w[...], NT) + dot(up_low, up_w[...], NT)
        first_sum = first_sum + jnp.sum(pre_scaled * pre_normed, axis=0, keepdims=True)
        inputs_grad = norm_backward(pre_scaled * gain1[...], pre_normed, pre_inverse)
        result = (updated_grad + inputs_grad).astype(BF16)
        for step in range(2):
            for half in range(2):
                start = step * 128 + half * KEYS
                slab = result[start : start + KEYS]
                pair_out[half * 8 + 2 * chunk + step] = slab.reshape(2, 32, PAIR)
    gate_part = dot(pre_s[...], gate_s[...], TN).astype(BF16)
    up_part = dot(pre_s[...], up_s[...], TN).astype(BF16)
    for block in range(4):
        lanes = slice(block * 128, (block + 1) * 128)
        weights[block * 128 : (block + 1) * 128, :] = gate_part[:, lanes]
        weights[512 + block * 128 : 512 + (block + 1) * 128, :] = up_part[:, lanes]
    weights[1024:1536, :] = dot(hidden_s[...], updated_s[...], TN).astype(BF16)
    weights[1536:1552, :] = dot(low_s[...], post_s[...], NN).astype(BF16)
    gains = jnp.concatenate([first_sum, second_sum, jnp.zeros((14, PAIR), F32)], axis=0)
    weights[1552:1568, :] = gains.astype(BF16)
    weights[1568:, :] = jnp.zeros((CHUNK_ROWS * CHUNKS - 1568, PAIR), BF16)


def shifted(value, axis, shift):
    size = lax.axis_size(axis)
    return lax.ppermute(value, axis, [(i, (i + shift) % size) for i in range(size)])


def all_to_all(value, axes):
    return lax.all_to_all(value, axes, 0, 0, tiled=True)


def local(
    pair_rep, query_rows, key_rows, value_rows, output_grad,
    gain_first, gate_weight, up_weight, down_weight, gain_second, head_weight,
):
    x, zl = lax.axis_index("x"), lax.axis_index("zl")
    y, zh, qi = lax.axis_index("y"), lax.axis_index("zh"), lax.axis_index("qi")
    place = jnp.stack([zl * 4 + x, x, y, zh, qi]).astype(jnp.int32)
    params = (
        gain_first[None], gate_weight, up_weight, down_weight, gain_second[None], head_weight.T,
    )

    def shape(dims, dtype):
        return jax.ShapeDtypeStruct(dims, dtype)

    def whole(array):
        return pl.BlockSpec(array.shape, lambda i, p: (0,) * array.ndim)

    own = pl.pallas_call(
        bias_kernel,
        grid_spec=pltpu.PrefetchScalarGridSpec(
            num_scalar_prefetch=1,
            grid=(4,),
            in_specs=[
                pl.BlockSpec((SUB, 2, 32, PAIR), lambda i, p: (i * 4 + p[1], 0, 0, 0)),
                *[whole(a) for a in params],
            ],
            out_specs=pl.BlockSpec((1, 128, 128), lambda i, p: (i, 0, 0)),
            scratch_shapes=[pltpu.VMEM((128, 128), F32)],
        ),
        out_shape=shape((4, 128, 128), BF16),
        compiler_params=PARAMS,
        name="pair_bias",
    )(place, pair_rep, *params)
    pieces = [shifted(own, "x", s) for s in (1, 2, 3)]

    big = shape((HEADS * KEYS, ROWS), F32)
    small = shape((HEADS * KEYS, ROWS), BF16)
    flat = shape((ROWS, WIDTH), BF16)
    scores, attend, query_p, grad_p, wide_keys = pl.pallas_call(
        product_kernel,
        in_specs=[VMEM] * 4,
        out_specs=[VMEM] * 5,
        out_shape=[big, big, flat, flat, shape((HEADS * KEYS, WIDTH), BF16)],
        compiler_params=PARAMS,
        name="products",
    )(query_rows[0], output_grad[0], key_rows[0], value_rows[0])

    expo, stats = pl.pallas_call(
        stats_kernel,
        in_specs=[SMEM] + [VMEM] * 6,
        out_specs=[VMEM] * 2,
        out_shape=[big, shape((3 * HEADS, ROWS), F32)],
        scratch_shapes=[pltpu.VMEM((4, 4, 128, 128), F32)],
        compiler_params=PARAMS,
        name="softmax_stats",
    )(place, scores, attend, own, *pieces)

    gathered = all_to_all(jnp.broadcast_to(stats[None], (8, *stats.shape)), ("zh", "y"))

    send, score_low, attend_low = pl.pallas_call(
        grad_kernel,
        in_specs=[VMEM] * 4,
        out_specs=[VMEM] * 3,
        out_shape=[shape((16, 128, 128), BF16), small, small],
        compiler_params=PARAMS,
        name="score_grads",
    )(stats, gathered, expo, attend)

    received = all_to_all(send, NOISE)

    query_send, kv_send = pl.pallas_call(
        rows_kernel,
        in_specs=[SMEM] + [VMEM] * 5,
        out_specs=[VMEM] * 2,
        out_shape=[shape((2, 4, 32, WIDTH), BF16), shape((2, 32, 2 * WIDTH), F32)],
        compiler_params=PARAMS,
        name="row_grads",
    )(place, score_low, attend_low, query_p, grad_p, wide_keys)

    half = query_send[0].astype(F32) + shifted(query_send[1], "zh", 1).astype(F32)
    quarter = half.astype(BF16)
    query_sum = half[0]
    for s in (1, 2, 3):
        query_sum = query_sum + shifted(quarter[s], "y", s).astype(F32)
    query_grad = query_sum.astype(BF16)[None]
    kv_sum = (kv_send[0] + shifted(kv_send[1], "qi", 1)).astype(BF16)
    key_grad = kv_sum[None, :, :WIDTH]
    value_grad = kv_sum[None, :, WIDTH:]

    weight_rows = CHUNK_ROWS * CHUNKS
    pair_low, weights = pl.pallas_call(
        pair_kernel,
        grid_spec=pltpu.PrefetchScalarGridSpec(
            num_scalar_prefetch=1,
            grid=(1,),
            in_specs=[
                pl.BlockSpec((SUB, 2, 32, PAIR), lambda i, p: (p[0], 0, 0, 0)),
                whole(received),
                *[whole(a) for a in params],
            ],
            out_specs=[
                pl.BlockSpec((SUB, 2, 32, PAIR), lambda i, p: (0, 0, 0, 0)),
                pl.BlockSpec((weight_rows, PAIR), lambda i, p: (0, 0)),
            ],
            scratch_shapes=[
                pltpu.VMEM((128, 128), F32),
                pltpu.VMEM((1024, PAIR), BF16),
                pltpu.VMEM((1024, FF), BF16),
                pltpu.VMEM((1024, FF), BF16),
                pltpu.VMEM((1024, FF), BF16),
                pltpu.VMEM((1024, PAIR), BF16),
                pltpu.VMEM((1024, PAIR), BF16),
                pltpu.VMEM((HEADS, 1024), BF16),
            ],
        ),
        out_shape=[shape((SUB, 2, 32, PAIR), BF16), shape((weight_rows, PAIR), BF16)],
        compiler_params=PARAMS,
        name="pair_backward",
    )(place, pair_rep, received, *params)
    pair_grad = pair_low[None, None]

    parts = all_to_all(weights.reshape(CHUNKS, CHUNK_ROWS, PAIR), PLANE)
    share = jnp.sum(parts.astype(F32), axis=0).astype(BF16)
    columns = all_to_all(jnp.broadcast_to(share[None], (8, *share.shape)), COLUMN)
    total = jnp.sum(columns.astype(F32), axis=0).astype(BF16)
    everything = all_to_all(jnp.broadcast_to(total[None], (CHUNKS, *total.shape)), PLANE)
    factor = 1.0 / 512
    table = everything.reshape(weight_rows, PAIR).astype(F32) * factor

    def wide_rows(start):
        block = table[start : start + 512].reshape(4, 128, 128)
        return block.transpose(1, 0, 2).reshape(PAIR, FF)

    return (
        query_grad,
        key_grad,
        value_grad,
        pair_grad,
        wide_rows(0),
        wide_rows(512),
        table[1024:1536],
        table[1536:1552].T,
        table[1552],
        table[1553],
    )


def solution(mesh):
    fine = Mesh(mesh.devices.reshape(4, 4, 2, 2, 4), ("zl", "x", "qi", "zh", "y"))
    kj = ("zh", "y")
    return jax.shard_map(
        local,
        mesh=fine,
        in_specs=(
            P("qi", None, kj, None),
            P(NOISE, "qi", None),
            P(NOISE, None, kj, None),
            P(NOISE, None, kj, None),
            P(NOISE, "qi", None),
            P(),
            P(),
            P(),
            P(),
            P(),
            P(),
        ),
        out_specs=(
            P(NOISE, ("qi", "zh", "y"), None),
            P(NOISE, ("qi", "zh", "y"), None),
            P(NOISE, ("qi", "zh", "y"), None),
            P("qi", NOISE, None, None, kj, None),
            P(),
            P(),
            P(),
            P(),
            P(),
            P(),
        ),
        check_vma=False,
    )
```

time: 632 us -> 145 us (0.23)
  blocking collectives: 300 us -> 22.2 us
  waiting for transfers between devices: 161 us -> 35.2 us
  matrix products: 90.3 us -> 0 us
  starting transfers between devices: 0.13 us -> 43.7 us
  other arithmetic: 24.7 us -> 0.88 us
  Pallas kernels: 0 us -> 23.8 us
  local copies, waits for them, and re-layouts: 35.6 us -> 17.4 us
  between operations: 15.9 us -> 0.94 us
    psum x2 -> x0, blocking collectives: 185 us -> none  [the longest x1 106 us: local(): lax.psum((weight_parts[0], weight_parts[1], weight_parts[2], weight_parts...]
    psum x1 -> x0, waiting for transfers between devices: 161 us -> none  [local(): lax.psum((weight_parts[0], weight_parts[1], weight_parts[2], weight_parts...]
    all_gather x3 -> x0, blocking collectives: 116 us -> none  [merged(): everything = jax.tree.map(lambda part: lax.all_gather(part, axis), value)]
    dot_general x64 -> x0, matrix products: 90.3 us -> none  [the longest x17 32.3 us: transition_forward(): jnp.dot(hidden, down_weight, preferred_element_type=jnp.float32)]
    all_to_all x0 -> x4, starting transfers between devices: none -> 32.3 us  [all_to_all(): return lax.all_to_all(value, axes, 0, 0, tiled=True)]
    all_to_all x0 -> x4, waiting for transfers between devices: none -> 28.7 us  [all_to_all(): return lax.all_to_all(value, axes, 0, 0, tiled=True)]
    pallas_call x0 -> x6, Pallas kernels: none -> 23.8 us  [the longest x1 12.5 us: local(): pl.pallas_call(bias_kernel, grid_spec=pltpu.PrefetchScalarGridSpec(num_sc...]
    all_to_all x0 -> x1, blocking collectives: none -> 22.2 us  [all_to_all(): return lax.all_to_all(value, axes, 0, 0, tiled=True)]
  transfers between devices with their start and end apart: 3 -> 12, of which waited for: 1 -> 7; matrix products, arithmetic and copies ran while one was open for 4% -> 2% of each run, Pallas kernels for 0% -> 6%
where the time goes in v1:
time: 145 us; the launch traced here: 144 us
  starting transfers between devices  43.7 us (30%)
  waiting for transfers between devices  35.2 us (24%)
  Pallas kernels  23.8 us (16%)
  blocking collectives  22.2 us (15%)
  local copies, waits for them, and re-layouts  17.4 us (12%)
    all_to_all x4, starting transfers between devices, all_to_all(): return lax.all_to_all(value, axes, 0, 0, tiled=True)  32.3 us
    all_to_all x4, waiting for transfers between devices, all_to_all(): return lax.all_to_all(value, axes, 0, 0, tiled=True)  28.7 us
    all_to_all x1, blocking collectives, all_to_all(): return lax.all_to_all(value, axes, 0, 0, tiled=True)  22.2 us
    pallas_call x1, Pallas kernels, local(): pl.pallas_call(bias_kernel, grid_spec=pltpu.PrefetchScalarGridSpec(num_sc...  12.5 us
    unnamed x52, local copies, waits for them, and re-layouts  12.4 us
    ppermute x8, starting transfers between devices, shifted(): lax.ppermute(value, axis, [(i, (i + shift) % size) for i in range(size)])  11.4 us
    ppermute x8, waiting for transfers between devices, shifted(): lax.ppermute(value, axis, [(i, (i + shift) % size) for i in range(size)])  6.55 us
    pallas_call x1, Pallas kernels, local(): pl.pallas_call(pair_kernel, grid_spec=pltpu.PrefetchScalarGridSpec(num_sc...  5.96 us
  transfers between devices with their start and end apart: 12, of which 7 were waited for; matrix products, arithmetic and copies ran while one was open for 2% of the time, Pallas kernels for 6%

profile of v1, /device:TPU:1, one launch (start us, length us, event | category | flops | bytes accessed | tf_op | source)
XLA Modules:
  0.0 144.1 jit_solution(18333772929802269096)
XLA Ops:
  0.7 0.1 stack.23.place
  0.7 2.2 %copy-done = bf16[256,2,32,128]{3,2,1,0:T(8,128)(2,1)S(1)} copy-done((bf16[256,2,32,128]{3,2,1,0:T(8,128)(2,1)S(1)}, bf16[256,2,32,128]{3,2,1,0:T(8,128)(2,1)}, u32[]{:S(2)}) %copy-start) | copy-done | bytes 4194328
  2.9 0.9 copy-done.2
  3.8 0.9 copy-done.4
  4.7 0.9 copy-done.6
  5.6 0.7 copy-done.20
  6.3 0.7 copy-done.22
  7.0 0.7 copy-done.24
  7.6 12.5 %pair_bias.1.own = bf16[4,128,128]{2,1,0:T(8,128)(2,1)S(1)} custom-call(s32[5]{0:T(128)S(1)} %stack.23.place, bf16[256,2,32,128]{3,2,1,0:T(8,128)(2,1)S(1)} %copy-done, f32[1,128]{1,0:T(1,128)S(1)} %bitcast.76, bf16[128,512]{1,0:T(8,128)(2,1)S(1)} %copy-done.2, bf16[128,512]{1,0:T(8,128)(2,1)S(1)} %copy-done.4, bf16[512,128]{1,0:T(8,128)(2,1)S(1)} %copy-done.6, ...), custom_call_target="tpu_custom_call" | custom-call | tf_op jit(solution)/shard_map/pair_bias/pallas_call | solution.py:266
  20.2 3.4 %collective-permute-start.2 = (bf16[4,128,128]{2,1,0:T(8,128)(2,1)S(1)}, bf16[4,128,128]{2,1,0:T(8,128)(2,1)S(1)}, u32[]{:S(2)}, u32[]{:S(2)}) collective-permute-start(bf16[4,128,128]{2,1,0:T(8,128)(2,1)S(1)} %pair_bias.1.own), channel_id=1, source_target_pairs={{0,48},{16,0},{32,16},{48,32},{1,49},{17,1},{33,17},{49,33},{2,50}... | collective-permute-start | bytes 393224 | tf_op jit(solution)/shard_map/ppermute | solution.py:242
  23.5 0.5 collective-permute-start.1
  24.1 0.6 collective-permute-start
  24.7 0.0 copy-done.19
  24.7 1.1 products.1
  25.8 0.7 copy-done.14
  26.5 0.5 collective-permute-done.2.third
  27.1 1.9 %collective-permute-done.1.second = bf16[4,128,128]{2,1,0:T(8,128)(2,1)S(1)} collective-permute-done((bf16[4,128,128]{2,1,0:T(8,128)(2,1)S(1)}, bf16[4,128,128]{2,1,0:T(8,128)(2,1)S(1)}, u32[]{:S(2)}, u32[]{:S(2)}) %collective-permute-start.1) | collective-permute-done | bytes 131104 | tf_op jit(solution)/shard_map/ppermute | solution.py:242
  29.0 4.1 %collective-permute-done.first = bf16[4,128,128]{2,1,0:T(8,128)(2,1)S(1)} collective-permute-done((bf16[4,128,128]{2,1,0:T(8,128)(2,1)S(1)}, bf16[4,128,128]{2,1,0:T(8,128)(2,1)S(1)}, u32[]{:S(2)}, u32[]{:S(2)}) %collective-permute-start) | collective-permute-done | bytes 131104 | tf_op jit(solution)/shard_map/ppermute | solution.py:242
  33.1 1.1 softmax_stats.1
  34.2 0.0 copy-start.3
  34.2 0.0 copy-start.5
  34.3 0.0 copy-start.7
  34.3 0.0 copy-start.21
  34.3 0.0 copy-start.23
  34.3 0.0 copy-start.25
  34.3 22.2 %all_to_all.25.gathered = f32[8,48,256]{2,1,0:T(8,128)S(1)} all-to-all(f32[8,48,256]{2,1,0:T(8,128)S(1)} %broadcast_in_dim.38), channel_id=1, replica_groups=mesh['zl'=4,'x'=4,'qi'=2,'zh'=2,'y'=4] {'zh','y'}, dimensions={0} | all-to-all | bytes 786432 | tf_op jit(solution)/shard_map/all_to_all | solution.py:246
  56.5 1.1 score_grads.1
  57.7 0.0 copy-done.16
  57.7 7.1 %all-to-all-start.1 = ((bf16[16,128,128]{2,1,0:T(8,128)(2,1)}), bf16[16,128,128]{2,1,0:T(8,128)(2,1)S(1)}, u32[]{:S(2)}, u32[]{:S(2)}) async-start(bf16[16,128,128]{2,1,0:T(8,128)(2,1)} %get-tuple-element.35), calls=%async_computation.1 | async-start | bytes 1048576 | tf_op jit(solution)/shard_map/all_to_all | solution.py:246
  64.8 1.0 copy-done.15
  65.8 1.0 copy-done.17
  66.8 2.0 %row_grads.1 = (bf16[2,4,32,768]{3,2,1,0:T(8,128)(2,1)S(1)}, f32[2,32,1536]{2,1,0:T(8,128)S(1)}) custom-call(s32[5]{0:T(128)S(1)} %stack.23.place, bf16[1024,256]{1,0:T(8,128)(2,1)S(1)} %get-tuple-element.28.score_low, bf16[1024,256]{1,0:T(8,128)(2,1)S(1)} %get-tuple-element.29.attend_low, bf16[256,768]{1,0:T(8,128)(2,1)S(1)} %copy-done.15, ...), custom_call_target="tpu_custom_call" | custom-call | tf_op jit(solution)/shard_map/row_grads/pallas_call | solution.py:319
  68.8 0.4 collective-permute-start.3
  69.2 0.3 copy-done.8
  69.5 0.2 copy-done.12
  69.7 2.1 %collective-permute-start.7 = (f32[32,1536]{1,0:T(8,128)S(1)}, f32[32,1536]{1,0:T(8,128)S(1)}, u32[]{:S(2)}, u32[]{:S(2)}) collective-permute-start(f32[32,1536]{1,0:T(8,128)S(1)} %slice_bitcast_fusion), channel_id=1, source_target_pairs={{0,8},{8,0},{1,9},{9,1},{2,10},{10,2},{3,11},{11,3},{4,12},{12,4},... | collective-permute-start | bytes 589832 | tf_op jit(solution)/shard_map/ppermute | solution.py:242
  71.8 5.7 %all-to-all-done.1.received = bf16[16,128,128]{2,1,0:T(8,128)(2,1)S(1)} async-done(((bf16[16,128,128]{2,1,0:T(8,128)(2,1)}), bf16[16,128,128]{2,1,0:T(8,128)(2,1)S(1)}, u32[]{:S(2)}, u32[]{:S(2)}) %all-to-all-start.1) | async-done | bytes 524320 | tf_op jit(solution)/shard_map/all_to_all | solution.py:246
  77.6 0.0 copy-start.1
  77.6 2.2 %copy-done.1 = bf16[256,2,32,128]{3,2,1,0:T(8,128)(2,1)S(1)} copy-done((bf16[256,2,32,128]{3,2,1,0:T(8,128)(2,1)S(1)}, bf16[256,2,32,128]{3,2,1,0:T(8,128)(2,1)}, u32[]{:S(2)}) %copy-start.1) | copy-done | bytes 4194328
  79.8 6.0 %pair_backward.1 = (bf16[16,2,32,128]{3,2,1,0:T(8,128)(2,1)}, bf16[1792,128]{1,0:T(8,128)(2,1)}) custom-call(s32[5]{0:T(128)S(1)} %stack.23.place, bf16[256,2,32,128]{3,2,1,0:T(8,128)(2,1)S(1)} %copy-done.1, bf16[16,128,128]{2,1,0:T(8,128)(2,1)S(1)} %all-to-all-done.1.received, f32[1,128]{1,0:T(1,128)S(1)} %bitcast.77, bf16[128,512]{1,0:T(8,128)(2,1)S(1)} %copy-done.3, ...), custom_call_target="tpu_custom_call" | custom-call | tf_op jit(solution)/shard_map/pair_backward/pallas_call | solution.py:339
  85.7 16.0 %all-to-all-start.2 = ((bf16[32,56,128]{2,1,0:T(8,128)(2,1)}), bf16[32,56,128]{2,1,0:T(8,128)(2,1)S(1)}, u32[]{:S(2)}, u32[]{:S(2)}) async-start(bf16[32,56,128]{2,1,0:T(8,128)(2,1)} %bitcast.24), calls=%async_computation.2 | async-start | bytes 917504 | tf_op jit(solution)/shard_map/all_to_all | solution.py:246
  101.7 0.0 collective-permute-done.3
  101.8 1.5 %collective-permute-start.4 = (bf16[32,768]{1,0:T(8,128)(2,1)S(1)}, bf16[32,768]{1,0:T(8,128)(2,1)S(1)}, u32[]{:S(2)}, u32[]{:S(2)}) collective-permute-start(bf16[32,768]{1,0:T(8,128)(2,1)S(1)} %get-tuple-element.45), channel_id=1, source_target_pairs={{0,1},{1,2},{2,3},{3,0},{4,5},{5,6},{6,7},{7,4},{8,9},{9,10},{10,1... | collective-permute-start | bytes 147464 | tf_op jit(solution)/shard_map/ppermute | solution.py:242
  103.3 1.3 collective-permute-start.6
  104.6 1.7 %collective-permute-start.5 = (bf16[32,768]{1,0:T(8,128)(2,1)S(1)}, bf16[32,768]{1,0:T(8,128)(2,1)S(1)}, u32[]{:S(2)}, u32[]{:S(2)}) collective-permute-start(bf16[32,768]{1,0:T(8,128)(2,1)S(1)} %get-tuple-element.47), channel_id=1, source_target_pairs={{0,2},{1,3},{2,0},{3,1},{4,6},{5,7},{6,4},{7,5},{8,10},{9,11},{10,... | collective-permute-start | bytes 147464 | tf_op jit(solution)/shard_map/ppermute | solution.py:242
  106.3 6.1 %all-to-all-done.2 = bf16[32,56,128]{2,1,0:T(8,128)(2,1)S(1)} async-done(((bf16[32,56,128]{2,1,0:T(8,128)(2,1)}), bf16[32,56,128]{2,1,0:T(8,128)(2,1)S(1)}, u32[]{:S(2)}, u32[]{:S(2)}) %all-to-all-start.2) | async-done | bytes 458784 | tf_op jit(solution)/shard_map/all_to_all | solution.py:246
  112.4 0.1 reduce_sum.24
  112.5 0.7 broadcast_in_dim.43
  113.1 3.4 %all-to-all-start.3 = ((bf16[8,56,128]{2,1,0:T(8,128)(2,1)}), bf16[8,56,128]{2,1,0:T(8,128)(2,1)S(1)}, u32[]{:S(2)}, u32[]{:S(2)}) async-start(bf16[8,56,128]{2,1,0:T(8,128)(2,1)} %broadcast_in_dim.43), calls=%async_computation.3 | async-start | bytes 229376 | tf_op jit(solution)/shard_map/all_to_all | solution.py:246
  116.5 0.0 collective-permute-done.7
  116.6 7.5 %all-to-all-done.3 = bf16[8,56,128]{2,1,0:T(8,128)(2,1)S(1)} async-done(((bf16[8,56,128]{2,1,0:T(8,128)(2,1)}), bf16[8,56,128]{2,1,0:T(8,128)(2,1)S(1)}, u32[]{:S(2)}, u32[]{:S(2)}) %all-to-all-start.3) | async-done | bytes 114720 | tf_op jit(solution)/shard_map/all_to_all | solution.py:246
  124.1 0.8 broadcast_in_dim.44
  124.9 5.8 %all-to-all-start.4 = ((bf16[32,56,128]{2,1,0:T(8,128)(2,1)}), bf16[32,56,128]{2,1,0:T(8,128)(2,1)S(1)}, u32[]{:S(2)}, u32[]{:S(2)}) async-start(bf16[32,56,128]{2,1,0:T(8,128)(2,1)} %broadcast_in_dim.44), calls=%async_computation.4 | async-start | bytes 917504 | tf_op jit(solution)/shard_map/all_to_all | solution.py:246
  130.8 0.6 slice_bitcast_fusion.3
  131.4 0.0 collective-permute-done.4
  131.4 0.0 collective-permute-done.6
  131.4 0.0 collective-permute-done.5
  131.4 0.6 fusion.5
  132.1 9.3 %all-to-all-done.4 = bf16[32,56,128]{2,1,0:T(8,128)(2,1)S(1)} async-done(((bf16[32,56,128]{2,1,0:T(8,128)(2,1)}), bf16[32,56,128]{2,1,0:T(8,128)(2,1)S(1)}, u32[]{:S(2)}, u32[]{:S(2)}) %all-to-all-start.4) | async-done | bytes 458784 | tf_op jit(solution)/shard_map/all_to_all | solution.py:246
  141.3 0.1 convert_multiply_fusion
  141.4 0.5 slice_bitcast_fusion.9
  141.9 0.6 slice_bitcast_fusion.8
  142.5 0.8 fusion.7
  143.3 0.9 copy_bitcast_fusion
  (37 shorter events, 0.2 us)
Async XLA Ops:
  0.7 2.2 %copy-start = (bf16[256,2,32,128]{3,2,1,0:T(8,128)(2,1)S(1)}, bf16[256,2,32,128]{3,2,1,0:T(8,128)(2,1)}, u32[]{:S(2)}) copy-start(bf16[256,2,32,128]{3,2,1,0:T(8,128)(2,1)} %pair.3) | copy-start | bytes 12582916
  2.9 0.9 copy-start.2
  3.8 0.9 copy-start.4
  4.7 0.9 copy-start.6
  5.6 0.7 copy-start.20
  6.3 0.7 copy-start.22
  7.0 0.7 copy-start.24
  7.6 17.0 %copy-start.10 = (bf16[1,256,768]{2,1,0:T(8,128)(2,1)S(1)}, bf16[1,256,768]{2,1,0:T(8,128)(2,1)}, u32[]{:S(2)}) copy-start(bf16[1,256,768]{2,1,0:T(8,128)(2,1)} %param.12) | copy-start | bytes 1179652
  7.6 17.0 %copy-start.11 = (bf16[1,256,768]{2,1,0:T(8,128)(2,1)S(1)}, bf16[1,256,768]{2,1,0:T(8,128)(2,1)}, u32[]{:S(2)}) copy-start(bf16[1,256,768]{2,1,0:T(8,128)(2,1)} %param.15) | copy-start | bytes 1179652
  7.6 17.0 %copy-start.18 = (bf16[1,2,32,768]{3,2,1,0:T(8,128)(2,1)S(1)}, bf16[1,2,32,768]{3,2,1,0:T(8,128)(2,1)}, u32[]{:S(2)}) copy-start(bf16[1,2,32,768]{3,2,1,0:T(8,128)(2,1)} %param.13) | copy-start | bytes 294916
  7.6 17.0 %copy-start.19 = (bf16[1,2,32,768]{3,2,1,0:T(8,128)(2,1)S(1)}, bf16[1,2,32,768]{3,2,1,0:T(8,128)(2,1)}, u32[]{:S(2)}) copy-start(bf16[1,2,32,768]{3,2,1,0:T(8,128)(2,1)} %param.14) | copy-start | bytes 294916
  20.2 6.9 %collective-permute-start.2 = (bf16[4,128,128]{2,1,0:T(8,128)(2,1)S(1)}, bf16[4,128,128]{2,1,0:T(8,128)(2,1)S(1)}, u32[]{:S(2)}, u32[]{:S(2)}) collective-permute-start(bf16[4,128,128]{2,1,0:T(8,128)(2,1)S(1)} %pair_bias.1.own), channel_id=1, source_target_pairs={{0,48},{16,0},{32,16},{48,32},{1,49},{17,1},{33,17},{49,33},{2,50}... | collective-permute-start | bytes 393224 | tf_op jit(solution)/shard_map/ppermute | solution.py:242
  23.5 5.4 %collective-permute-start.1 = (bf16[4,128,128]{2,1,0:T(8,128)(2,1)S(1)}, bf16[4,128,128]{2,1,0:T(8,128)(2,1)S(1)}, u32[]{:S(2)}, u32[]{:S(2)}) collective-permute-start(bf16[4,128,128]{2,1,0:T(8,128)(2,1)S(1)} %pair_bias.1.own), channel_id=1, source_target_pairs={{0,32},{16,48},{32,0},{48,16},{1,33},{17,49},{33,1},{49,17},{2,34}... | collective-permute-start | bytes 393224 | tf_op jit(solution)/shard_map/ppermute | solution.py:242
  24.1 9.0 %collective-permute-start = (bf16[4,128,128]{2,1,0:T(8,128)(2,1)S(1)}, bf16[4,128,128]{2,1,0:T(8,128)(2,1)S(1)}, u32[]{:S(2)}, u32[]{:S(2)}) collective-permute-start(bf16[4,128,128]{2,1,0:T(8,128)(2,1)S(1)} %pair_bias.1.own), channel_id=1, source_target_pairs={{0,16},{16,32},{32,48},{48,0},{1,17},{17,33},{33,49},{49,1},{2,18}... | collective-permute-start | bytes 393224 | tf_op jit(solution)/shard_map/ppermute | solution.py:242
  25.8 0.8 copy-start.14
  26.5 31.1 %copy-start.16 = (bf16[256,768]{1,0:T(8,128)(2,1)}, bf16[256,768]{1,0:T(8,128)(2,1)S(1)}, u32[]{:S(2)}) copy-start(bf16[256,768]{1,0:T(8,128)(2,1)S(1)} %get-tuple-element.31.grad) | copy-start | bytes 1179652
  34.2 43.3 %copy-start.3 = (bf16[128,512]{1,0:T(8,128)(2,1)S(1)}, bf16[128,512]{1,0:T(8,128)(2,1)}, u32[]{:S(2)}) copy-start(bf16[128,512]{1,0:T(8,128)(2,1)} %gate_w.3) | copy-start | bytes 393220
  34.2 43.3 %copy-start.5 = (bf16[128,512]{1,0:T(8,128)(2,1)S(1)}, bf16[128,512]{1,0:T(8,128)(2,1)}, u32[]{:S(2)}) copy-start(bf16[128,512]{1,0:T(8,128)(2,1)} %up_w.3) | copy-start | bytes 393220
  34.3 43.3 %copy-start.7 = (bf16[512,128]{1,0:T(8,128)(2,1)S(1)}, bf16[512,128]{1,0:T(8,128)(2,1)}, u32[]{:S(2)}) copy-start(bf16[512,128]{1,0:T(8,128)(2,1)} %down_w.3) | copy-start | bytes 393220
  34.3 43.3 %copy-start.21 = (bf16[128,16]{0,1:T(8,128)(2,1)S(1)}, bf16[128,16]{0,1:T(8,128)(2,1)}, u32[]{:S(2)}) copy-start(bf16[128,16]{0,1:T(8,128)(2,1)} %param.21) | copy-start | bytes 12292
  34.3 43.3 %copy-start.23 = (f32[128]{0:T(128)S(1)}, f32[128]{0:T(128)}, u32[]{:S(2)}) copy-start(f32[128]{0:T(128)} %param.16) | copy-start | bytes 1540
  34.3 43.3 %copy-start.25 = (f32[128]{0:T(128)S(1)}, f32[128]{0:T(128)}, u32[]{:S(2)}) copy-start(f32[128]{0:T(128)} %param.20) | copy-start | bytes 1540
  57.7 19.8 %all-to-all-start.1 = ((bf16[16,128,128]{2,1,0:T(8,128)(2,1)}), bf16[16,128,128]{2,1,0:T(8,128)(2,1)S(1)}, u32[]{:S(2)}, u32[]{:S(2)}) async-start(bf16[16,128,128]{2,1,0:T(8,128)(2,1)} %get-tuple-element.35), calls=%async_computation.1 | async-start | bytes 1048576 | tf_op jit(solution)/shard_map/all_to_all | solution.py:246
  64.8 1.0 copy-start.15
  65.8 1.0 copy-start.17
  68.7 0.8 copy-start.8
  68.7 0.9 copy-start.12
  68.8 33.0 %collective-permute-start.3 = (bf16[4,32,768]{2,1,0:T(8,128)(2,1)S(1)}, bf16[4,32,768]{2,1,0:T(8,128)(2,1)S(1)}, u32[]{:S(2)}, u32[]{:S(2)}) collective-permute-start(bf16[4,32,768]{2,1,0:T(8,128)(2,1)S(1)} %slice_bitcast_fusion.1), channel_id=1, source_target_pairs={{0,4},{4,0},{1,5},{5,1},{2,6},{6,2},{3,7},{7,3},{8,12},{12,8},{9,1... | collective-permute-start | bytes 589832 | tf_op jit(solution)/shard_map/ppermute | solution.py:242
  69.7 46.9 %collective-permute-start.7 = (f32[32,1536]{1,0:T(8,128)S(1)}, f32[32,1536]{1,0:T(8,128)S(1)}, u32[]{:S(2)}, u32[]{:S(2)}) collective-permute-start(f32[32,1536]{1,0:T(8,128)S(1)} %slice_bitcast_fusion), channel_id=1, source_target_pairs={{0,8},{8,0},{1,9},{9,1},{2,10},{10,2},{3,11},{11,3},{4,12},{12,4},... | collective-permute-start | bytes 589832 | tf_op jit(solution)/shard_map/ppermute | solution.py:242
  77.6 2.2 %copy-start.1 = (bf16[256,2,32,128]{3,2,1,0:T(8,128)(2,1)S(1)}, bf16[256,2,32,128]{3,2,1,0:T(8,128)(2,1)}, u32[]{:S(2)}) copy-start(bf16[256,2,32,128]{3,2,1,0:T(8,128)(2,1)} %pair.3) | copy-start | bytes 12582916
  79.8 22.0 %copy-start.13 = (bf16[2,4,32,768]{3,2,1,0:T(8,128)(2,1)S(1)}, bf16[2,4,32,768]{3,2,1,0:T(8,128)(2,1)}, u32[]{:S(2)}) copy-start(bf16[2,4,32,768]{3,2,1,0:T(8,128)(2,1)} %copy-done.12) | copy-start | bytes 1179652
  79.8 36.8 %copy-start.9 = (f32[2,32,1536]{2,1,0:T(8,128)S(1)}, f32[2,32,1536]{2,1,0:T(8,128)}, u32[]{:S(2)}) copy-start(f32[2,32,1536]{2,1,0:T(8,128)} %copy-done.8) | copy-start | bytes 1179652
  85.7 26.7 %all-to-all-start.2 = ((bf16[32,56,128]{2,1,0:T(8,128)(2,1)}), bf16[32,56,128]{2,1,0:T(8,128)(2,1)S(1)}, u32[]{:S(2)}, u32[]{:S(2)}) async-start(bf16[32,56,128]{2,1,0:T(8,128)(2,1)} %bitcast.24), calls=%async_computation.2 | async-start | bytes 917504 | tf_op jit(solution)/shard_map/all_to_all | solution.py:246
  101.8 29.5 %collective-permute-start.4 = (bf16[32,768]{1,0:T(8,128)(2,1)S(1)}, bf16[32,768]{1,0:T(8,128)(2,1)S(1)}, u32[]{:S(2)}, u32[]{:S(2)}) collective-permute-start(bf16[32,768]{1,0:T(8,128)(2,1)S(1)} %get-tuple-element.45), channel_id=1, source_target_pairs={{0,1},{1,2},{2,3},{3,0},{4,5},{5,6},{6,7},{7,4},{8,9},{9,10},{10,1... | collective-permute-start | bytes 147464 | tf_op jit(solution)/shard_map/ppermute | solution.py:242
  103.3 28.1 %collective-permute-start.6 = (bf16[32,768]{1,0:T(8,128)(2,1)S(1)}, bf16[32,768]{1,0:T(8,128)(2,1)S(1)}, u32[]{:S(2)}, u32[]{:S(2)}) collective-permute-start(bf16[32,768]{1,0:T(8,128)(2,1)S(1)} %get-tuple-element.46), channel_id=1, source_target_pairs={{0,3},{1,0},{2,1},{3,2},{4,7},{5,4},{6,5},{7,6},{8,11},{9,8},{10,9... | collective-permute-start | bytes 147464 | tf_op jit(solution)/shard_map/ppermute | solution.py:242
  104.6 26.8 %collective-permute-start.5 = (bf16[32,768]{1,0:T(8,128)(2,1)S(1)}, bf16[32,768]{1,0:T(8,128)(2,1)S(1)}, u32[]{:S(2)}, u32[]{:S(2)}) collective-permute-start(bf16[32,768]{1,0:T(8,128)(2,1)S(1)} %get-tuple-element.47), channel_id=1, source_target_pairs={{0,2},{1,3},{2,0},{3,1},{4,6},{5,7},{6,4},{7,5},{8,10},{9,11},{10,... | collective-permute-start | bytes 147464 | tf_op jit(solution)/shard_map/ppermute | solution.py:242
  113.1 10.9 %all-to-all-start.3 = ((bf16[8,56,128]{2,1,0:T(8,128)(2,1)}), bf16[8,56,128]{2,1,0:T(8,128)(2,1)S(1)}, u32[]{:S(2)}, u32[]{:S(2)}) async-start(bf16[8,56,128]{2,1,0:T(8,128)(2,1)} %broadcast_in_dim.43), calls=%async_computation.3 | async-start | bytes 229376 | tf_op jit(solution)/shard_map/all_to_all | solution.py:246
  124.9 16.4 %all-to-all-start.4 = ((bf16[32,56,128]{2,1,0:T(8,128)(2,1)}), bf16[32,56,128]{2,1,0:T(8,128)(2,1)S(1)}, u32[]{:S(2)}, u32[]{:S(2)}) async-start(bf16[32,56,128]{2,1,0:T(8,128)(2,1)} %broadcast_in_dim.44), calls=%async_computation.4 | async-start | bytes 917504 | tf_op jit(solution)/shard_map/all_to_all | solution.py:246

commit v2 on v1

v2 whole, which is shorter than its diff:
```python
import functools

import jax
import jax.numpy as jnp
from jax import lax
from jax.experimental import pallas as pl
from jax.experimental.pallas import tpu as pltpu
from jax.sharding import Mesh, PartitionSpec as P

HEADS = 16
HEAD_DIM = 48
WIDTH = HEADS * HEAD_DIM
PAIR = 128
FF = 512
KEYS = 64
ROWS = 256
SUB = 16
EPSILON = 1e-05
SCALE = HEAD_DIM**-0.5
CHUNK_ROWS = 56
CHUNKS = 32
GROUP = 4
F32 = jnp.float32
BF16 = jnp.bfloat16
NOISE = ("zl", "x")
PLANE = ("x", "qi", "y")
COLUMN = ("zh", "zl")

VMEM = pl.BlockSpec(memory_space=pltpu.VMEM)
SMEM = pl.BlockSpec(memory_space=pltpu.SMEM)
HBM = pl.BlockSpec(memory_space=pltpu.HBM)
BLOCK = pl.BlockSpec()
PARAMS = pltpu.CompilerParams(vmem_limit_bytes=48 * 1024 * 1024)


def dot(left, right, dims):
    return lax.dot_general(left, right, (dims, ((), ())), preferred_element_type=F32)


NN = ((1,), (0,))
NT = ((1,), (1,))
TN = ((0,), (0,))


def layer_norm(values):
    center = values - jnp.mean(values, axis=1, keepdims=True)
    inverse = lax.rsqrt(jnp.mean(center * center, axis=1, keepdims=True) + EPSILON)
    return center * inverse, inverse


def norm_backward(grad, normed, inverse):
    first = jnp.mean(grad, axis=1, keepdims=True)
    second = jnp.mean(grad * normed, axis=1, keepdims=True)
    return inverse * (grad - first - normed * second)


def block_cells(read_row):
    slabs = [read_row(half * 8 + step) for step in range(8) for half in range(2)]
    return jnp.concatenate(slabs, axis=0)


def silu_parts(gate):
    half = 0.5 * gate
    curve = jnp.tanh(half)
    return half + half * curve, 0.5 + 0.5 * curve


def fetch(sources, targets, sems):
    copies = [
        pltpu.make_async_copy(source, target, sems.at[k])
        for k, (source, target) in enumerate(zip(sources, targets))
    ]
    for copy in copies:
        copy.start()
    return copies


def bias_kernel(
    place, pair, gain1_h, gate_h, up_h, down_h, gain2_h, head_h, out,
    cells_v, gain1, gate_w, up_w, down_w, gain2, head_t, rows, sems,
):
    x = place[1]
    blocks = [pair.at[pl.ds((zl * 4 + x) * SUB, SUB)] for zl in range(4)]
    copies = fetch(
        (blocks[0], gain1_h, gate_h, up_h, down_h, gain2_h, head_h, *blocks[1:]),
        (
            cells_v.at[0], gain1, gate_w, up_w, down_w, gain2, head_t,
            cells_v.at[1], cells_v.at[2], cells_v.at[3],
        ),
        sems,
    )
    for copy in copies:
        copy.wait()
    for start in range(0, 4, GROUP):
        blocks = range(start, start + GROUP)
        cells = jnp.concatenate(
            [block_cells(lambda r: cells_v[k, r].reshape(KEYS, PAIR)) for k in blocks], axis=0
        ).astype(F32)
        normed, _ = layer_norm(cells)
        lowered = (normed * gain1[...]).astype(BF16)
        gate = dot(lowered, gate_w[...], NN)
        up = dot(lowered, up_w[...], NN)
        hidden = (silu_parts(gate)[0] * up).astype(BF16)
        updated = cells + dot(hidden, down_w[...], NN)
        post, _ = layer_norm(updated)
        post_low = (post * gain2[...]).astype(BF16)
        bias = dot(head_t[...], post_low, NT)
        for place_k, k in enumerate(blocks):
            for step in range(8):
                lane = place_k * 1024 + step * 128
                rows[k, pl.ds(step, HEADS, stride=8), :] = bias[:, lane : lane + 128]
            out[k] = rows[k].astype(BF16)


def head_mask(shape, head):
    column = lax.broadcasted_iota(jnp.int32, shape, 1)
    return (column >= head * HEAD_DIM) & (column < (head + 1) * HEAD_DIM)


def spread_heads(tile):
    wide = tile.astype(F32)
    parts = [
        jnp.where(head_mask(wide.shape, h), wide, 0.0).astype(BF16) for h in range(HEADS)
    ]
    return jnp.concatenate(parts, axis=0)


def permute_rows(tile):
    width = tile.shape[1]
    wide = tile.astype(F32).reshape(16, 2, 8, width)
    parts = [wide[:, half].reshape(128, width) for half in range(2)]
    return jnp.concatenate(parts, axis=0).astype(BF16)


def product_kernel(query, grad, keys, values, scores, attend, query_out, grad_out, keys_out):
    query_p = permute_rows(query[...])
    grad_p = permute_rows(grad[...])
    query_out[...] = query_p
    grad_out[...] = grad_p
    wide_keys = spread_heads(keys[...].reshape(KEYS, WIDTH))
    keys_out[...] = wide_keys
    scores[...] = dot(wide_keys, query_p, NT) * SCALE
    wide_values = spread_heads(values[...].reshape(KEYS, WIDTH))
    attend[...] = dot(wide_values, grad_p, NT)


def stats_kernel(place, scores, attend, own, first, second, third, total_out, stats, wide):
    x = place[1]
    for shift, piece in enumerate((own, first, second, third)):
        origin = lax.rem(x + 4 - shift, 4)
        for zl in range(4):
            wide[zl, origin] = piece[zl].astype(F32)
    logs, means = [], []
    for h in range(HEADS):
        block = wide[:, :, 8 * h : 8 * h + 8, :].reshape(128, 128).T
        bias = jnp.concatenate([block[:KEYS], block[KEYS:]], axis=1)
        rows = slice(h * KEYS, (h + 1) * KEYS)
        total = scores[rows, :] + bias
        total_out[rows, :] = total
        largest = jnp.max(total, axis=0, keepdims=True)
        powers = jnp.exp(total - largest)
        amount = jnp.sum(powers, axis=0, keepdims=True)
        weighted = jnp.sum(powers * attend[rows, :], axis=0, keepdims=True)
        logs.append(largest + jnp.log(amount))
        means.append(weighted / amount)
    packed = jnp.concatenate(logs + means, axis=0)
    for j in range(8):
        stats[j] = packed


def grad_kernel(gathered, total, attend, send, score_low, attend_low):
    peers = [gathered[j] for j in range(8)]
    largest = functools.reduce(jnp.maximum, [p[:HEADS] for p in peers])
    amount = jnp.zeros((HEADS, ROWS), F32)
    weighted = jnp.zeros((HEADS, ROWS), F32)
    for p in peers:
        power = jnp.exp(p[:HEADS] - largest)
        amount = amount + power
        weighted = weighted + p[HEADS:] * power
    level = largest + jnp.log(amount)
    delta = weighted / amount
    for pair in range(HEADS // 2):
        blocks = []
        for h in (2 * pair, 2 * pair + 1):
            rows = slice(h * KEYS, (h + 1) * KEYS)
            weights = jnp.exp(total[rows, :] - level[h : h + 1])
            score = weights * (attend[rows, :] - delta[h : h + 1])
            score_low[rows, :] = score.astype(BF16)
            attend_low[rows, :] = weights.astype(BF16)
            block = jnp.concatenate([score[:, :128], score[:, 128:]], axis=0).T
            blocks.append(block.reshape(16, 8, 128))
        send[:, 16 * pair : 16 * pair + 16, :] = jnp.concatenate(blocks, axis=1).astype(BF16)


def rows_kernel(
    place, score_low, attend_low, query, grad, keys,
    query_0, query_1, query_2, query_3, kv_keep, kv_send, sends,
):
    y, zh, qi = place[2], place[3], place[4]
    product = dot(score_low[...], keys[...], TN) * SCALE
    for target in range(8):
        rel_z = lax.rem(target // 4 + zh, 2)
        rel_y = lax.rem(target % 4 + 4 - y, 4)
        parts = []
        for block in (2 * target, 2 * target + 1):
            for half in range(2):
                start = half * 128 + block * 8
                parts.append(product[start : start + 8])
        sends[rel_y, rel_z] = jnp.concatenate(parts, axis=0).astype(BF16)
    for shift, out in enumerate((query_0, query_1, query_2, query_3)):
        out[...] = sends[shift]
    for which, (low, rows) in enumerate(((score_low, query), (attend_low, grad))):
        result = jnp.zeros((KEYS, WIDTH), F32)
        for quad in range(4):
            part = dot(low[quad * 256 : quad * 256 + 256, :], rows[...], NN)
            for step in range(4):
                piece = part[step * KEYS : (step + 1) * KEYS]
                mask = head_mask(piece.shape, quad * 4 + step)
                result = result + jnp.where(mask, piece, 0.0)
        if which == 0:
            result = result * SCALE
        lanes = slice(which * WIDTH, (which + 1) * WIDTH)
        first, second = result[:32], result[32:]
        kv_keep[:, lanes] = jnp.where(qi == 0, first, second)
        kv_send[:, lanes] = jnp.where(qi == 0, second, first)


def pair_kernel(
    place, received, pair, gain1, gate_w, up_w, down_w, gain2, head_t,
    pair_out, weights, rows, cells_v, sems,
):
    copies = fetch((pair.at[pl.ds(place[0] * SUB, SUB)],), (cells_v,), sems)
    rows[...] = jnp.sum(received[...].astype(F32), axis=0)
    low = jnp.concatenate(
        [rows[pl.ds(step, HEADS, stride=8), :] for step in range(8)], axis=1
    ).astype(BF16)
    post_scaled = dot(low, head_t[...], TN)
    for copy in copies:
        copy.wait()
    cells = block_cells(lambda r: cells_v[r].reshape(KEYS, PAIR)).astype(F32)
    pre_normed, pre_inverse = layer_norm(cells)
    pre_low = (pre_normed * gain1[...]).astype(BF16)
    gate = dot(pre_low, gate_w[...], NN)
    up = dot(pre_low, up_w[...], NN)
    silu, sigmoid = silu_parts(gate)
    hidden = (silu * up).astype(BF16)
    gate_slope = up * (sigmoid + silu * (1.0 - sigmoid))
    updated = cells + dot(hidden, down_w[...], NN)
    post_normed, post_inverse = layer_norm(updated)
    post_low = (post_normed * gain2[...]).astype(BF16)
    second_sum = jnp.sum(post_scaled * post_normed, axis=0, keepdims=True)
    updated_grad = norm_backward(post_scaled * gain2[...], post_normed, post_inverse)
    updated_low = updated_grad.astype(BF16)
    hidden_grad = dot(updated_low, down_w[...], NT)
    gate_low = (hidden_grad * gate_slope).astype(BF16)
    up_low = (hidden_grad * silu).astype(BF16)
    gate_part = dot(pre_low, gate_low, TN).astype(BF16)
    up_part = dot(pre_low, up_low, TN).astype(BF16)
    for block in range(4):
        lanes = slice(block * 128, (block + 1) * 128)
        weights[block * 128 : (block + 1) * 128, :] = gate_part[:, lanes]
        weights[512 + block * 128 : 512 + (block + 1) * 128, :] = up_part[:, lanes]
    weights[1024:1536, :] = dot(hidden, updated_low, TN).astype(BF16)
    weights[1536:1552, :] = dot(low, post_low, NN).astype(BF16)
    pre_scaled = dot(gate_low, gate_w[...], NT) + dot(up_low, up_w[...], NT)
    first_sum = jnp.sum(pre_scaled * pre_normed, axis=0, keepdims=True)
    inputs_grad = norm_backward(pre_scaled * gain1[...], pre_normed, pre_inverse)
    result = (updated_grad + inputs_grad).astype(BF16)
    for step in range(8):
        for half in range(2):
            start = step * 128 + half * KEYS
            slab = result[start : start + KEYS]
            pair_out[half * 8 + step] = slab.reshape(2, 32, PAIR)
    gains = jnp.concatenate([first_sum, second_sum, jnp.zeros((14, PAIR), F32)], axis=0)
    weights[1552:1568, :] = gains.astype(BF16)
    weights[1568:, :] = jnp.zeros((CHUNK_ROWS * CHUNKS - 1568, PAIR), BF16)


def sum_kernel(parts, out):
    total = jnp.sum(parts[...].astype(F32), axis=0).astype(out.dtype)
    for j in range(out.shape[0]):
        out[j] = total


def unpack_kernel(table, gate_out, up_out, down_out, head_out, first_out, second_out):
    factor = 1.0 / 512
    for block in range(4):
        lanes = slice(block * 128, (block + 1) * 128)
        rows = slice(block * 128, (block + 1) * 128)
        later = slice(512 + block * 128, 512 + (block + 1) * 128)
        gate_out[:, lanes] = table[rows, :].astype(F32) * factor
        up_out[:, lanes] = table[later, :].astype(F32) * factor
    down_out[...] = table[1024:1536, :].astype(F32) * factor
    rest = table[1536:1568, :].astype(F32) * factor
    head_out[...] = rest[:16]
    first_out[...] = rest[16:17]
    second_out[...] = rest[17:18]


def shifted(value, axis, shift):
    size = lax.axis_size(axis)
    return lax.ppermute(value, axis, [(i, (i + shift) % size) for i in range(size)])


def all_to_all(value, axes):
    return lax.all_to_all(value, axes, 0, 0, tiled=True)


def local(
    pair_rep, query_rows, key_rows, value_rows, output_grad,
    gain_first, gate_weight, up_weight, down_weight, gain_second, head_weight,
):
    x, zl = lax.axis_index("x"), lax.axis_index("zl")
    y, zh, qi = lax.axis_index("y"), lax.axis_index("zh"), lax.axis_index("qi")
    place = jnp.stack([zl * 4 + x, x, y, zh, qi]).astype(jnp.int32)
    params = (
        gain_first[None], gate_weight, up_weight, down_weight, gain_second[None], head_weight.T,
    )

    def call(kernel, ins, outs, name, scratch=()):
        return pl.pallas_call(
            kernel,
            in_specs=[spec for spec, _ in ins],
            out_specs=[spec for spec, _ in outs],
            out_shape=[out for _, out in outs],
            scratch_shapes=list(scratch),
            compiler_params=PARAMS,
            name=name,
        )(*[value for _, value in ins])

    def vmem(*values):
        return [(VMEM, value) for value in values]

    def kept(*values):
        return [(BLOCK, pltpu.with_memory_space_constraint(v, pltpu.HBM)) for v in values]

    def f32(*dims):
        return (VMEM, jax.ShapeDtypeStruct(dims, F32))

    def bf16(*dims):
        return (VMEM, jax.ShapeDtypeStruct(dims, BF16))

    def f32_kept(*dims):
        return (BLOCK, pltpu.HBM(dims, F32))

    def bf16_kept(*dims):
        return (BLOCK, pltpu.HBM(dims, BF16))

    def in_hbm(value):
        return (HBM, pltpu.with_memory_space_constraint(value, pltpu.HBM))

    (own,) = call(
        bias_kernel,
        [(SMEM, place), in_hbm(pair_rep), *[in_hbm(p) for p in params]],
        [bf16(4, 128, 128)],
        "pair_bias",
        [
            pltpu.VMEM((4, SUB, 2, 32, PAIR), BF16),
            *[pltpu.VMEM(p.shape, p.dtype) for p in params],
            pltpu.VMEM((4, 128, 128), F32),
            pltpu.SemaphoreType.DMA((10,)),
        ],
    )
    first, third, second = [shifted(own, "x", s) for s in (1, 3, 2)]

    scores, attend, query_p, grad_p, wide_keys = call(
        product_kernel,
        vmem(query_rows[0], output_grad[0], key_rows[0], value_rows[0]),
        [
            f32(HEADS * KEYS, ROWS), f32(HEADS * KEYS, ROWS), bf16_kept(ROWS, WIDTH),
            bf16_kept(ROWS, WIDTH), bf16_kept(HEADS * KEYS, WIDTH),
        ],
        "products",
    )

    total, stats = call(
        stats_kernel,
        [(SMEM, place), *vmem(scores, attend, own, first, second, third)],
        [f32(HEADS * KEYS, ROWS), f32_kept(8, 2 * HEADS, ROWS)],
        "softmax_stats",
        [pltpu.VMEM((4, 4, 128, 128), F32)],
    )

    gathered = all_to_all(stats, ("zh", "y"))

    send, score_low, attend_low = call(
        grad_kernel,
        vmem(gathered, total, attend),
        [bf16_kept(16, 128, 128), *[bf16_kept(HEADS * KEYS, ROWS)] * 2],
        "score_grads",
    )

    received = all_to_all(send, NOISE)

    *query_parts, kv_keep, kv_send = call(
        rows_kernel,
        [(SMEM, place), *kept(score_low, attend_low, query_p, grad_p, wide_keys)],
        [*[bf16(2, 32, WIDTH)] * 4, *[f32(32, 2 * WIDTH)] * 2],
        "row_grads",
        [pltpu.VMEM((4, 2, 32, WIDTH), BF16)],
    )

    half = query_parts[0].astype(F32)
    for s in (1, 3, 2):
        half = half + shifted(query_parts[s], "y", s).astype(F32)
    query_sum = half[0] + shifted(half[1].astype(BF16), "zh", 1).astype(F32)
    query_grad = query_sum.astype(BF16)[None]
    kv_sum = (kv_keep + shifted(kv_send, "qi", 1)).astype(BF16)
    key_grad = kv_sum[None, :, :WIDTH]
    value_grad = kv_sum[None, :, WIDTH:]

    weight_rows = CHUNK_ROWS * CHUNKS
    pair_low, weights = call(
        pair_kernel,
        [(SMEM, place), *vmem(received), in_hbm(pair_rep), *vmem(*params)],
        [bf16_kept(SUB, 2, 32, PAIR), bf16_kept(weight_rows, PAIR)],
        "pair_backward",
        [
            pltpu.VMEM((128, 128), F32),
            pltpu.VMEM((SUB, 2, 32, PAIR), BF16),
            pltpu.SemaphoreType.DMA((1,)),
        ],
    )
    pair_grad = pair_low[None, None]

    parts = all_to_all(weights.reshape(CHUNKS, CHUNK_ROWS, PAIR), PLANE)
    (shares,) = call(sum_kernel, vmem(parts), [bf16_kept(8, CHUNK_ROWS, PAIR)], "plane_sum")
    columns = all_to_all(shares, COLUMN)
    (totals,) = call(
        sum_kernel, vmem(columns), [bf16_kept(CHUNKS, CHUNK_ROWS, PAIR)], "column_sum"
    )
    table = all_to_all(totals, PLANE).reshape(weight_rows, PAIR)
    gate_grad, up_grad, down_grad, head_grad, first_grad, second_grad = call(
        unpack_kernel,
        vmem(table),
        [
            f32_kept(PAIR, FF), f32_kept(PAIR, FF), f32_kept(FF, PAIR),
            f32_kept(HEADS, PAIR), f32_kept(1, PAIR), f32_kept(1, PAIR),
        ],
        "unpack",
    )
    return (
        query_grad, key_grad, value_grad, pair_grad, gate_grad, up_grad, down_grad,
        head_grad.T, first_grad[0], second_grad[0],
    )


def solution(mesh):
    fine = Mesh(mesh.devices.reshape(4, 4, 2, 2, 4), ("zl", "x", "qi", "zh", "y"))
    kj = ("zh", "y")
    return jax.shard_map(
        local,
        mesh=fine,
        in_specs=(
            P("qi", None, kj, None),
            P(NOISE, "qi", None),
            P(NOISE, None, kj, None),
            P(NOISE, None, kj, None),
            P(NOISE, "qi", None),
            P(),
            P(),
            P(),
            P(),
            P(),
            P(),
        ),
        out_specs=(
            P(NOISE, ("qi", "zh", "y"), None),
            P(NOISE, ("qi", "zh", "y"), None),
            P(NOISE, ("qi", "zh", "y"), None),
            P("qi", NOISE, None, None, kj, None),
            P(),
            P(),
            P(),
            P(),
            P(),
            P(),
        ),
        check_vma=False,
    )
```

time: 145 us -> 119 us (0.82)
  local copies, waits for them, and re-layouts: 17.4 us -> 0.78 us
  starting transfers between devices: 43.7 us -> 31.4 us
  waiting for transfers between devices: 35.2 us -> 38.1 us
  Pallas kernels: 23.8 us -> 25.6 us
    unnamed x52 -> x20, local copies, waits for them, and re-layouts: 12.4 us -> 0.04 us
    all_to_all x4, starting transfers between devices: 32.3 us -> 22.9 us  [all_to_all(): return lax.all_to_all(value, axes, 0, 0, tiled=True)]
    all_to_all x4, waiting for transfers between devices: 28.7 us -> 31.9 us  [all_to_all(): return lax.all_to_all(value, axes, 0, 0, tiled=True)]
    ppermute x8, starting transfers between devices: 11.4 us -> 8.5 us  [shifted(): lax.ppermute(value, axis, [(i, (i + shift) % size) for i in range(size)])]
    pallas_call x6 -> x9, Pallas kernels: 23.8 us -> 25.6 us  [call(): pl.pallas_call(kernel, in_specs=[spec for spec, _ in ins], out_specs=[spe...]
    broadcast_in_dim x3 -> x0, local copies, waits for them, and re-layouts: 1.51 us -> none  [the longest x1 0.82 us: local(): jnp.broadcast_to(total[None], (CHUNKS, *total.shape))]
  transfers between devices with their start and end apart: 12 -> 12, of which waited for: 7 -> 7; matrix products, arithmetic and copies ran while one was open for 2% -> 1% of each run, Pallas kernels for 6% -> 12%
where the time goes in v2:
time: 119 us; the launch traced here: 118 us
  waiting for transfers between devices  38.1 us (32%)
  starting transfers between devices  31.4 us (26%)
  Pallas kernels  25.6 us (22%)
  blocking collectives  21 us (18%)
    all_to_all x4, waiting for transfers between devices, all_to_all(): return lax.all_to_all(value, axes, 0, 0, tiled=True)  31.9 us
    pallas_call x9, Pallas kernels, call(): pl.pallas_call(kernel, in_specs=[spec for spec, _ in ins], out_specs=[spe...  25.6 us
    all_to_all x4, starting transfers between devices, all_to_all(): return lax.all_to_all(value, axes, 0, 0, tiled=True)  22.9 us
    all_to_all x1, blocking collectives, all_to_all(): return lax.all_to_all(value, axes, 0, 0, tiled=True)  21 us
    ppermute x8, starting transfers between devices, shifted(): lax.ppermute(value, axis, [(i, (i + shift) % size) for i in range(size)])  8.5 us
    ppermute x8, waiting for transfers between devices, shifted(): lax.ppermute(value, axis, [(i, (i + shift) % size) for i in range(size)])  6.2 us
  transfers between devices with their start and end apart: 12, of which 7 were waited for; matrix products, arithmetic and copies ran while one was open for 1% of the time, Pallas kernels for 12%

profile of v2, /device:TPU:1, one launch (start us, length us, event | category | flops | bytes accessed | tf_op | source)
XLA Modules:
  0.0 118.5 jit_solution(7818000870257989104)
XLA Ops:
  0.6 0.0 copy-start.4
  0.7 0.0 copy-start.6
  0.7 0.0 copy-start.5
  0.7 0.0 copy-start.3
  0.7 0.1 stack.23.place
  0.8 7.7 %pair_bias.1.own = bf16[4,128,128]{2,1,0:T(8,128)(2,1)S(1)} custom-call(s32[5]{0:T(128)S(1)} %stack.23.place, bf16[256,2,32,128]{3,2,1,0:T(8,128)(2,1)} %pair.3, f32[1,128]{1,0:T(1,128)} %bitcast.41, bf16[128,512]{1,0:T(8,128)(2,1)} %gate_w.1, bf16[128,512]{1,0:T(8,128)(2,1)} %up_w.1, bf16[512,128]{1,0:T(8,128)(2,1)} %down_w.1, f32[1,128]{1,0:T(1,128)} %bitcast.43, ...), custom_call_target="tpu_custom_call" | custom-call | tf_op jit(solution)/shard_map/pair_bias/pallas_call | solution.py:321
  8.5 3.4 %collective-permute-start.2 = (bf16[4,128,128]{2,1,0:T(8,128)(2,1)S(1)}, bf16[4,128,128]{2,1,0:T(8,128)(2,1)S(1)}, u32[]{:S(2)}, u32[]{:S(2)}) collective-permute-start(bf16[4,128,128]{2,1,0:T(8,128)(2,1)S(1)} %pair_bias.1.own), channel_id=1, source_target_pairs={{0,48},{16,0},{32,16},{48,32},{1,49},{17,1},{33,17},{49,33},{2,50}... | collective-permute-start | bytes 393224 | tf_op jit(solution)/shard_map/ppermute | solution.py:302
  11.9 0.5 collective-permute-start.1
  12.4 0.6 collective-permute-start
  13.0 0.0 copy-done.4
  13.0 0.0 copy-done.6
  13.0 0.0 copy-done.5
  13.0 0.0 copy-done.3
  13.0 2.2 %products.1 = (f32[1024,256]{1,0:T(8,128)S(1)}, f32[1024,256]{1,0:T(8,128)S(1)}, bf16[256,768]{1,0:T(8,128)(2,1)}, bf16[256,768]{1,0:T(8,128)(2,1)}, bf16[1024,768]{1,0:T(8,128)(2,1)}) custom-call(bf16[256,768]{1,0:T(8,128)(2,1)S(1)} %bitcast.35, bf16[256,768]{1,0:T(8,128)(2,1)S(1)} %bitcast.36, bf16[2,32,768]{2,1,0:T(8,128)(2,1)S(1)} %bitcast.37, ...), custom_call_target="tpu_custom_call" | custom-call | tf_op jit(solution)/shard_map/products/pallas_call | solution.py:321
  15.2 0.2 collective-permute-done.2.third
  15.4 1.9 %collective-permute-done.1.second = bf16[4,128,128]{2,1,0:T(8,128)(2,1)S(1)} collective-permute-done((bf16[4,128,128]{2,1,0:T(8,128)(2,1)S(1)}, bf16[4,128,128]{2,1,0:T(8,128)(2,1)S(1)}, u32[]{:S(2)}, u32[]{:S(2)}) %collective-permute-start.1) | collective-permute-done | bytes 131104 | tf_op jit(solution)/shard_map/ppermute | solution.py:302
  17.3 4.1 %collective-permute-done.first = bf16[4,128,128]{2,1,0:T(8,128)(2,1)S(1)} collective-permute-done((bf16[4,128,128]{2,1,0:T(8,128)(2,1)S(1)}, bf16[4,128,128]{2,1,0:T(8,128)(2,1)S(1)}, u32[]{:S(2)}, u32[]{:S(2)}) %collective-permute-start) | collective-permute-done | bytes 131104 | tf_op jit(solution)/shard_map/ppermute | solution.py:302
  21.4 1.9 %softmax_stats.1 = (f32[1024,256]{1,0:T(8,128)S(1)}, f32[8,32,256]{2,1,0:T(8,128)}) custom-call(s32[5]{0:T(128)S(1)} %stack.23.place, f32[1024,256]{1,0:T(8,128)S(1)} %get-tuple-element.34.scores, f32[1024,256]{1,0:T(8,128)S(1)} %get-tuple-element.35.attend, bf16[4,128,128]{2,1,0:T(8,128)(2,1)S(1)} %pair_bias.1.own, ...), custom_call_target="tpu_custom_call" | custom-call | tf_op jit(solution)/shard_map/softmax_stats/pallas_call | solution.py:321
  23.3 0.0 copy-start
  23.3 0.0 copy-start.1
  23.3 0.0 copy-start.2
  23.3 0.0 copy-start.7
  23.3 0.0 copy-start.8
  23.3 0.0 copy-start.9
  23.3 21.0 %all_to_all.25.gathered = f32[8,32,256]{2,1,0:T(8,128)S(1)} all-to-all(f32[8,32,256]{2,1,0:T(8,128)} %get-tuple-element.36), channel_id=1, replica_groups=mesh['zl'=4,'x'=4,'qi'=2,'zh'=2,'y'=4] {'zh','y'}, dimensions={0} | all-to-all | bytes 524288 | tf_op jit(solution)/shard_map/all_to_all | solution.py:306
  44.3 1.5 %score_grads.1 = (bf16[16,128,128]{2,1,0:T(8,128)(2,1)}, bf16[1024,256]{1,0:T(8,128)(2,1)}, bf16[1024,256]{1,0:T(8,128)(2,1)}) custom-call(f32[8,32,256]{2,1,0:T(8,128)S(1)} %all_to_all.25.gathered, f32[1024,256]{1,0:T(8,128)S(1)} %get-tuple-element.37.total, f32[1024,256]{1,0:T(8,128)S(1)} %get-tuple-element.35.attend), custom_call_target="tpu_custom_call" | custom-call | tf_op jit(solution)/shard_map/score_grads/pallas_call | solution.py:321
  45.8 5.0 %all-to-all-start.1 = ((bf16[16,128,128]{2,1,0:T(8,128)(2,1)}), bf16[16,128,128]{2,1,0:T(8,128)(2,1)S(1)}, u32[]{:S(2)}, u32[]{:S(2)}) async-start(bf16[16,128,128]{2,1,0:T(8,128)(2,1)} %get-tuple-element.49), calls=%async_computation.1 | async-start | bytes 1048576 | tf_op jit(solution)/shard_map/all_to_all | solution.py:306
  50.8 3.4 %row_grads.1 = (bf16[2,32,768]{2,1,0:T(8,128)(2,1)S(1)}, bf16[2,32,768]{2,1,0:T(8,128)(2,1)S(1)}, bf16[2,32,768]{2,1,0:T(8,128)(2,1)S(1)}, bf16[2,32,768]{2,1,0:...) custom-call(s32[5]{0:T(128)S(1)} %stack.23.place, bf16[1024,256]{1,0:T(8,128)(2,1)} %get-tuple-element.38.score_low, ...), custom_call_target="tpu_custom_call" | custom-call | tf_op jit(solution)/shard_map/row_grads/pallas_call | solution.py:321
  54.2 0.1 collective-permute-start.3
  54.3 2.7 %collective-permute-start.4 = (bf16[2,32,768]{2,1,0:T(8,128)(2,1)S(1)}, bf16[2,32,768]{2,1,0:T(8,128)(2,1)S(1)}, u32[]{:S(2)}, u32[]{:S(2)}) collective-permute-start(bf16[2,32,768]{2,1,0:T(8,128)(2,1)S(1)} %get-tuple-element.45), channel_id=1, source_target_pairs={{0,3},{1,0},{2,1},{3,2},{4,7},{5,4},{6,5},{7,6},{8,11},{9,8},{10,9... | collective-permute-start | bytes 294920 | tf_op jit(solution)/shard_map/ppermute | solution.py:302
  57.0 0.4 collective-permute-start.5
  57.3 5.6 %all-to-all-done.1.received = bf16[16,128,128]{2,1,0:T(8,128)(2,1)S(1)} async-done(((bf16[16,128,128]{2,1,0:T(8,128)(2,1)}), bf16[16,128,128]{2,1,0:T(8,128)(2,1)S(1)}, u32[]{:S(2)}, u32[]{:S(2)}) %all-to-all-start.1) | async-done | bytes 524320 | tf_op jit(solution)/shard_map/all_to_all | solution.py:306
  62.9 0.0 copy-done
  62.9 0.0 copy-done.1
  62.9 0.0 copy-done.2
  62.9 0.0 copy-done.7
  63.0 0.0 copy-done.8
  63.0 0.0 copy-done.9
  63.0 6.5 %pair_backward.1 = (bf16[16,2,32,128]{3,2,1,0:T(8,128)(2,1)}, bf16[1792,128]{1,0:T(8,128)(2,1)}) custom-call(s32[5]{0:T(128)S(1)} %stack.23.place, bf16[16,128,128]{2,1,0:T(8,128)(2,1)S(1)} %all-to-all-done.1.received, bf16[256,2,32,128]{3,2,1,0:T(8,128)(2,1)} %pair.3, f32[1,128]{1,0:T(1,128)S(1)} %bitcast.42, bf16[128,512]{1,0:T(8,128)(2,1)S(1)} %copy-done, ...), custom_call_target="tpu_custom_call" | custom-call | tf_op jit(solution)/shard_map/pair_backward/pallas_call | solution.py:321
  69.5 8.8 %all-to-all-start.2 = ((bf16[32,56,128]{2,1,0:T(8,128)(2,1)}), bf16[32,56,128]{2,1,0:T(8,128)(2,1)S(1)}, u32[]{:S(2)}, u32[]{:S(2)}) async-start(bf16[32,56,128]{2,1,0:T(8,128)(2,1)} %bitcast.45), calls=%async_computation.2 | async-start | bytes 917504 | tf_op jit(solution)/shard_map/all_to_all | solution.py:306
  78.3 0.0 collective-permute-done.3
  78.3 0.0 collective-permute-done.4
  78.3 0.0 collective-permute-done.5
  78.3 0.1 convert_add_fusion
  78.4 0.4 collective-permute-start.6
  78.8 0.5 collective-permute-start.7
  79.3 9.5 %all-to-all-done.2.parts = bf16[32,56,128]{2,1,0:T(8,128)(2,1)S(1)} async-done(((bf16[32,56,128]{2,1,0:T(8,128)(2,1)}), bf16[32,56,128]{2,1,0:T(8,128)(2,1)S(1)}, u32[]{:S(2)}, u32[]{:S(2)}) %all-to-all-start.2) | async-done | bytes 458784 | tf_op jit(solution)/shard_map/all_to_all | solution.py:306
  88.8 0.7 plane_sum.1
  89.5 3.4 %all-to-all-start.3 = ((bf16[8,56,128]{2,1,0:T(8,128)(2,1)}), bf16[8,56,128]{2,1,0:T(8,128)(2,1)S(1)}, u32[]{:S(2)}, u32[]{:S(2)}) async-start(bf16[8,56,128]{2,1,0:T(8,128)(2,1)} %plane_sum.1), calls=%async_computation.3 | async-start | bytes 229376 | tf_op jit(solution)/shard_map/all_to_all | solution.py:306
  92.9 0.0 collective-permute-done.6
  92.9 0.6 fusion.2
  93.6 6.9 %all-to-all-done.3.parts = bf16[8,56,128]{2,1,0:T(8,128)(2,1)S(1)} async-done(((bf16[8,56,128]{2,1,0:T(8,128)(2,1)}), bf16[8,56,128]{2,1,0:T(8,128)(2,1)S(1)}, u32[]{:S(2)}, u32[]{:S(2)}) %all-to-all-start.3) | async-done | bytes 114720 | tf_op jit(solution)/shard_map/all_to_all | solution.py:306
  100.4 0.8 column_sum.1
  101.3 5.7 %all-to-all-start.4 = ((bf16[32,56,128]{2,1,0:T(8,128)(2,1)}), bf16[32,56,128]{2,1,0:T(8,128)(2,1)S(1)}, u32[]{:S(2)}, u32[]{:S(2)}) async-start(bf16[32,56,128]{2,1,0:T(8,128)(2,1)} %column_sum.1), calls=%async_computation.4 | async-start | bytes 917504 | tf_op jit(solution)/shard_map/all_to_all | solution.py:306
  107.0 0.0 collective-permute-done.7
  107.0 0.6 slice_bitcast_fusion.1
  107.7 9.9 %all-to-all-done.4 = bf16[32,56,128]{2,1,0:T(8,128)(2,1)S(1)} async-done(((bf16[32,56,128]{2,1,0:T(8,128)(2,1)}), bf16[32,56,128]{2,1,0:T(8,128)(2,1)S(1)}, u32[]{:S(2)}, u32[]{:S(2)}) %all-to-all-start.4) | async-done | bytes 458784 | tf_op jit(solution)/shard_map/all_to_all | solution.py:306
  117.6 0.9 unpack.1
  (2 shorter events, 0.0 us)
Async XLA Ops:
  0.6 12.3 %copy-start.4 = (bf16[1,256,768]{2,1,0:T(8,128)(2,1)S(1)}, bf16[1,256,768]{2,1,0:T(8,128)(2,1)}, u32[]{:S(2)}) copy-start(bf16[1,256,768]{2,1,0:T(8,128)(2,1)} %param.15) | copy-start | bytes 1179652
  0.7 12.3 %copy-start.6 = (bf16[1,2,32,768]{3,2,1,0:T(8,128)(2,1)S(1)}, bf16[1,2,32,768]{3,2,1,0:T(8,128)(2,1)}, u32[]{:S(2)}) copy-start(bf16[1,2,32,768]{3,2,1,0:T(8,128)(2,1)} %param.14) | copy-start | bytes 294916
  0.7 12.3 %copy-start.5 = (bf16[1,2,32,768]{3,2,1,0:T(8,128)(2,1)S(1)}, bf16[1,2,32,768]{3,2,1,0:T(8,128)(2,1)}, u32[]{:S(2)}) copy-start(bf16[1,2,32,768]{3,2,1,0:T(8,128)(2,1)} %param.13) | copy-start | bytes 294916
  0.7 12.3 %copy-start.3 = (bf16[1,256,768]{2,1,0:T(8,128)(2,1)S(1)}, bf16[1,256,768]{2,1,0:T(8,128)(2,1)}, u32[]{:S(2)}) copy-start(bf16[1,256,768]{2,1,0:T(8,128)(2,1)} %param.12) | copy-start | bytes 1179652
  8.5 6.9 %collective-permute-start.2 = (bf16[4,128,128]{2,1,0:T(8,128)(2,1)S(1)}, bf16[4,128,128]{2,1,0:T(8,128)(2,1)S(1)}, u32[]{:S(2)}, u32[]{:S(2)}) collective-permute-start(bf16[4,128,128]{2,1,0:T(8,128)(2,1)S(1)} %pair_bias.1.own), channel_id=1, source_target_pairs={{0,48},{16,0},{32,16},{48,32},{1,49},{17,1},{33,17},{49,33},{2,50}... | collective-permute-start | bytes 393224 | tf_op jit(solution)/shard_map/ppermute | solution.py:302
  11.9 5.4 %collective-permute-start.1 = (bf16[4,128,128]{2,1,0:T(8,128)(2,1)S(1)}, bf16[4,128,128]{2,1,0:T(8,128)(2,1)S(1)}, u32[]{:S(2)}, u32[]{:S(2)}) collective-permute-start(bf16[4,128,128]{2,1,0:T(8,128)(2,1)S(1)} %pair_bias.1.own), channel_id=1, source_target_pairs={{0,32},{16,48},{32,0},{48,16},{1,33},{17,49},{33,1},{49,17},{2,34}... | collective-permute-start | bytes 393224 | tf_op jit(solution)/shard_map/ppermute | solution.py:302
  12.4 9.0 %collective-permute-start = (bf16[4,128,128]{2,1,0:T(8,128)(2,1)S(1)}, bf16[4,128,128]{2,1,0:T(8,128)(2,1)S(1)}, u32[]{:S(2)}, u32[]{:S(2)}) collective-permute-start(bf16[4,128,128]{2,1,0:T(8,128)(2,1)S(1)} %pair_bias.1.own), channel_id=1, source_target_pairs={{0,16},{16,32},{32,48},{48,0},{1,17},{17,33},{33,49},{49,1},{2,18}... | collective-permute-start | bytes 393224 | tf_op jit(solution)/shard_map/ppermute | solution.py:302
  23.3 39.7 %copy-start = (bf16[128,512]{1,0:T(8,128)(2,1)S(1)}, bf16[128,512]{1,0:T(8,128)(2,1)}, u32[]{:S(2)}) copy-start(bf16[128,512]{1,0:T(8,128)(2,1)} %gate_w.1) | copy-start | bytes 393220
  23.3 39.7 %copy-start.1 = (bf16[128,512]{1,0:T(8,128)(2,1)S(1)}, bf16[128,512]{1,0:T(8,128)(2,1)}, u32[]{:S(2)}) copy-start(bf16[128,512]{1,0:T(8,128)(2,1)} %up_w.1) | copy-start | bytes 393220
  23.3 39.7 %copy-start.2 = (bf16[512,128]{1,0:T(8,128)(2,1)S(1)}, bf16[512,128]{1,0:T(8,128)(2,1)}, u32[]{:S(2)}) copy-start(bf16[512,128]{1,0:T(8,128)(2,1)} %down_w.1) | copy-start | bytes 393220
  23.3 39.7 %copy-start.7 = (bf16[128,16]{0,1:T(8,128)(2,1)S(1)}, bf16[128,16]{0,1:T(8,128)(2,1)}, u32[]{:S(2)}) copy-start(bf16[128,16]{0,1:T(8,128)(2,1)} %param.21) | copy-start | bytes 12292
  23.3 39.7 %copy-start.8 = (f32[128]{0:T(128)S(1)}, f32[128]{0:T(128)}, u32[]{:S(2)}) copy-start(f32[128]{0:T(128)} %param.16) | copy-start | bytes 1540
  23.3 39.7 %copy-start.9 = (f32[128]{0:T(128)S(1)}, f32[128]{0:T(128)}, u32[]{:S(2)}) copy-start(f32[128]{0:T(128)} %param.20) | copy-start | bytes 1540
  45.8 17.1 %all-to-all-start.1 = ((bf16[16,128,128]{2,1,0:T(8,128)(2,1)}), bf16[16,128,128]{2,1,0:T(8,128)(2,1)S(1)}, u32[]{:S(2)}, u32[]{:S(2)}) async-start(bf16[16,128,128]{2,1,0:T(8,128)(2,1)} %get-tuple-element.49), calls=%async_computation.1 | async-start | bytes 1048576 | tf_op jit(solution)/shard_map/all_to_all | solution.py:306
  54.2 24.1 %collective-permute-start.3 = (bf16[2,32,768]{2,1,0:T(8,128)(2,1)S(1)}, bf16[2,32,768]{2,1,0:T(8,128)(2,1)S(1)}, u32[]{:S(2)}, u32[]{:S(2)}) collective-permute-start(bf16[2,32,768]{2,1,0:T(8,128)(2,1)S(1)} %get-tuple-element.44), channel_id=1, source_target_pairs={{0,1},{1,2},{2,3},{3,0},{4,5},{5,6},{6,7},{7,4},{8,9},{9,10},{10,1... | collective-permute-start | bytes 294920 | tf_op jit(solution)/shard_map/ppermute | solution.py:302
  54.3 24.0 %collective-permute-start.4 = (bf16[2,32,768]{2,1,0:T(8,128)(2,1)S(1)}, bf16[2,32,768]{2,1,0:T(8,128)(2,1)S(1)}, u32[]{:S(2)}, u32[]{:S(2)}) collective-permute-start(bf16[2,32,768]{2,1,0:T(8,128)(2,1)S(1)} %get-tuple-element.45), channel_id=1, source_target_pairs={{0,3},{1,0},{2,1},{3,2},{4,7},{5,4},{6,5},{7,6},{8,11},{9,8},{10,9... | collective-permute-start | bytes 294920 | tf_op jit(solution)/shard_map/ppermute | solution.py:302
  57.0 21.4 %collective-permute-start.5 = (bf16[2,32,768]{2,1,0:T(8,128)(2,1)S(1)}, bf16[2,32,768]{2,1,0:T(8,128)(2,1)S(1)}, u32[]{:S(2)}, u32[]{:S(2)}) collective-permute-start(bf16[2,32,768]{2,1,0:T(8,128)(2,1)S(1)} %get-tuple-element.46), channel_id=1, source_target_pairs={{0,2},{1,3},{2,0},{3,1},{4,6},{5,7},{6,4},{7,5},{8,10},{9,11},{10,... | collective-permute-start | bytes 294920 | tf_op jit(solution)/shard_map/ppermute | solution.py:302
  69.5 19.4 %all-to-all-start.2 = ((bf16[32,56,128]{2,1,0:T(8,128)(2,1)}), bf16[32,56,128]{2,1,0:T(8,128)(2,1)S(1)}, u32[]{:S(2)}, u32[]{:S(2)}) async-start(bf16[32,56,128]{2,1,0:T(8,128)(2,1)} %bitcast.45), calls=%async_computation.2 | async-start | bytes 917504 | tf_op jit(solution)/shard_map/all_to_all | solution.py:306
  78.4 14.5 %collective-permute-start.6 = (bf16[32,768]{1,0:T(8,128)(2,1)S(1)}, bf16[32,768]{1,0:T(8,128)(2,1)S(1)}, u32[]{:S(2)}, u32[]{:S(2)}) collective-permute-start(bf16[32,768]{1,0:T(8,128)(2,1)S(1)} %fusion.3), channel_id=1, source_target_pairs={{0,4},{4,0},{1,5},{5,1},{2,6},{6,2},{3,7},{7,3},{8,12},{12,8},{9,1... | collective-permute-start | bytes 147464 | tf_op jit(solution)/shard_map/ppermute | solution.py:302
  78.8 28.2 %collective-permute-start.7 = (f32[32,1536]{1,0:T(8,128)S(1)}, f32[32,1536]{1,0:T(8,128)S(1)}, u32[]{:S(2)}, u32[]{:S(2)}) collective-permute-start(f32[32,1536]{1,0:T(8,128)S(1)} %get-tuple-element.48), channel_id=1, source_target_pairs={{0,8},{8,0},{1,9},{9,1},{2,10},{10,2},{3,11},{11,3},{4,12},{12,4},... | collective-permute-start | bytes 589832 | tf_op jit(solution)/shard_map/ppermute | solution.py:302
  89.5 10.9 %all-to-all-start.3 = ((bf16[8,56,128]{2,1,0:T(8,128)(2,1)}), bf16[8,56,128]{2,1,0:T(8,128)(2,1)S(1)}, u32[]{:S(2)}, u32[]{:S(2)}) async-start(bf16[8,56,128]{2,1,0:T(8,128)(2,1)} %plane_sum.1), calls=%async_computation.3 | async-start | bytes 229376 | tf_op jit(solution)/shard_map/all_to_all | solution.py:306
  101.3 16.3 %all-to-all-start.4 = ((bf16[32,56,128]{2,1,0:T(8,128)(2,1)}), bf16[32,56,128]{2,1,0:T(8,128)(2,1)S(1)}, u32[]{:S(2)}, u32[]{:S(2)}) async-start(bf16[32,56,128]{2,1,0:T(8,128)(2,1)} %column_sum.1), calls=%async_computation.4 | async-start | bytes 917504 | tf_op jit(solution)/shard_map/all_to_all | solution.py:306

commit v3 on v2

--- a/solution.py
+++ b/solution.py
@@ -163,22 +163,25 @@
         weighted = jnp.sum(powers * attend[rows, :], axis=0, keepdims=True)
         logs.append(largest + jnp.log(amount))
         means.append(weighted / amount)
-    packed = jnp.concatenate(logs + means, axis=0)
-    for j in range(8):
-        stats[j] = packed
-
-
-def grad_kernel(gathered, total, attend, send, score_low, attend_low):
-    peers = [gathered[j] for j in range(8)]
-    largest = functools.reduce(jnp.maximum, [p[:HEADS] for p in peers])
-    amount = jnp.zeros((HEADS, ROWS), F32)
-    weighted = jnp.zeros((HEADS, ROWS), F32)
-    for p in peers:
-        power = jnp.exp(p[:HEADS] - largest)
-        amount = amount + power
-        weighted = weighted + p[HEADS:] * power
-    level = largest + jnp.log(amount)
-    delta = weighted / amount
+    stats[...] = jnp.concatenate(logs + means, axis=0)
+
+
+def merge_stats(parts):
+    largest = functools.reduce(jnp.maximum, [p[:HEADS] for p in parts])
+    powers = [jnp.exp(p[:HEADS] - largest) for p in parts]
+    amount = functools.reduce(jnp.add, powers)
+    weighted = functools.reduce(jnp.add, [p[HEADS:] * w for p, w in zip(parts, powers)])
+    return largest + jnp.log(amount), weighted / amount
+
+
+def merge_kernel(own, received, after, merged):
+    level, delta = merge_stats([own[...], received[...]])
+    merged[:HEADS, :] = level
+    merged[HEADS:, :] = delta
+
+
+def grad_kernel(own, first, second, third, total, attend, send, score_low, attend_low):
+    level, delta = merge_stats([own[...], first[...], second[...], third[...]])
     for pair in range(HEADS // 2):
         blocks = []
         for h in (2 * pair, 2 * pair + 1):
@@ -225,76 +228,117 @@
         kv_send[:, lanes] = jnp.where(qi == 0, second, first)
 
 
-def pair_kernel(
-    place, received, pair, gain1, gate_w, up_w, down_w, gain2, head_t,
-    pair_out, weights, rows, cells_v, sems,
-):
-    copies = fetch((pair.at[pl.ds(place[0] * SUB, SUB)],), (cells_v,), sems)
+def state_kernel(
+    place, after, pair, gain1, gate_w, up_w, down_w, gain2, head_t,
+    post_normed_s, post_inverse_s, gate_slope, up_slope, pre_t, hidden_s, post_low,
+    pre_normed_s, pre_inverse_s, cells_v, sems,
+):
+    for copy in fetch((pair.at[pl.ds(place[0] * SUB, SUB)],), (cells_v,), sems):
+        copy.wait()
+    cells = block_cells(lambda r: cells_v[r].reshape(KEYS, PAIR)).astype(F32)
+    normed, inverse = layer_norm(cells)
+    pre_normed_s[...] = normed
+    pre_inverse_s[...] = jnp.broadcast_to(inverse, normed.shape)
+    scaled = normed * gain1[...]
+    pre_t[...] = scaled.T.astype(BF16)
+    lowered = scaled.astype(BF16)
+    gate = dot(lowered, gate_w[...], NN)
+    up = dot(lowered, up_w[...], NN)
+    silu, sigmoid = silu_parts(gate)
+    hidden = (silu * up).astype(BF16)
+    hidden_s[...] = hidden
+    up_slope[...] = silu.astype(BF16)
+    gate_slope[...] = (up * (sigmoid + silu * (1.0 - sigmoid))).astype(BF16)
+    updated = cells + dot(hidden, down_w[...], NN)
+    normed, inverse = layer_norm(updated)
+    post_normed_s[...] = normed
+    post_inverse_s[...] = jnp.broadcast_to(inverse, normed.shape)
+    post_low[...] = (normed * gain2[...]).astype(BF16)
+
+
+def weight_kernel(
+    received, down_w, gain2, head_t, after, h0, h1, h2, h3, h4, h5, h6,
+    weights, updated_out, rows, weights_v, updated_v,
+    post_normed, post_inverse, gate_slope, up_slope, pre_t, hidden, post_low, sems, out_sems,
+):
+    held = (post_normed, post_inverse, gate_slope, up_slope, pre_t, hidden, post_low)
+    copies = fetch((h0, h1, h2, h3, h4, h5, h6), held, sems)
     rows[...] = jnp.sum(received[...].astype(F32), axis=0)
     low = jnp.concatenate(
         [rows[pl.ds(step, HEADS, stride=8), :] for step in range(8)], axis=1
     ).astype(BF16)
     post_scaled = dot(low, head_t[...], TN)
-    for copy in copies:
-        copy.wait()
-    cells = block_cells(lambda r: cells_v[r].reshape(KEYS, PAIR)).astype(F32)
-    pre_normed, pre_inverse = layer_norm(cells)
-    pre_low = (pre_normed * gain1[...]).astype(BF16)
-    gate = dot(pre_low, gate_w[...], NN)
-    up = dot(pre_low, up_w[...], NN)
-    silu, sigmoid = silu_parts(gate)
-    hidden = (silu * up).astype(BF16)
-    gate_slope = up * (sigmoid + silu * (1.0 - sigmoid))
-    updated = cells + dot(hidden, down_w[...], NN)
-    post_normed, post_inverse = layer_norm(updated)
-    post_low = (post_normed * gain2[...]).astype(BF16)
-    second_sum = jnp.sum(post_scaled * post_normed, axis=0, keepdims=True)
-    updated_grad = norm_backward(post_scaled * gain2[...], post_normed, post_inverse)
+    copies[0].wait()
+    copies[1].wait()
+    updated_grad = norm_backward(post_scaled * gain2[...], post_normed[...], post_inverse[...])
+    updated_v[...] = updated_grad
+    outs = fetch((updated_v,), (updated_out,), out_sems)
     updated_low = updated_grad.astype(BF16)
     hidden_grad = dot(updated_low, down_w[...], NT)
-    gate_low = (hidden_grad * gate_slope).astype(BF16)
-    up_low = (hidden_grad * silu).astype(BF16)
-    gate_part = dot(pre_low, gate_low, TN).astype(BF16)
-    up_part = dot(pre_low, up_low, TN).astype(BF16)
+    for copy in copies[2:]:
+        copy.wait()
+    gate_low = (hidden_grad * gate_slope[...]).astype(BF16)
+    up_low = (hidden_grad * up_slope[...]).astype(BF16)
+    gate_part = dot(pre_t[...], gate_low, NN).astype(BF16)
+    up_part = dot(pre_t[...], up_low, NN).astype(BF16)
+    down_part = dot(updated_low, hidden[...], TN).astype(BF16)
     for block in range(4):
         lanes = slice(block * 128, (block + 1) * 128)
-        weights[block * 128 : (block + 1) * 128, :] = gate_part[:, lanes]
-        weights[512 + block * 128 : 512 + (block + 1) * 128, :] = up_part[:, lanes]
-    weights[1024:1536, :] = dot(hidden, updated_low, TN).astype(BF16)
-    weights[1536:1552, :] = dot(low, post_low, NN).astype(BF16)
+        for first, part in ((0, gate_part), (512, up_part), (1024, down_part)):
+            weights_v[first + block * 128 : first + (block + 1) * 128, :] = part[:, lanes]
+    weights_v[1536:1552, :] = dot(low, post_low[...], NN).astype(BF16)
+    weights_v[1552:, :] = jnp.zeros((CHUNKS * CHUNK_ROWS - 1552, PAIR), BF16)
+    last = fetch((weights_v,), (weights,), out_sems.at[pl.ds(1, 1)])
+    for copy in (*outs, *last):
+        copy.wait()
+
+
+def inputs_kernel(
+    after, updated_grad, gate_slope, up_slope, pre_normed, pre_inverse, gain1, gate_w, up_w, down_w,
+    pair_out,
+):
+    hidden_grad = dot(updated_grad[...].astype(BF16), down_w[...], NT)
+    gate_low = (hidden_grad * gate_slope[...]).astype(BF16)
+    up_low = (hidden_grad * up_slope[...]).astype(BF16)
     pre_scaled = dot(gate_low, gate_w[...], NT) + dot(up_low, up_w[...], NT)
-    first_sum = jnp.sum(pre_scaled * pre_normed, axis=0, keepdims=True)
-    inputs_grad = norm_backward(pre_scaled * gain1[...], pre_normed, pre_inverse)
-    result = (updated_grad + inputs_grad).astype(BF16)
+    inputs_grad = norm_backward(pre_scaled * gain1[...], pre_normed[...], pre_inverse[...])
+    result = (updated_grad[...] + inputs_grad).astype(BF16)
     for step in range(8):
         for half in range(2):
             start = step * 128 + half * KEYS
             slab = result[start : start + KEYS]
             pair_out[half * 8 + step] = slab.reshape(2, 32, PAIR)
-    gains = jnp.concatenate([first_sum, second_sum, jnp.zeros((14, PAIR), F32)], axis=0)
-    weights[1552:1568, :] = gains.astype(BF16)
-    weights[1568:, :] = jnp.zeros((CHUNK_ROWS * CHUNKS - 1568, PAIR), BF16)
-
-
-def sum_kernel(parts, out):
+
+
+def sum_kernel(parts, *rest):
+    out = rest[-1]
     total = jnp.sum(parts[...].astype(F32), axis=0).astype(out.dtype)
     for j in range(out.shape[0]):
         out[j] = total
 
 
-def unpack_kernel(table, gate_out, up_out, down_out, head_out, first_out, second_out):
+def unpack_kernel(
+    table, gain1, gate_w, up_w, gain2, head_t,
+    gate_out, up_out, down_out, head_out, first_out, second_out,
+):
     factor = 1.0 / 512
-    for block in range(4):
-        lanes = slice(block * 128, (block + 1) * 128)
-        rows = slice(block * 128, (block + 1) * 128)
-        later = slice(512 + block * 128, 512 + (block + 1) * 128)
-        gate_out[:, lanes] = table[rows, :].astype(F32) * factor
-        up_out[:, lanes] = table[later, :].astype(F32) * factor
-    down_out[...] = table[1024:1536, :].astype(F32) * factor
-    rest = table[1536:1568, :].astype(F32) * factor
-    head_out[...] = rest[:16]
-    first_out[...] = rest[16:17]
-    second_out[...] = rest[17:18]
+
+    def block(k):
+        return table[k * 128 : (k + 1) * 128, :].astype(F32) * factor
+
+    total = jnp.zeros((PAIR, 128), F32)
+    for k in range(4):
+        lanes = slice(k * 128, (k + 1) * 128)
+        gate, up = block(k), block(4 + k)
+        gate_out[:, lanes] = gate
+        up_out[:, lanes] = up
+        down_out[lanes, :] = block(8 + k).T
+        total = total + gate * gate_w[:, lanes].astype(F32) + up * up_w[:, lanes].astype(F32)
+    head = block(12)[:HEADS]
+    head_out[...] = head
+    first_out[...] = jnp.sum(total.T, axis=0, keepdims=True) / gain1[...]
+    second = jnp.sum(head * head_t[...].astype(F32), axis=0, keepdims=True)
+    second_out[...] = second / gain2[...]
 
 
 def shifted(value, axis, shift):
@@ -376,16 +420,35 @@
     total, stats = call(
         stats_kernel,
         [(SMEM, place), *vmem(scores, attend, own, first, second, third)],
-        [f32(HEADS * KEYS, ROWS), f32_kept(8, 2 * HEADS, ROWS)],
+        [f32(HEADS * KEYS, ROWS), f32(2 * HEADS, ROWS)],
         "softmax_stats",
         [pltpu.VMEM((4, 4, 128, 128), F32)],
     )
 
-    gathered = all_to_all(stats, ("zh", "y"))
+    cells = SUB * KEYS
+    states = call(
+        state_kernel,
+        [(SMEM, place), *vmem(total), in_hbm(pair_rep), *vmem(*params)],
+        [
+            f32_kept(cells, PAIR), f32_kept(cells, PAIR), bf16_kept(cells, FF),
+            bf16_kept(cells, FF), bf16_kept(PAIR, cells), bf16_kept(cells, FF),
+            bf16_kept(cells, PAIR), f32_kept(cells, PAIR), f32_kept(cells, PAIR),
+        ],
+        "pair_states",
+        [pltpu.VMEM((SUB, 2, 32, PAIR), BF16), pltpu.SemaphoreType.DMA((1,))],
+    )
+
+    (merged,) = call(
+        merge_kernel,
+        [*vmem(stats, shifted(stats, "zh", 1)), in_hbm(states[0])],
+        [f32(2 * HEADS, ROWS)],
+        "merge_stats",
+    )
+    peers = [shifted(merged, "y", s) for s in (1, 3, 2)]
 
     send, score_low, attend_low = call(
         grad_kernel,
-        vmem(gathered, total, attend),
+        vmem(merged, *peers, total, attend),
         [bf16_kept(16, 128, 128), *[bf16_kept(HEADS * KEYS, ROWS)] * 2],
         "score_grads",
     )
@@ -410,21 +473,40 @@
     value_grad = kv_sum[None, :, WIDTH:]
 
     weight_rows = CHUNK_ROWS * CHUNKS
-    pair_low, weights = call(
-        pair_kernel,
-        [(SMEM, place), *vmem(received), in_hbm(pair_rep), *vmem(*params)],
-        [bf16_kept(SUB, 2, 32, PAIR), bf16_kept(weight_rows, PAIR)],
-        "pair_backward",
+    weights, updated_grad = call(
+        weight_kernel,
+        [
+            *vmem(received, *params[3:], half),
+            *[in_hbm(v) for v in states[:7]],
+        ],
+        [
+            (HBM, pltpu.HBM((weight_rows, PAIR), BF16)),
+            (HBM, pltpu.HBM((cells, PAIR), F32)),
+        ],
+        "pair_weights",
         [
             pltpu.VMEM((128, 128), F32),
-            pltpu.VMEM((SUB, 2, 32, PAIR), BF16),
-            pltpu.SemaphoreType.DMA((1,)),
-        ],
+            pltpu.VMEM((weight_rows, PAIR), BF16),
+            pltpu.VMEM((cells, PAIR), F32),
+            *[pltpu.VMEM(v.shape, v.dtype) for v in states[:7]],
+            pltpu.SemaphoreType.DMA((7,)),
+            pltpu.SemaphoreType.DMA((2,)),
+        ],
+    )
+    (pair_low,) = call(
+        inputs_kernel,
+        [in_hbm(weights), *kept(updated_grad, *states[2:4], *states[7:9], *params[:4])],
+        [bf16_kept(SUB, 2, 32, PAIR)],
+        "pair_inputs",
     )
     pair_grad = pair_low[None, None]
-
     parts = all_to_all(weights.reshape(CHUNKS, CHUNK_ROWS, PAIR), PLANE)
-    (shares,) = call(sum_kernel, vmem(parts), [bf16_kept(8, CHUNK_ROWS, PAIR)], "plane_sum")
+    (shares,) = call(
+        sum_kernel,
+        [*vmem(parts), in_hbm(pair_low)],
+        [bf16_kept(8, CHUNK_ROWS, PAIR)],
+        "plane_sum",
+    )
     columns = all_to_all(shares, COLUMN)
     (totals,) = call(
         sum_kernel, vmem(columns), [bf16_kept(CHUNKS, CHUNK_ROWS, PAIR)], "column_sum"
@@ -432,7 +514,7 @@
     table = all_to_all(totals, PLANE).reshape(weight_rows, PAIR)
     gate_grad, up_grad, down_grad, head_grad, first_grad, second_grad = call(
         unpack_kernel,
-        vmem(table),
+        vmem(table, *params[:3], *params[4:]),
         [
             f32_kept(PAIR, FF), f32_kept(PAIR, FF), f32_kept(FF, PAIR),
             f32_kept(HEADS, PAIR), f32_kept(1, PAIR), f32_kept(1, PAIR),

time: 119 us -> 115 us (0.966)
  blocking collectives: 21 us -> 0 us
  starting transfers between devices: 31.4 us -> 43.4 us
  Pallas kernels: 25.6 us -> 32.4 us
  waiting for transfers between devices: 38.1 us -> 36.1 us
    all_to_all x1 -> x0, blocking collectives: 21 us -> none  [all_to_all(): return lax.all_to_all(value, axes, 0, 0, tiled=True)]
    ppermute x8 -> x12, starting transfers between devices: 8.5 us -> 21.2 us  [shifted(): lax.ppermute(value, axis, [(i, (i + shift) % size) for i in range(size)])]
    all_to_all x4, waiting for transfers between devices: 31.9 us -> 21.4 us  [all_to_all(): return lax.all_to_all(value, axes, 0, 0, tiled=True)]
    ppermute x8 -> x12, waiting for transfers between devices: 6.2 us -> 14.7 us  [shifted(): lax.ppermute(value, axis, [(i, (i + shift) % size) for i in range(size)])]
    pallas_call x9 -> x12, Pallas kernels: 25.6 us -> 32.4 us  [call(): pl.pallas_call(kernel, in_specs=[spec for spec, _ in ins], out_specs=[spe...]
  transfers between devices with their start and end apart: 12 -> 16, of which waited for: 7 -> 12; matrix products, arithmetic and copies ran while one was open for 1% -> 1% of each run, Pallas kernels for 12% -> 15%
where the time goes in v3:
time: 115 us; the launch traced here: 114 us
  starting transfers between devices  43.4 us (38%)
  waiting for transfers between devices  36.1 us (31%)
  Pallas kernels  32.4 us (28%)
    pallas_call x12, Pallas kernels, call(): pl.pallas_call(kernel, in_specs=[spec for spec, _ in ins], out_specs=[spe...  32.4 us
    all_to_all x4, starting transfers between devices, all_to_all(): return lax.all_to_all(value, axes, 0, 0, tiled=True)  22.2 us
    all_to_all x4, waiting for transfers between devices, all_to_all(): return lax.all_to_all(value, axes, 0, 0, tiled=True)  21.4 us
    ppermute x12, starting transfers between devices, shifted(): lax.ppermute(value, axis, [(i, (i + shift) % size) for i in range(size)])  21.2 us
    ppermute x12, waiting for transfers between devices, shifted(): lax.ppermute(value, axis, [(i, (i + shift) % size) for i in range(size)])  14.7 us
  transfers between devices with their start and end apart: 16, of which 12 were waited for; matrix products, arithmetic and copies ran while one was open for 1% of the time, Pallas kernels for 15%

profile of v3, /device:TPU:1, one launch (start us, length us, event | category | flops | bytes accessed | tf_op | source)
XLA Modules:
  0.0 114.4 jit_solution(18299272064545351532)
XLA Ops:
  0.6 0.0 copy-start.6
  0.7 0.0 copy-start.8
  0.7 0.0 copy-start.7
  0.7 0.0 copy-start
  0.7 0.0 copy-start.1
  0.7 0.0 copy-start.3
  0.7 0.0 copy-start.9
  0.7 0.0 copy-start.10
  0.7 0.0 copy-start.12
  0.8 0.1 stack.23.place
  0.8 7.7 %pair_bias.1.own = bf16[4,128,128]{2,1,0:T(8,128)(2,1)S(1)} custom-call(s32[5]{0:T(128)S(1)} %stack.23.place, bf16[256,2,32,128]{3,2,1,0:T(8,128)(2,1)} %pair.3, f32[1,128]{1,0:T(1,128)} %bitcast.43, bf16[128,512]{1,0:T(8,128)(2,1)} %gate_w.5, bf16[128,512]{1,0:T(8,128)(2,1)} %up_w.5, bf16[512,128]{1,0:T(8,128)(2,1)} %down_w.5, f32[1,128]{1,0:T(1,128)} %bitcast.47, ...), custom_call_target="tpu_custom_call" | custom-call | tf_op jit(solution)/shard_map/pair_bias/pallas_call | solution.py:365
  8.5 3.4 %collective-permute-start.2 = (bf16[4,128,128]{2,1,0:T(8,128)(2,1)S(1)}, bf16[4,128,128]{2,1,0:T(8,128)(2,1)S(1)}, u32[]{:S(2)}, u32[]{:S(2)}) collective-permute-start(bf16[4,128,128]{2,1,0:T(8,128)(2,1)S(1)} %pair_bias.1.own), channel_id=1, source_target_pairs={{0,48},{16,0},{32,16},{48,32},{1,49},{17,1},{33,17},{49,33},{2,50}... | collective-permute-start | bytes 393224 | tf_op jit(solution)/shard_map/ppermute | solution.py:346
  11.9 0.5 collective-permute-start.1
  12.5 0.6 collective-permute-start
  13.1 0.0 copy-done.6
  13.1 0.0 copy-done.7
  13.1 2.2 %products.1 = (f32[1024,256]{1,0:T(8,128)S(1)}, f32[1024,256]{1,0:T(8,128)S(1)}, bf16[256,768]{1,0:T(8,128)(2,1)}, bf16[256,768]{1,0:T(8,128)(2,1)}, bf16[1024,768]{1,0:T(8,128)(2,1)}) custom-call(bf16[256,768]{1,0:T(8,128)(2,1)S(1)} %bitcast.35, bf16[256,768]{1,0:T(8,128)(2,1)S(1)} %bitcast.36, bf16[2,32,768]{2,1,0:T(8,128)(2,1)S(1)} %bitcast.37, ...), custom_call_target="tpu_custom_call" | custom-call | tf_op jit(solution)/shard_map/products/pallas_call | solution.py:365
  15.3 0.3 collective-permute-done.2.third
  15.5 1.8 %collective-permute-done.1.second = bf16[4,128,128]{2,1,0:T(8,128)(2,1)S(1)} collective-permute-done((bf16[4,128,128]{2,1,0:T(8,128)(2,1)S(1)}, bf16[4,128,128]{2,1,0:T(8,128)(2,1)S(1)}, u32[]{:S(2)}, u32[]{:S(2)}) %collective-permute-start.1) | collective-permute-done | bytes 131104 | tf_op jit(solution)/shard_map/ppermute | solution.py:346
  17.4 4.1 %collective-permute-done.first = bf16[4,128,128]{2,1,0:T(8,128)(2,1)S(1)} collective-permute-done((bf16[4,128,128]{2,1,0:T(8,128)(2,1)S(1)}, bf16[4,128,128]{2,1,0:T(8,128)(2,1)S(1)}, u32[]{:S(2)}, u32[]{:S(2)}) %collective-permute-start) | collective-permute-done | bytes 131104 | tf_op jit(solution)/shard_map/ppermute | solution.py:346
  21.5 1.1 %softmax_stats.1 = (f32[1024,256]{1,0:T(8,128)S(1)}, f32[32,256]{1,0:T(8,128)S(1)}) custom-call(s32[5]{0:T(128)S(1)} %stack.23.place, f32[1024,256]{1,0:T(8,128)S(1)} %get-tuple-element.43.scores, f32[1024,256]{1,0:T(8,128)S(1)} %get-tuple-element.44.attend, bf16[4,128,128]{2,1,0:T(8,128)(2,1)S(1)} %pair_bias.1.own, ...), custom_call_target="tpu_custom_call" | custom-call | tf_op jit(solution)/shard_map/softmax_stats/pallas_call | solution.py:365
  22.6 7.0 %collective-permute-start.3 = (f32[32,256]{1,0:T(8,128)S(1)}, f32[32,256]{1,0:T(8,128)S(1)}, u32[]{:S(2)}, u32[]{:S(2)}) collective-permute-start(f32[32,256]{1,0:T(8,128)S(1)} %get-tuple-element.45.own), channel_id=1, source_target_pairs={{0,4},{4,0},{1,5},{5,1},{2,6},{6,2},{3,7},{7,3},{8,12},{12,8},{9,1... | collective-permute-start | bytes 98312 | tf_op jit(solution)/shard_map/ppermute | solution.py:346
  29.6 0.0 copy-done
  29.6 0.0 copy-done.10
  29.6 0.0 copy-done.12
  29.7 5.6 %pair_states.1 = (f32[1024,128]{1,0:T(8,128)}, f32[1024,128]{1,0:T(8,128)}, bf16[1024,512]{1,0:T(8,128)(2,1)}, bf16[1024,512]{1,0:T(8,128)(2,1)}, bf16[128,1024]...) custom-call(s32[5]{0:T(128)S(1)} %stack.23.place, ...), custom_call_target="tpu_custom_call" | custom-call | tf_op jit(solution)/shard_map/pair_states/pallas_call | solution.py:365
  35.3 0.0 collective-permute-done.3.received
  35.3 3.0 %collective-permute-start.6 = (f32[32,256]{1,0:T(8,128)S(1)}, f32[32,256]{1,0:T(8,128)S(1)}, u32[]{:S(2)}, u32[]{:S(2)}) collective-permute-start(f32[32,256]{1,0:T(8,128)S(1)} %merge_stats.1.own), channel_id=1, source_target_pairs={{0,2},{1,3},{2,0},{3,1},{4,6},{5,7},{6,4},{7,5},{8,10},{9,11},{10,... | collective-permute-start | bytes 98312 | tf_op jit(solution)/shard_map/ppermute | solution.py:346
  38.3 0.8 collective-permute-start.5
  39.1 0.7 collective-permute-start.4
  39.8 0.0 collective-permute-done.6.third
  39.8 1.6 %collective-permute-done.5.second = f32[32,256]{1,0:T(8,128)S(1)} collective-permute-done((f32[32,256]{1,0:T(8,128)S(1)}, f32[32,256]{1,0:T(8,128)S(1)}, u32[]{:S(2)}, u32[]{:S(2)}) %collective-permute-start.5) | collective-permute-done | bytes 32800 | tf_op jit(solution)/shard_map/ppermute | solution.py:346
  41.4 1.7 %collective-permute-done.4.first = f32[32,256]{1,0:T(8,128)S(1)} collective-permute-done((f32[32,256]{1,0:T(8,128)S(1)}, f32[32,256]{1,0:T(8,128)S(1)}, u32[]{:S(2)}, u32[]{:S(2)}) %collective-permute-start.4) | collective-permute-done | bytes 32800 | tf_op jit(solution)/shard_map/ppermute | solution.py:346
  43.1 1.5 %score_grads.1 = (bf16[16,128,128]{2,1,0:T(8,128)(2,1)}, bf16[1024,256]{1,0:T(8,128)(2,1)}, bf16[1024,256]{1,0:T(8,128)(2,1)}) custom-call(f32[32,256]{1,0:T(8,128)S(1)} %merge_stats.1.own, f32[32,256]{1,0:T(8,128)S(1)} %collective-permute-done.4.first, f32[32,256]{1,0:T(8,128)S(1)} %collective-permute-done.5.second, ...), custom_call_target="tpu_custom_call" | custom-call | tf_op jit(solution)/shard_map/score_grads/pallas_call | solution.py:365
  44.6 3.6 %all-to-all-start = ((bf16[16,128,128]{2,1,0:T(8,128)(2,1)}), bf16[16,128,128]{2,1,0:T(8,128)(2,1)S(1)}, u32[]{:S(2)}, u32[]{:S(2)}) async-start(bf16[16,128,128]{2,1,0:T(8,128)(2,1)} %get-tuple-element.59), calls=%async_computation | async-start | bytes 1048576 | tf_op jit(solution)/shard_map/all_to_all | solution.py:350
  48.2 3.4 %row_grads.1 = (bf16[2,32,768]{2,1,0:T(8,128)(2,1)S(1)}, bf16[2,32,768]{2,1,0:T(8,128)(2,1)S(1)}, bf16[2,32,768]{2,1,0:T(8,128)(2,1)S(1)}, bf16[2,32,768]{2,1,0:...) custom-call(s32[5]{0:T(128)S(1)} %stack.23.place, bf16[1024,256]{1,0:T(8,128)(2,1)} %get-tuple-element.48.score_low, ...), custom_call_target="tpu_custom_call" | custom-call | tf_op jit(solution)/shard_map/row_grads/pallas_call | solution.py:365
  51.6 0.2 collective-permute-start.7
  51.8 2.6 %collective-permute-start.8 = (bf16[2,32,768]{2,1,0:T(8,128)(2,1)S(1)}, bf16[2,32,768]{2,1,0:T(8,128)(2,1)S(1)}, u32[]{:S(2)}, u32[]{:S(2)}) collective-permute-start(bf16[2,32,768]{2,1,0:T(8,128)(2,1)S(1)} %get-tuple-element.55), channel_id=1, source_target_pairs={{0,3},{1,0},{2,1},{3,2},{4,7},{5,4},{6,5},{7,6},{8,11},{9,8},{10,9... | collective-permute-start | bytes 294920 | tf_op jit(solution)/shard_map/ppermute | solution.py:346
  54.4 0.0 collective-permute-start.9
  54.4 2.3 %collective-permute-done.7 = bf16[2,32,768]{2,1,0:T(8,128)(2,1)S(1)} collective-permute-done((bf16[2,32,768]{2,1,0:T(8,128)(2,1)S(1)}, bf16[2,32,768]{2,1,0:T(8,128)(2,1)S(1)}, u32[]{:S(2)}, u32[]{:S(2)}) %collective-permute-start.7) | collective-permute-done | bytes 98336 | tf_op jit(solution)/shard_map/ppermute | solution.py:346
  56.6 0.3 collective-permute-done.8
  57.0 2.7 %collective-permute-done.9 = bf16[2,32,768]{2,1,0:T(8,128)(2,1)S(1)} collective-permute-done((bf16[2,32,768]{2,1,0:T(8,128)(2,1)S(1)}, bf16[2,32,768]{2,1,0:T(8,128)(2,1)S(1)}, u32[]{:S(2)}, u32[]{:S(2)}) %collective-permute-start.9) | collective-permute-done | bytes 98336 | tf_op jit(solution)/shard_map/ppermute | solution.py:346
  59.7 0.6 all-to-all-done.received
  60.2 4.0 %pair_weights.1 = (bf16[1792,128]{1,0:T(8,128)(2,1)}, f32[1024,128]{1,0:T(8,128)}) custom-call(bf16[16,128,128]{2,1,0:T(8,128)(2,1)S(1)} %all-to-all-done.received, bf16[512,128]{1,0:T(8,128)(2,1)S(1)} %copy-done, f32[1,128]{1,0:T(1,128)S(1)} %bitcast.49, bf16[16,128]{1,0:T(8,128)(2,1)S(1)} %bitcast.41, f32[2,32,768]{2,1,0:T(8,128)S(1)} %convert_add_fusion.after, ...), custom_call_target="tpu_custom_call" | custom-call | tf_op jit(solution)/shard_map/pair_weights/pallas_call | solution.py:365
  64.2 8.6 %all-to-all-start.1 = ((bf16[32,56,128]{2,1,0:T(8,128)(2,1)}), bf16[32,56,128]{2,1,0:T(8,128)(2,1)S(1)}, u32[]{:S(2)}, u32[]{:S(2)}) async-start(bf16[32,56,128]{2,1,0:T(8,128)(2,1)} %bitcast.51), calls=%async_computation.1 | async-start | bytes 917504 | tf_op jit(solution)/shard_map/all_to_all | solution.py:350
  72.8 0.0 copy-start.2
  72.8 0.0 copy-start.4
  72.9 0.0 copy-start.11
  72.9 1.9 %collective-permute-start.10 = (bf16[32,768]{1,0:T(8,128)(2,1)S(1)}, bf16[32,768]{1,0:T(8,128)(2,1)S(1)}, u32[]{:S(2)}, u32[]{:S(2)}) collective-permute-start(bf16[32,768]{1,0:T(8,128)(2,1)S(1)} %fusion.3), channel_id=1, source_target_pairs={{0,4},{4,0},{1,5},{5,1},{2,6},{6,2},{3,7},{7,3},{8,12},{12,8},{9,1... | collective-permute-start | bytes 147464 | tf_op jit(solution)/shard_map/ppermute | solution.py:346
  74.8 0.5 collective-permute-start.11
  75.3 4.2 %pair_inputs.1.rest_0_ = bf16[16,2,32,128]{3,2,1,0:T(8,128)(2,1)} custom-call(bf16[1792,128]{1,0:T(8,128)(2,1)} %get-tuple-element.66.after, f32[1024,128]{1,0:T(8,128)} %get-tuple-element.67.updated_grad, bf16[1024,512]{1,0:T(8,128)(2,1)} %get-tuple-element.61.h2.gate_slope, bf16[1024,512]{1,0:T(8,128)(2,1)} %get-tuple-element.62.h3.up_slope, ...), custom_call_target="tpu_custom_call" | custom-call | tf_op jit(solution)/shard_map/pair_inputs/pallas_call | solution.py:365
  79.6 3.7 %all-to-all-done.1.parts = bf16[32,56,128]{2,1,0:T(8,128)(2,1)S(1)} async-done(((bf16[32,56,128]{2,1,0:T(8,128)(2,1)}), bf16[32,56,128]{2,1,0:T(8,128)(2,1)S(1)}, u32[]{:S(2)}, u32[]{:S(2)}) %all-to-all-start.1) | async-done | bytes 458784 | tf_op jit(solution)/shard_map/all_to_all | solution.py:350
  83.3 0.7 plane_sum.1
  84.1 4.3 %all-to-all-start.2 = ((bf16[8,56,128]{2,1,0:T(8,128)(2,1)}), bf16[8,56,128]{2,1,0:T(8,128)(2,1)S(1)}, u32[]{:S(2)}, u32[]{:S(2)}) async-start(bf16[8,56,128]{2,1,0:T(8,128)(2,1)} %plane_sum.1), calls=%async_computation.2 | async-start | bytes 229376 | tf_op jit(solution)/shard_map/all_to_all | solution.py:350
  88.3 0.0 collective-permute-done.10
  88.3 0.6 fusion.2
  89.0 7.2 %all-to-all-done.2.parts = bf16[8,56,128]{2,1,0:T(8,128)(2,1)S(1)} async-done(((bf16[8,56,128]{2,1,0:T(8,128)(2,1)}), bf16[8,56,128]{2,1,0:T(8,128)(2,1)S(1)}, u32[]{:S(2)}, u32[]{:S(2)}) %all-to-all-start.2) | async-done | bytes 114720 | tf_op jit(solution)/shard_map/all_to_all | solution.py:350
  96.1 0.8 column_sum.1
  97.0 5.8 %all-to-all-start.3 = ((bf16[32,56,128]{2,1,0:T(8,128)(2,1)}), bf16[32,56,128]{2,1,0:T(8,128)(2,1)S(1)}, u32[]{:S(2)}, u32[]{:S(2)}) async-start(bf16[32,56,128]{2,1,0:T(8,128)(2,1)} %column_sum.1), calls=%async_computation.3 | async-start | bytes 917504 | tf_op jit(solution)/shard_map/all_to_all | solution.py:350
  102.8 0.0 collective-permute-done.11
  102.8 0.6 slice_bitcast_fusion.1
  103.4 9.9 %all-to-all-done.3 = bf16[32,56,128]{2,1,0:T(8,128)(2,1)S(1)} async-done(((bf16[32,56,128]{2,1,0:T(8,128)(2,1)}), bf16[32,56,128]{2,1,0:T(8,128)(2,1)S(1)}, u32[]{:S(2)}, u32[]{:S(2)}) %all-to-all-start.3) | async-done | bytes 458784 | tf_op jit(solution)/shard_map/all_to_all | solution.py:350
  113.4 0.0 copy-done.11
  113.4 1.0 unpack.1
  (12 shorter events, 0.1 us)
Async XLA Ops:
  0.6 12.4 %copy-start.6 = (bf16[1,256,768]{2,1,0:T(8,128)(2,1)S(1)}, bf16[1,256,768]{2,1,0:T(8,128)(2,1)}, u32[]{:S(2)}) copy-start(bf16[1,256,768]{2,1,0:T(8,128)(2,1)} %param.15) | copy-start | bytes 1179652
  0.7 12.4 %copy-start.8 = (bf16[1,2,32,768]{3,2,1,0:T(8,128)(2,1)S(1)}, bf16[1,2,32,768]{3,2,1,0:T(8,128)(2,1)}, u32[]{:S(2)}) copy-start(bf16[1,2,32,768]{3,2,1,0:T(8,128)(2,1)} %param.14) | copy-start | bytes 294916
  0.7 12.4 %copy-start.7 = (bf16[1,2,32,768]{3,2,1,0:T(8,128)(2,1)S(1)}, bf16[1,2,32,768]{3,2,1,0:T(8,128)(2,1)}, u32[]{:S(2)}) copy-start(bf16[1,2,32,768]{3,2,1,0:T(8,128)(2,1)} %param.13) | copy-start | bytes 294916
  0.7 12.4 %copy-start.5 = (bf16[1,256,768]{2,1,0:T(8,128)(2,1)S(1)}, bf16[1,256,768]{2,1,0:T(8,128)(2,1)}, u32[]{:S(2)}) copy-start(bf16[1,256,768]{2,1,0:T(8,128)(2,1)} %param.12) | copy-start | bytes 1179652
  0.7 28.9 %copy-start = (bf16[512,128]{1,0:T(8,128)(2,1)S(1)}, bf16[512,128]{1,0:T(8,128)(2,1)}, u32[]{:S(2)}) copy-start(bf16[512,128]{1,0:T(8,128)(2,1)} %down_w.5) | copy-start | bytes 393220
  0.7 28.9 %copy-start.1 = (bf16[128,512]{1,0:T(8,128)(2,1)S(1)}, bf16[128,512]{1,0:T(8,128)(2,1)}, u32[]{:S(2)}) copy-start(bf16[128,512]{1,0:T(8,128)(2,1)} %gate_w.5) | copy-start | bytes 393220
  0.7 28.9 %copy-start.3 = (bf16[128,512]{1,0:T(8,128)(2,1)S(1)}, bf16[128,512]{1,0:T(8,128)(2,1)}, u32[]{:S(2)}) copy-start(bf16[128,512]{1,0:T(8,128)(2,1)} %up_w.5) | copy-start | bytes 393220
  0.7 28.9 %copy-start.9 = (bf16[128,16]{0,1:T(8,128)(2,1)S(1)}, bf16[128,16]{0,1:T(8,128)(2,1)}, u32[]{:S(2)}) copy-start(bf16[128,16]{0,1:T(8,128)(2,1)} %param.21) | copy-start | bytes 12292
  0.7 28.9 %copy-start.10 = (f32[128]{0:T(128)S(1)}, f32[128]{0:T(128)}, u32[]{:S(2)}) copy-start(f32[128]{0:T(128)} %param.16) | copy-start | bytes 1540
  0.7 28.9 %copy-start.12 = (f32[128]{0:T(128)S(1)}, f32[128]{0:T(128)}, u32[]{:S(2)}) copy-start(f32[128]{0:T(128)} %param.20) | copy-start | bytes 1540
  8.5 7.0 %collective-permute-start.2 = (bf16[4,128,128]{2,1,0:T(8,128)(2,1)S(1)}, bf16[4,128,128]{2,1,0:T(8,128)(2,1)S(1)}, u32[]{:S(2)}, u32[]{:S(2)}) collective-permute-start(bf16[4,128,128]{2,1,0:T(8,128)(2,1)S(1)} %pair_bias.1.own), channel_id=1, source_target_pairs={{0,48},{16,0},{32,16},{48,32},{1,49},{17,1},{33,17},{49,33},{2,50}... | collective-permute-start | bytes 393224 | tf_op jit(solution)/shard_map/ppermute | solution.py:346
  11.9 5.4 %collective-permute-start.1 = (bf16[4,128,128]{2,1,0:T(8,128)(2,1)S(1)}, bf16[4,128,128]{2,1,0:T(8,128)(2,1)S(1)}, u32[]{:S(2)}, u32[]{:S(2)}) collective-permute-start(bf16[4,128,128]{2,1,0:T(8,128)(2,1)S(1)} %pair_bias.1.own), channel_id=1, source_target_pairs={{0,32},{16,48},{32,0},{48,16},{1,33},{17,49},{33,1},{49,17},{2,34}... | collective-permute-start | bytes 393224 | tf_op jit(solution)/shard_map/ppermute | solution.py:346
  12.5 9.0 %collective-permute-start = (bf16[4,128,128]{2,1,0:T(8,128)(2,1)S(1)}, bf16[4,128,128]{2,1,0:T(8,128)(2,1)S(1)}, u32[]{:S(2)}, u32[]{:S(2)}) collective-permute-start(bf16[4,128,128]{2,1,0:T(8,128)(2,1)S(1)} %pair_bias.1.own), channel_id=1, source_target_pairs={{0,16},{16,32},{32,48},{48,0},{1,17},{17,33},{33,49},{49,1},{2,18}... | collective-permute-start | bytes 393224 | tf_op jit(solution)/shard_map/ppermute | solution.py:346
  22.6 12.7 %collective-permute-start.3 = (f32[32,256]{1,0:T(8,128)S(1)}, f32[32,256]{1,0:T(8,128)S(1)}, u32[]{:S(2)}, u32[]{:S(2)}) collective-permute-start(f32[32,256]{1,0:T(8,128)S(1)} %get-tuple-element.45.own), channel_id=1, source_target_pairs={{0,4},{4,0},{1,5},{5,1},{2,6},{6,2},{3,7},{7,3},{8,12},{12,8},{9,1... | collective-permute-start | bytes 98312 | tf_op jit(solution)/shard_map/ppermute | solution.py:346
  35.3 4.5 %collective-permute-start.6 = (f32[32,256]{1,0:T(8,128)S(1)}, f32[32,256]{1,0:T(8,128)S(1)}, u32[]{:S(2)}, u32[]{:S(2)}) collective-permute-start(f32[32,256]{1,0:T(8,128)S(1)} %merge_stats.1.own), channel_id=1, source_target_pairs={{0,2},{1,3},{2,0},{3,1},{4,6},{5,7},{6,4},{7,5},{8,10},{9,11},{10,... | collective-permute-start | bytes 98312 | tf_op jit(solution)/shard_map/ppermute | solution.py:346
  38.3 3.1 %collective-permute-start.5 = (f32[32,256]{1,0:T(8,128)S(1)}, f32[32,256]{1,0:T(8,128)S(1)}, u32[]{:S(2)}, u32[]{:S(2)}) collective-permute-start(f32[32,256]{1,0:T(8,128)S(1)} %merge_stats.1.own), channel_id=1, source_target_pairs={{0,3},{1,0},{2,1},{3,2},{4,7},{5,4},{6,5},{7,6},{8,11},{9,8},{10,9... | collective-permute-start | bytes 98312 | tf_op jit(solution)/shard_map/ppermute | solution.py:346
  39.1 4.0 %collective-permute-start.4 = (f32[32,256]{1,0:T(8,128)S(1)}, f32[32,256]{1,0:T(8,128)S(1)}, u32[]{:S(2)}, u32[]{:S(2)}) collective-permute-start(f32[32,256]{1,0:T(8,128)S(1)} %merge_stats.1.own), channel_id=1, source_target_pairs={{0,1},{1,2},{2,3},{3,0},{4,5},{5,6},{6,7},{7,4},{8,9},{9,10},{10,1... | collective-permute-start | bytes 98312 | tf_op jit(solution)/shard_map/ppermute | solution.py:346
  44.6 15.6 %all-to-all-start = ((bf16[16,128,128]{2,1,0:T(8,128)(2,1)}), bf16[16,128,128]{2,1,0:T(8,128)(2,1)S(1)}, u32[]{:S(2)}, u32[]{:S(2)}) async-start(bf16[16,128,128]{2,1,0:T(8,128)(2,1)} %get-tuple-element.59), calls=%async_computation | async-start | bytes 1048576 | tf_op jit(solution)/shard_map/all_to_all | solution.py:350
  51.6 5.0 %collective-permute-start.7 = (bf16[2,32,768]{2,1,0:T(8,128)(2,1)S(1)}, bf16[2,32,768]{2,1,0:T(8,128)(2,1)S(1)}, u32[]{:S(2)}, u32[]{:S(2)}) collective-permute-start(bf16[2,32,768]{2,1,0:T(8,128)(2,1)S(1)} %get-tuple-element.54), channel_id=1, source_target_pairs={{0,1},{1,2},{2,3},{3,0},{4,5},{5,6},{6,7},{7,4},{8,9},{9,10},{10,1... | collective-permute-start | bytes 294920 | tf_op jit(solution)/shard_map/ppermute | solution.py:346
  51.8 5.2 %collective-permute-start.8 = (bf16[2,32,768]{2,1,0:T(8,128)(2,1)S(1)}, bf16[2,32,768]{2,1,0:T(8,128)(2,1)S(1)}, u32[]{:S(2)}, u32[]{:S(2)}) collective-permute-start(bf16[2,32,768]{2,1,0:T(8,128)(2,1)S(1)} %get-tuple-element.55), channel_id=1, source_target_pairs={{0,3},{1,0},{2,1},{3,2},{4,7},{5,4},{6,5},{7,6},{8,11},{9,8},{10,9... | collective-permute-start | bytes 294920 | tf_op jit(solution)/shard_map/ppermute | solution.py:346
  54.4 5.3 %collective-permute-start.9 = (bf16[2,32,768]{2,1,0:T(8,128)(2,1)S(1)}, bf16[2,32,768]{2,1,0:T(8,128)(2,1)S(1)}, u32[]{:S(2)}, u32[]{:S(2)}) collective-permute-start(bf16[2,32,768]{2,1,0:T(8,128)(2,1)S(1)} %get-tuple-element.56), channel_id=1, source_target_pairs={{0,2},{1,3},{2,0},{3,1},{4,6},{5,7},{6,4},{7,5},{8,10},{9,11},{10,... | collective-permute-start | bytes 294920 | tf_op jit(solution)/shard_map/ppermute | solution.py:346
  64.2 19.1 %all-to-all-start.1 = ((bf16[32,56,128]{2,1,0:T(8,128)(2,1)}), bf16[32,56,128]{2,1,0:T(8,128)(2,1)S(1)}, u32[]{:S(2)}, u32[]{:S(2)}) async-start(bf16[32,56,128]{2,1,0:T(8,128)(2,1)} %bitcast.51), calls=%async_computation.1 | async-start | bytes 917504 | tf_op jit(solution)/shard_map/all_to_all | solution.py:350
  72.8 40.5 %copy-start.2 = (bf16[128,512]{1,0:T(8,128)(2,1)S(1)}, bf16[128,512]{1,0:T(8,128)(2,1)}, u32[]{:S(2)}) copy-start(bf16[128,512]{1,0:T(8,128)(2,1)} %gate_w.5) | copy-start | bytes 393220
  72.8 40.5 %copy-start.4 = (bf16[128,512]{1,0:T(8,128)(2,1)S(1)}, bf16[128,512]{1,0:T(8,128)(2,1)}, u32[]{:S(2)}) copy-start(bf16[128,512]{1,0:T(8,128)(2,1)} %up_w.5) | copy-start | bytes 393220
  72.9 40.5 %copy-start.11 = (f32[128]{0:T(128)S(1)}, f32[128]{0:T(128)}, u32[]{:S(2)}) copy-start(f32[128]{0:T(128)} %param.16) | copy-start | bytes 1540
  72.9 15.5 %collective-permute-start.10 = (bf16[32,768]{1,0:T(8,128)(2,1)S(1)}, bf16[32,768]{1,0:T(8,128)(2,1)S(1)}, u32[]{:S(2)}, u32[]{:S(2)}) collective-permute-start(bf16[32,768]{1,0:T(8,128)(2,1)S(1)} %fusion.3), channel_id=1, source_target_pairs={{0,4},{4,0},{1,5},{5,1},{2,6},{6,2},{3,7},{7,3},{8,12},{12,8},{9,1... | collective-permute-start | bytes 147464 | tf_op jit(solution)/shard_map/ppermute | solution.py:346
  74.8 27.9 %collective-permute-start.11 = (f32[32,1536]{1,0:T(8,128)S(1)}, f32[32,1536]{1,0:T(8,128)S(1)}, u32[]{:S(2)}, u32[]{:S(2)}) collective-permute-start(f32[32,1536]{1,0:T(8,128)S(1)} %get-tuple-element.58), channel_id=1, source_target_pairs={{0,8},{8,0},{1,9},{9,1},{2,10},{10,2},{3,11},{11,3},{4,12},{12,4},... | collective-permute-start | bytes 589832 | tf_op jit(solution)/shard_map/ppermute | solution.py:346
  84.1 12.1 %all-to-all-start.2 = ((bf16[8,56,128]{2,1,0:T(8,128)(2,1)}), bf16[8,56,128]{2,1,0:T(8,128)(2,1)S(1)}, u32[]{:S(2)}, u32[]{:S(2)}) async-start(bf16[8,56,128]{2,1,0:T(8,128)(2,1)} %plane_sum.1), calls=%async_computation.2 | async-start | bytes 229376 | tf_op jit(solution)/shard_map/all_to_all | solution.py:350
  97.0 16.4 %all-to-all-start.3 = ((bf16[32,56,128]{2,1,0:T(8,128)(2,1)}), bf16[32,56,128]{2,1,0:T(8,128)(2,1)S(1)}, u32[]{:S(2)}, u32[]{:S(2)}) async-start(bf16[32,56,128]{2,1,0:T(8,128)(2,1)} %column_sum.1), calls=%async_computation.3 | async-start | bytes 917504 | tf_op jit(solution)/shard_map/all_to_all | solution.py:350

commit v4 on v3

--- a/solution.py
+++ b/solution.py
@@ -59,8 +59,7 @@
     return jnp.concatenate(slabs, axis=0)
 
 
-def silu_parts(gate):
-    half = 0.5 * gate
+def silu_parts(half):
     curve = jnp.tanh(half)
     return half + half * curve, 0.5 + 0.5 * curve
 
@@ -82,14 +81,14 @@
     x = place[1]
     blocks = [pair.at[pl.ds((zl * 4 + x) * SUB, SUB)] for zl in range(4)]
     copies = fetch(
-        (blocks[0], gain1_h, gate_h, up_h, down_h, gain2_h, head_h, *blocks[1:]),
+        (*blocks, gain1_h, gate_h, up_h, down_h, gain2_h, head_h),
         (
-            cells_v.at[0], gain1, gate_w, up_w, down_w, gain2, head_t,
-            cells_v.at[1], cells_v.at[2], cells_v.at[3],
+            cells_v.at[0], cells_v.at[1], cells_v.at[2], cells_v.at[3],
+            gain1, gate_w, up_w, down_w, gain2, head_t,
         ),
         sems,
     )
-    for copy in copies:
+    for copy in copies[:4]:
         copy.wait()
     for start in range(0, 4, GROUP):
         blocks = range(start, start + GROUP)
@@ -97,10 +96,13 @@
             [block_cells(lambda r: cells_v[k, r].reshape(KEYS, PAIR)) for k in blocks], axis=0
         ).astype(F32)
         normed, _ = layer_norm(cells)
+        if start == 0:
+            for copy in copies[4:]:
+                copy.wait()
         lowered = (normed * gain1[...]).astype(BF16)
-        gate = dot(lowered, gate_w[...], NN)
+        half = dot(lowered, gate_w[...] * 0.5, NN)
         up = dot(lowered, up_w[...], NN)
-        hidden = (silu_parts(gate)[0] * up).astype(BF16)
+        hidden = (silu_parts(half)[0] * up).astype(BF16)
         updated = cells + dot(hidden, down_w[...], NN)
         post, _ = layer_norm(updated)
         post_low = (post * gain2[...]).astype(BF16)
@@ -231,20 +233,18 @@
 def state_kernel(
     place, after, pair, gain1, gate_w, up_w, down_w, gain2, head_t,
     post_normed_s, post_inverse_s, gate_slope, up_slope, pre_t, hidden_s, post_low,
-    pre_normed_s, pre_inverse_s, cells_v, sems,
+    cells_v, sems,
 ):
     for copy in fetch((pair.at[pl.ds(place[0] * SUB, SUB)],), (cells_v,), sems):
         copy.wait()
     cells = block_cells(lambda r: cells_v[r].reshape(KEYS, PAIR)).astype(F32)
-    normed, inverse = layer_norm(cells)
-    pre_normed_s[...] = normed
-    pre_inverse_s[...] = jnp.broadcast_to(inverse, normed.shape)
+    normed, _ = layer_norm(cells)
     scaled = normed * gain1[...]
     pre_t[...] = scaled.T.astype(BF16)
     lowered = scaled.astype(BF16)
-    gate = dot(lowered, gate_w[...], NN)
+    half = dot(lowered, gate_w[...] * 0.5, NN)
     up = dot(lowered, up_w[...], NN)
-    silu, sigmoid = silu_parts(gate)
+    silu, sigmoid = silu_parts(half)
     hidden = (silu * up).astype(BF16)
     hidden_s[...] = hidden
     up_slope[...] = silu.astype(BF16)
@@ -279,29 +279,40 @@
         copy.wait()
     gate_low = (hidden_grad * gate_slope[...]).astype(BF16)
     up_low = (hidden_grad * up_slope[...]).astype(BF16)
-    gate_part = dot(pre_t[...], gate_low, NN).astype(BF16)
-    up_part = dot(pre_t[...], up_low, NN).astype(BF16)
-    down_part = dot(updated_low, hidden[...], TN).astype(BF16)
-    for block in range(4):
-        lanes = slice(block * 128, (block + 1) * 128)
-        for first, part in ((0, gate_part), (512, up_part), (1024, down_part)):
+    def give(first, rows_of, k):
+        part = pl.ds(first, rows_of)
+        outs.extend(fetch((weights_v.at[part],), (weights.at[part],), out_sems.at[pl.ds(k, 1)]))
+
+    def place_part(first, part, k):
+        for block in range(4):
+            lanes = slice(block * 128, (block + 1) * 128)
             weights_v[first + block * 128 : first + (block + 1) * 128, :] = part[:, lanes]
+        give(first, 512, k)
+
+    rest = CHUNKS * CHUNK_ROWS - 1536
     weights_v[1536:1552, :] = dot(low, post_low[...], NN).astype(BF16)
-    weights_v[1552:, :] = jnp.zeros((CHUNKS * CHUNK_ROWS - 1552, PAIR), BF16)
-    last = fetch((weights_v,), (weights,), out_sems.at[pl.ds(1, 1)])
-    for copy in (*outs, *last):
+    weights_v[1552:, :] = jnp.zeros((rest - 16, PAIR), BF16)
+    give(1536, rest, 1)
+    place_part(1024, dot(updated_low, hidden[...], TN).astype(BF16), 2)
+    place_part(0, dot(pre_t[...], gate_low, NN).astype(BF16), 3)
+    place_part(512, dot(pre_t[...], up_low, NN).astype(BF16), 4)
+    for copy in outs:
         copy.wait()
 
 
 def inputs_kernel(
-    after, updated_grad, gate_slope, up_slope, pre_normed, pre_inverse, gain1, gate_w, up_w, down_w,
-    pair_out,
-):
+    place, after, pair, updated_grad, gate_slope, up_slope, gain1, gate_w, up_w, down_w,
+    pair_out, cells_v, sems,
+):
+    copies = fetch((pair.at[pl.ds(place[0] * SUB, SUB)],), (cells_v,), sems)
     hidden_grad = dot(updated_grad[...].astype(BF16), down_w[...], NT)
     gate_low = (hidden_grad * gate_slope[...]).astype(BF16)
     up_low = (hidden_grad * up_slope[...]).astype(BF16)
     pre_scaled = dot(gate_low, gate_w[...], NT) + dot(up_low, up_w[...], NT)
-    inputs_grad = norm_backward(pre_scaled * gain1[...], pre_normed[...], pre_inverse[...])
+    for copy in copies:
+        copy.wait()
+    cells = block_cells(lambda r: cells_v[r].reshape(KEYS, PAIR)).astype(F32)
+    inputs_grad = norm_backward(pre_scaled * gain1[...], *layer_norm(cells))
     result = (updated_grad[...] + inputs_grad).astype(BF16)
     for step in range(8):
         for half in range(2):
@@ -310,8 +321,7 @@
             pair_out[half * 8 + step] = slab.reshape(2, 32, PAIR)
 
 
-def sum_kernel(parts, *rest):
-    out = rest[-1]
+def sum_kernel(parts, out):
     total = jnp.sum(parts[...].astype(F32), axis=0).astype(out.dtype)
     for j in range(out.shape[0]):
         out[j] = total
@@ -432,7 +442,7 @@
         [
             f32_kept(cells, PAIR), f32_kept(cells, PAIR), bf16_kept(cells, FF),
             bf16_kept(cells, FF), bf16_kept(PAIR, cells), bf16_kept(cells, FF),
-            bf16_kept(cells, PAIR), f32_kept(cells, PAIR), f32_kept(cells, PAIR),
+            bf16_kept(cells, PAIR),
         ],
         "pair_states",
         [pltpu.VMEM((SUB, 2, 32, PAIR), BF16), pltpu.SemaphoreType.DMA((1,))],
@@ -490,20 +500,13 @@
             pltpu.VMEM((cells, PAIR), F32),
             *[pltpu.VMEM(v.shape, v.dtype) for v in states[:7]],
             pltpu.SemaphoreType.DMA((7,)),
-            pltpu.SemaphoreType.DMA((2,)),
-        ],
-    )
-    (pair_low,) = call(
-        inputs_kernel,
-        [in_hbm(weights), *kept(updated_grad, *states[2:4], *states[7:9], *params[:4])],
-        [bf16_kept(SUB, 2, 32, PAIR)],
-        "pair_inputs",
-    )
-    pair_grad = pair_low[None, None]
+            pltpu.SemaphoreType.DMA((5,)),
+        ],
+    )
     parts = all_to_all(weights.reshape(CHUNKS, CHUNK_ROWS, PAIR), PLANE)
     (shares,) = call(
         sum_kernel,
-        [*vmem(parts), in_hbm(pair_low)],
+        vmem(parts),
         [bf16_kept(8, CHUNK_ROWS, PAIR)],
         "plane_sum",
     )
@@ -511,6 +514,17 @@
     (totals,) = call(
         sum_kernel, vmem(columns), [bf16_kept(CHUNKS, CHUNK_ROWS, PAIR)], "column_sum"
     )
+    (pair_low,) = call(
+        inputs_kernel,
+        [
+            (SMEM, place), in_hbm(totals), in_hbm(pair_rep),
+            *kept(updated_grad, *states[2:4], *params[:4]),
+        ],
+        [bf16_kept(SUB, 2, 32, PAIR)],
+        "pair_inputs",
+        [pltpu.VMEM((SUB, 2, 32, PAIR), BF16), pltpu.SemaphoreType.DMA((1,))],
+    )
+    pair_grad = pair_low[None, None]
     table = all_to_all(totals, PLANE).reshape(weight_rows, PAIR)
     gate_grad, up_grad, down_grad, head_grad, first_grad, second_grad = call(
         unpack_kernel,

time: 115 us -> 113 us (0.983)
  Pallas kernels: 32.4 us -> 31.1 us
    pallas_call x12, Pallas kernels: 32.4 us -> 31.1 us  [call(): pl.pallas_call(kernel, in_specs=[spec for spec, _ in ins], out_specs=[spe...]
where the time goes in v4:
time: 113 us
  starting transfers between devices  43.9 us (39%)
  waiting for transfers between devices  35.4 us (31%)
  Pallas kernels  31.1 us (28%)
    pallas_call x12, Pallas kernels, call(): pl.pallas_call(kernel, in_specs=[spec for spec, _ in ins], out_specs=[spe...  31.1 us
    all_to_all x4, starting transfers between devices, all_to_all(): return lax.all_to_all(value, axes, 0, 0, tiled=True)  22.2 us
    ppermute x12, starting transfers between devices, shifted(): lax.ppermute(value, axis, [(i, (i + shift) % size) for i in range(size)])  21.7 us
    all_to_all x4, waiting for transfers between devices, all_to_all(): return lax.all_to_all(value, axes, 0, 0, tiled=True)  20.6 us
    ppermute x12, waiting for transfers between devices, shifted(): lax.ppermute(value, axis, [(i, (i + shift) % size) for i in range(size)])  14.7 us
  transfers between devices with their start and end apart: 16, of which 12 were waited for; matrix products, arithmetic and copies ran while one was open for 1% of the time, Pallas kernels for 15%

profile of v4, /device:TPU:1, one launch (start us, length us, event | category | flops | bytes accessed | tf_op | source)
XLA Modules:
  0.0 112.8 jit_solution(5929791680476732746)
XLA Ops:
  0.6 0.0 copy-start.6
  0.7 0.0 copy-start.8
  0.7 0.0 copy-start.7
  0.7 0.0 copy-start.5
  0.7 0.0 copy-start
  0.7 0.0 copy-start.1
  0.7 0.0 copy-start.3
  0.7 0.0 copy-start.9
  0.7 0.0 copy-start.10
  0.7 0.0 copy-start.12
  0.8 0.1 stack.23.place
  0.8 6.8 %pair_bias.1.own = bf16[4,128,128]{2,1,0:T(8,128)(2,1)S(1)} custom-call(s32[5]{0:T(128)S(1)} %stack.23.place, bf16[256,2,32,128]{3,2,1,0:T(8,128)(2,1)} %pair.5, f32[1,128]{1,0:T(1,128)} %bitcast.43, bf16[128,512]{1,0:T(8,128)(2,1)} %gate_w.5, bf16[128,512]{1,0:T(8,128)(2,1)} %up_w.5, bf16[512,128]{1,0:T(8,128)(2,1)} %down_w.5, f32[1,128]{1,0:T(1,128)} %bitcast.47, ...), custom_call_target="tpu_custom_call" | custom-call | tf_op jit(solution)/shard_map/pair_bias/pallas_call | solution.py:375
  7.7 3.4 %collective-permute-start.2 = (bf16[4,128,128]{2,1,0:T(8,128)(2,1)S(1)}, bf16[4,128,128]{2,1,0:T(8,128)(2,1)S(1)}, u32[]{:S(2)}, u32[]{:S(2)}) collective-permute-start(bf16[4,128,128]{2,1,0:T(8,128)(2,1)S(1)} %pair_bias.1.own), channel_id=1, source_target_pairs={{0,48},{16,0},{32,16},{48,32},{1,49},{17,1},{33,17},{49,33},{2,50}... | collective-permute-start | bytes 393224 | tf_op jit(solution)/shard_map/ppermute | solution.py:356
  11.1 0.5 collective-permute-start.1
  11.6 0.6 collective-permute-start
  12.2 0.0 copy-done.6
  12.2 2.2 %products.1 = (f32[1024,256]{1,0:T(8,128)S(1)}, f32[1024,256]{1,0:T(8,128)S(1)}, bf16[256,768]{1,0:T(8,128)(2,1)}, bf16[256,768]{1,0:T(8,128)(2,1)}, bf16[1024,768]{1,0:T(8,128)(2,1)}) custom-call(bf16[256,768]{1,0:T(8,128)(2,1)S(1)} %bitcast.35, bf16[256,768]{1,0:T(8,128)(2,1)S(1)} %bitcast.36, bf16[2,32,768]{2,1,0:T(8,128)(2,1)S(1)} %bitcast.37, ...), custom_call_target="tpu_custom_call" | custom-call | tf_op jit(solution)/shard_map/products/pallas_call | solution.py:375
  14.4 0.2 collective-permute-done.2.third
  14.6 1.9 %collective-permute-done.1.second = bf16[4,128,128]{2,1,0:T(8,128)(2,1)S(1)} collective-permute-done((bf16[4,128,128]{2,1,0:T(8,128)(2,1)S(1)}, bf16[4,128,128]{2,1,0:T(8,128)(2,1)S(1)}, u32[]{:S(2)}, u32[]{:S(2)}) %collective-permute-start.1) | collective-permute-done | bytes 131104 | tf_op jit(solution)/shard_map/ppermute | solution.py:356
  16.5 4.1 %collective-permute-done.first = bf16[4,128,128]{2,1,0:T(8,128)(2,1)S(1)} collective-permute-done((bf16[4,128,128]{2,1,0:T(8,128)(2,1)S(1)}, bf16[4,128,128]{2,1,0:T(8,128)(2,1)S(1)}, u32[]{:S(2)}, u32[]{:S(2)}) %collective-permute-start) | collective-permute-done | bytes 131104 | tf_op jit(solution)/shard_map/ppermute | solution.py:356
  20.6 1.1 softmax_stats.1
  21.7 7.0 %collective-permute-start.3 = (f32[32,256]{1,0:T(8,128)S(1)}, f32[32,256]{1,0:T(8,128)S(1)}, u32[]{:S(2)}, u32[]{:S(2)}) collective-permute-start(f32[32,256]{1,0:T(8,128)S(1)} %get-tuple-element.43.own), channel_id=1, source_target_pairs={{0,4},{4,0},{1,5},{5,1},{2,6},{6,2},{3,7},{7,3},{8,12},{12,8},{9,1... | collective-permute-start | bytes 98312 | tf_op jit(solution)/shard_map/ppermute | solution.py:356
  28.7 0.0 copy-done.9
  28.7 0.0 copy-done.10
  28.8 0.0 copy-done.12
  28.8 5.1 %pair_states.1 = (f32[1024,128]{1,0:T(8,128)}, f32[1024,128]{1,0:T(8,128)}, bf16[1024,512]{1,0:T(8,128)(2,1)}, bf16[1024,512]{1,0:T(8,128)(2,1)}, bf16[128,1024]...) custom-call(s32[5]{0:T(128)S(1)} %stack.23.place, ...), custom_call_target="tpu_custom_call" | custom-call | tf_op jit(solution)/shard_map/pair_states/pallas_call | solution.py:375
  33.9 0.0 collective-permute-done.3.received
  33.9 3.0 %collective-permute-start.6 = (f32[32,256]{1,0:T(8,128)S(1)}, f32[32,256]{1,0:T(8,128)S(1)}, u32[]{:S(2)}, u32[]{:S(2)}) collective-permute-start(f32[32,256]{1,0:T(8,128)S(1)} %merge_stats.1.own), channel_id=1, source_target_pairs={{0,2},{1,3},{2,0},{3,1},{4,6},{5,7},{6,4},{7,5},{8,10},{9,11},{10,... | collective-permute-start | bytes 98312 | tf_op jit(solution)/shard_map/ppermute | solution.py:356
  36.9 0.8 collective-permute-start.5
  37.7 0.7 collective-permute-start.4
  38.4 0.0 collective-permute-done.6.third
  38.4 1.6 %collective-permute-done.5.second = f32[32,256]{1,0:T(8,128)S(1)} collective-permute-done((f32[32,256]{1,0:T(8,128)S(1)}, f32[32,256]{1,0:T(8,128)S(1)}, u32[]{:S(2)}, u32[]{:S(2)}) %collective-permute-start.5) | collective-permute-done | bytes 32800 | tf_op jit(solution)/shard_map/ppermute | solution.py:356
  40.0 1.7 %collective-permute-done.4.first = f32[32,256]{1,0:T(8,128)S(1)} collective-permute-done((f32[32,256]{1,0:T(8,128)S(1)}, f32[32,256]{1,0:T(8,128)S(1)}, u32[]{:S(2)}, u32[]{:S(2)}) %collective-permute-start.4) | collective-permute-done | bytes 32800 | tf_op jit(solution)/shard_map/ppermute | solution.py:356
  41.7 1.5 %score_grads.1 = (bf16[16,128,128]{2,1,0:T(8,128)(2,1)}, bf16[1024,256]{1,0:T(8,128)(2,1)}, bf16[1024,256]{1,0:T(8,128)(2,1)}) custom-call(f32[32,256]{1,0:T(8,128)S(1)} %merge_stats.1.own, f32[32,256]{1,0:T(8,128)S(1)} %collective-permute-done.4.first, f32[32,256]{1,0:T(8,128)S(1)} %collective-permute-done.5.second, ...), custom_call_target="tpu_custom_call" | custom-call | tf_op jit(solution)/shard_map/score_grads/pallas_call | solution.py:375
  43.1 3.6 %all-to-all-start = ((bf16[16,128,128]{2,1,0:T(8,128)(2,1)}), bf16[16,128,128]{2,1,0:T(8,128)(2,1)S(1)}, u32[]{:S(2)}, u32[]{:S(2)}) async-start(bf16[16,128,128]{2,1,0:T(8,128)(2,1)} %get-tuple-element.57), calls=%async_computation | async-start | bytes 1048576 | tf_op jit(solution)/shard_map/all_to_all | solution.py:360
  46.7 3.4 %row_grads.1 = (bf16[2,32,768]{2,1,0:T(8,128)(2,1)S(1)}, bf16[2,32,768]{2,1,0:T(8,128)(2,1)S(1)}, bf16[2,32,768]{2,1,0:T(8,128)(2,1)S(1)}, bf16[2,32,768]{2,1,0:...) custom-call(s32[5]{0:T(128)S(1)} %stack.23.place, bf16[1024,256]{1,0:T(8,128)(2,1)} %get-tuple-element.46.score_low, ...), custom_call_target="tpu_custom_call" | custom-call | tf_op jit(solution)/shard_map/row_grads/pallas_call | solution.py:375
  50.1 0.2 collective-permute-start.7
  50.3 2.6 %collective-permute-start.8 = (bf16[2,32,768]{2,1,0:T(8,128)(2,1)S(1)}, bf16[2,32,768]{2,1,0:T(8,128)(2,1)S(1)}, u32[]{:S(2)}, u32[]{:S(2)}) collective-permute-start(bf16[2,32,768]{2,1,0:T(8,128)(2,1)S(1)} %get-tuple-element.53), channel_id=1, source_target_pairs={{0,3},{1,0},{2,1},{3,2},{4,7},{5,4},{6,5},{7,6},{8,11},{9,8},{10,9... | collective-permute-start | bytes 294920 | tf_op jit(solution)/shard_map/ppermute | solution.py:356
  52.9 0.0 collective-permute-start.9
  52.9 2.3 %collective-permute-done.7 = bf16[2,32,768]{2,1,0:T(8,128)(2,1)S(1)} collective-permute-done((bf16[2,32,768]{2,1,0:T(8,128)(2,1)S(1)}, bf16[2,32,768]{2,1,0:T(8,128)(2,1)S(1)}, u32[]{:S(2)}, u32[]{:S(2)}) %collective-permute-start.7) | collective-permute-done | bytes 98336 | tf_op jit(solution)/shard_map/ppermute | solution.py:356
  55.2 0.3 collective-permute-done.8
  55.5 2.7 %collective-permute-done.9 = bf16[2,32,768]{2,1,0:T(8,128)(2,1)S(1)} collective-permute-done((bf16[2,32,768]{2,1,0:T(8,128)(2,1)S(1)}, bf16[2,32,768]{2,1,0:T(8,128)(2,1)S(1)}, u32[]{:S(2)}, u32[]{:S(2)}) %collective-permute-start.9) | collective-permute-done | bytes 98336 | tf_op jit(solution)/shard_map/ppermute | solution.py:356
  58.2 0.6 all-to-all-done.received
  58.8 3.9 %pair_weights.1 = (bf16[1792,128]{1,0:T(8,128)(2,1)}, f32[1024,128]{1,0:T(8,128)}) custom-call(bf16[16,128,128]{2,1,0:T(8,128)(2,1)S(1)} %all-to-all-done.received, bf16[512,128]{1,0:T(8,128)(2,1)S(1)} %copy-done, f32[1,128]{1,0:T(1,128)S(1)} %bitcast.49, bf16[16,128]{1,0:T(8,128)(2,1)S(1)} %bitcast.41, f32[2,32,768]{2,1,0:T(8,128)S(1)} %convert_add_fusion.after, ...), custom_call_target="tpu_custom_call" | custom-call | tf_op jit(solution)/shard_map/pair_weights/pallas_call | solution.py:375
  62.7 8.6 %all-to-all-start.1 = ((bf16[32,56,128]{2,1,0:T(8,128)(2,1)}), bf16[32,56,128]{2,1,0:T(8,128)(2,1)S(1)}, u32[]{:S(2)}, u32[]{:S(2)}) async-start(bf16[32,56,128]{2,1,0:T(8,128)(2,1)} %bitcast.51), calls=%async_computation.1 | async-start | bytes 917504 | tf_op jit(solution)/shard_map/all_to_all | solution.py:360
  71.3 2.5 %collective-permute-start.10 = (bf16[32,768]{1,0:T(8,128)(2,1)S(1)}, bf16[32,768]{1,0:T(8,128)(2,1)S(1)}, u32[]{:S(2)}, u32[]{:S(2)}) collective-permute-start(bf16[32,768]{1,0:T(8,128)(2,1)S(1)} %fusion.3), channel_id=1, source_target_pairs={{0,4},{4,0},{1,5},{5,1},{2,6},{6,2},{3,7},{7,3},{8,12},{12,8},{9,1... | collective-permute-start | bytes 147464 | tf_op jit(solution)/shard_map/ppermute | solution.py:356
  73.7 0.5 collective-permute-start.11
  74.3 7.5 %all-to-all-done.1.parts = bf16[32,56,128]{2,1,0:T(8,128)(2,1)S(1)} async-done(((bf16[32,56,128]{2,1,0:T(8,128)(2,1)}), bf16[32,56,128]{2,1,0:T(8,128)(2,1)S(1)}, u32[]{:S(2)}, u32[]{:S(2)}) %all-to-all-start.1) | async-done | bytes 458784 | tf_op jit(solution)/shard_map/all_to_all | solution.py:360
  81.8 0.7 plane_sum.1
  82.5 4.3 %all-to-all-start.2 = ((bf16[8,56,128]{2,1,0:T(8,128)(2,1)}), bf16[8,56,128]{2,1,0:T(8,128)(2,1)S(1)}, u32[]{:S(2)}, u32[]{:S(2)}) async-start(bf16[8,56,128]{2,1,0:T(8,128)(2,1)} %plane_sum.1), calls=%async_computation.2 | async-start | bytes 229376 | tf_op jit(solution)/shard_map/all_to_all | solution.py:360
  86.8 0.0 collective-permute-done.10
  86.8 0.6 fusion.2
  87.4 7.2 %all-to-all-done.2.parts = bf16[8,56,128]{2,1,0:T(8,128)(2,1)S(1)} async-done(((bf16[8,56,128]{2,1,0:T(8,128)(2,1)}), bf16[8,56,128]{2,1,0:T(8,128)(2,1)S(1)}, u32[]{:S(2)}, u32[]{:S(2)}) %all-to-all-start.2) | async-done | bytes 114720 | tf_op jit(solution)/shard_map/all_to_all | solution.py:360
  94.6 0.8 column_sum.1.after
  95.4 5.8 %all-to-all-start.3 = ((bf16[32,56,128]{2,1,0:T(8,128)(2,1)}), bf16[32,56,128]{2,1,0:T(8,128)(2,1)S(1)}, u32[]{:S(2)}, u32[]{:S(2)}) async-start(bf16[32,56,128]{2,1,0:T(8,128)(2,1)} %column_sum.1.after), calls=%async_computation.3 | async-start | bytes 917504 | tf_op jit(solution)/shard_map/all_to_all | solution.py:360
  101.2 0.0 collective-permute-done.11
  101.2 0.0 copy-start.2
  101.2 0.0 copy-start.4
  101.2 0.0 copy-start.11
  101.3 0.6 slice_bitcast_fusion.1
  101.9 4.5 %pair_inputs.1 = bf16[16,2,32,128]{3,2,1,0:T(8,128)(2,1)} custom-call(s32[5]{0:T(128)S(1)} %stack.23.place, bf16[32,56,128]{2,1,0:T(8,128)(2,1)} %column_sum.1.after, bf16[256,2,32,128]{3,2,1,0:T(8,128)(2,1)} %pair.5, f32[1024,128]{1,0:T(8,128)} %get-tuple-element.65.updated_grad, bf16[1024,512]{1,0:T(8,128)(2,1)} %get-tuple-element.59.h2.gate_slope, ...), custom_call_target="tpu_custom_call" | custom-call | tf_op jit(solution)/shard_map/pair_inputs/pallas_call | solution.py:375
  106.4 5.4 %all-to-all-done.3 = bf16[32,56,128]{2,1,0:T(8,128)(2,1)S(1)} async-done(((bf16[32,56,128]{2,1,0:T(8,128)(2,1)}), bf16[32,56,128]{2,1,0:T(8,128)(2,1)S(1)}, u32[]{:S(2)}, u32[]{:S(2)}) %all-to-all-start.3) | async-done | bytes 458784 | tf_op jit(solution)/shard_map/all_to_all | solution.py:360
  111.8 0.0 copy-done.11
  111.8 1.0 unpack.1
  (12 shorter events, 0.1 us)
Async XLA Ops:
  0.6 11.6 %copy-start.6 = (bf16[1,256,768]{2,1,0:T(8,128)(2,1)S(1)}, bf16[1,256,768]{2,1,0:T(8,128)(2,1)}, u32[]{:S(2)}) copy-start(bf16[1,256,768]{2,1,0:T(8,128)(2,1)} %param.15) | copy-start | bytes 1179652
  0.7 11.5 %copy-start.8 = (bf16[1,2,32,768]{3,2,1,0:T(8,128)(2,1)S(1)}, bf16[1,2,32,768]{3,2,1,0:T(8,128)(2,1)}, u32[]{:S(2)}) copy-start(bf16[1,2,32,768]{3,2,1,0:T(8,128)(2,1)} %param.14) | copy-start | bytes 294916
  0.7 11.5 %copy-start.7 = (bf16[1,2,32,768]{3,2,1,0:T(8,128)(2,1)S(1)}, bf16[1,2,32,768]{3,2,1,0:T(8,128)(2,1)}, u32[]{:S(2)}) copy-start(bf16[1,2,32,768]{3,2,1,0:T(8,128)(2,1)} %param.13) | copy-start | bytes 294916
  0.7 11.5 %copy-start.5 = (bf16[1,256,768]{2,1,0:T(8,128)(2,1)S(1)}, bf16[1,256,768]{2,1,0:T(8,128)(2,1)}, u32[]{:S(2)}) copy-start(bf16[1,256,768]{2,1,0:T(8,128)(2,1)} %param.12) | copy-start | bytes 1179652
  0.7 28.0 %copy-start = (bf16[512,128]{1,0:T(8,128)(2,1)S(1)}, bf16[512,128]{1,0:T(8,128)(2,1)}, u32[]{:S(2)}) copy-start(bf16[512,128]{1,0:T(8,128)(2,1)} %down_w.5) | copy-start | bytes 393220
  0.7 28.0 %copy-start.1 = (bf16[128,512]{1,0:T(8,128)(2,1)S(1)}, bf16[128,512]{1,0:T(8,128)(2,1)}, u32[]{:S(2)}) copy-start(bf16[128,512]{1,0:T(8,128)(2,1)} %gate_w.5) | copy-start | bytes 393220
  0.7 28.0 %copy-start.3 = (bf16[128,512]{1,0:T(8,128)(2,1)S(1)}, bf16[128,512]{1,0:T(8,128)(2,1)}, u32[]{:S(2)}) copy-start(bf16[128,512]{1,0:T(8,128)(2,1)} %up_w.5) | copy-start | bytes 393220
  0.7 28.0 %copy-start.9 = (bf16[128,16]{0,1:T(8,128)(2,1)S(1)}, bf16[128,16]{0,1:T(8,128)(2,1)}, u32[]{:S(2)}) copy-start(bf16[128,16]{0,1:T(8,128)(2,1)} %param.21) | copy-start | bytes 12292
  0.7 28.0 %copy-start.10 = (f32[128]{0:T(128)S(1)}, f32[128]{0:T(128)}, u32[]{:S(2)}) copy-start(f32[128]{0:T(128)} %param.16) | copy-start | bytes 1540
  0.7 28.0 %copy-start.12 = (f32[128]{0:T(128)S(1)}, f32[128]{0:T(128)}, u32[]{:S(2)}) copy-start(f32[128]{0:T(128)} %param.20) | copy-start | bytes 1540
  7.7 6.9 %collective-permute-start.2 = (bf16[4,128,128]{2,1,0:T(8,128)(2,1)S(1)}, bf16[4,128,128]{2,1,0:T(8,128)(2,1)S(1)}, u32[]{:S(2)}, u32[]{:S(2)}) collective-permute-start(bf16[4,128,128]{2,1,0:T(8,128)(2,1)S(1)} %pair_bias.1.own), channel_id=1, source_target_pairs={{0,48},{16,0},{32,16},{48,32},{1,49},{17,1},{33,17},{49,33},{2,50}... | collective-permute-start | bytes 393224 | tf_op jit(solution)/shard_map/ppermute | solution.py:356
  11.1 5.4 %collective-permute-start.1 = (bf16[4,128,128]{2,1,0:T(8,128)(2,1)S(1)}, bf16[4,128,128]{2,1,0:T(8,128)(2,1)S(1)}, u32[]{:S(2)}, u32[]{:S(2)}) collective-permute-start(bf16[4,128,128]{2,1,0:T(8,128)(2,1)S(1)} %pair_bias.1.own), channel_id=1, source_target_pairs={{0,32},{16,48},{32,0},{48,16},{1,33},{17,49},{33,1},{49,17},{2,34}... | collective-permute-start | bytes 393224 | tf_op jit(solution)/shard_map/ppermute | solution.py:356
  11.6 9.0 %collective-permute-start = (bf16[4,128,128]{2,1,0:T(8,128)(2,1)S(1)}, bf16[4,128,128]{2,1,0:T(8,128)(2,1)S(1)}, u32[]{:S(2)}, u32[]{:S(2)}) collective-permute-start(bf16[4,128,128]{2,1,0:T(8,128)(2,1)S(1)} %pair_bias.1.own), channel_id=1, source_target_pairs={{0,16},{16,32},{32,48},{48,0},{1,17},{17,33},{33,49},{49,1},{2,18}... | collective-permute-start | bytes 393224 | tf_op jit(solution)/shard_map/ppermute | solution.py:356
  21.7 12.2 %collective-permute-start.3 = (f32[32,256]{1,0:T(8,128)S(1)}, f32[32,256]{1,0:T(8,128)S(1)}, u32[]{:S(2)}, u32[]{:S(2)}) collective-permute-start(f32[32,256]{1,0:T(8,128)S(1)} %get-tuple-element.43.own), channel_id=1, source_target_pairs={{0,4},{4,0},{1,5},{5,1},{2,6},{6,2},{3,7},{7,3},{8,12},{12,8},{9,1... | collective-permute-start | bytes 98312 | tf_op jit(solution)/shard_map/ppermute | solution.py:356
  33.9 4.5 %collective-permute-start.6 = (f32[32,256]{1,0:T(8,128)S(1)}, f32[32,256]{1,0:T(8,128)S(1)}, u32[]{:S(2)}, u32[]{:S(2)}) collective-permute-start(f32[32,256]{1,0:T(8,128)S(1)} %merge_stats.1.own), channel_id=1, source_target_pairs={{0,2},{1,3},{2,0},{3,1},{4,6},{5,7},{6,4},{7,5},{8,10},{9,11},{10,... | collective-permute-start | bytes 98312 | tf_op jit(solution)/shard_map/ppermute | solution.py:356
  36.9 3.1 %collective-permute-start.5 = (f32[32,256]{1,0:T(8,128)S(1)}, f32[32,256]{1,0:T(8,128)S(1)}, u32[]{:S(2)}, u32[]{:S(2)}) collective-permute-start(f32[32,256]{1,0:T(8,128)S(1)} %merge_stats.1.own), channel_id=1, source_target_pairs={{0,3},{1,0},{2,1},{3,2},{4,7},{5,4},{6,5},{7,6},{8,11},{9,8},{10,9... | collective-permute-start | bytes 98312 | tf_op jit(solution)/shard_map/ppermute | solution.py:356
  37.7 4.0 %collective-permute-start.4 = (f32[32,256]{1,0:T(8,128)S(1)}, f32[32,256]{1,0:T(8,128)S(1)}, u32[]{:S(2)}, u32[]{:S(2)}) collective-permute-start(f32[32,256]{1,0:T(8,128)S(1)} %merge_stats.1.own), channel_id=1, source_target_pairs={{0,1},{1,2},{2,3},{3,0},{4,5},{5,6},{6,7},{7,4},{8,9},{9,10},{10,1... | collective-permute-start | bytes 98312 | tf_op jit(solution)/shard_map/ppermute | solution.py:356
  43.1 15.7 %all-to-all-start = ((bf16[16,128,128]{2,1,0:T(8,128)(2,1)}), bf16[16,128,128]{2,1,0:T(8,128)(2,1)S(1)}, u32[]{:S(2)}, u32[]{:S(2)}) async-start(bf16[16,128,128]{2,1,0:T(8,128)(2,1)} %get-tuple-element.57), calls=%async_computation | async-start | bytes 1048576 | tf_op jit(solution)/shard_map/all_to_all | solution.py:360
  50.1 5.0 %collective-permute-start.7 = (bf16[2,32,768]{2,1,0:T(8,128)(2,1)S(1)}, bf16[2,32,768]{2,1,0:T(8,128)(2,1)S(1)}, u32[]{:S(2)}, u32[]{:S(2)}) collective-permute-start(bf16[2,32,768]{2,1,0:T(8,128)(2,1)S(1)} %get-tuple-element.52), channel_id=1, source_target_pairs={{0,1},{1,2},{2,3},{3,0},{4,5},{5,6},{6,7},{7,4},{8,9},{9,10},{10,1... | collective-permute-start | bytes 294920 | tf_op jit(solution)/shard_map/ppermute | solution.py:356
  50.3 5.2 %collective-permute-start.8 = (bf16[2,32,768]{2,1,0:T(8,128)(2,1)S(1)}, bf16[2,32,768]{2,1,0:T(8,128)(2,1)S(1)}, u32[]{:S(2)}, u32[]{:S(2)}) collective-permute-start(bf16[2,32,768]{2,1,0:T(8,128)(2,1)S(1)} %get-tuple-element.53), channel_id=1, source_target_pairs={{0,3},{1,0},{2,1},{3,2},{4,7},{5,4},{6,5},{7,6},{8,11},{9,8},{10,9... | collective-permute-start | bytes 294920 | tf_op jit(solution)/shard_map/ppermute | solution.py:356
  52.9 5.3 %collective-permute-start.9 = (bf16[2,32,768]{2,1,0:T(8,128)(2,1)S(1)}, bf16[2,32,768]{2,1,0:T(8,128)(2,1)S(1)}, u32[]{:S(2)}, u32[]{:S(2)}) collective-permute-start(bf16[2,32,768]{2,1,0:T(8,128)(2,1)S(1)} %get-tuple-element.54), channel_id=1, source_target_pairs={{0,2},{1,3},{2,0},{3,1},{4,6},{5,7},{6,4},{7,5},{8,10},{9,11},{10,... | collective-permute-start | bytes 294920 | tf_op jit(solution)/shard_map/ppermute | solution.py:356
  62.7 19.1 %all-to-all-start.1 = ((bf16[32,56,128]{2,1,0:T(8,128)(2,1)}), bf16[32,56,128]{2,1,0:T(8,128)(2,1)S(1)}, u32[]{:S(2)}, u32[]{:S(2)}) async-start(bf16[32,56,128]{2,1,0:T(8,128)(2,1)} %bitcast.51), calls=%async_computation.1 | async-start | bytes 917504 | tf_op jit(solution)/shard_map/all_to_all | solution.py:360
  71.3 15.5 %collective-permute-start.10 = (bf16[32,768]{1,0:T(8,128)(2,1)S(1)}, bf16[32,768]{1,0:T(8,128)(2,1)S(1)}, u32[]{:S(2)}, u32[]{:S(2)}) collective-permute-start(bf16[32,768]{1,0:T(8,128)(2,1)S(1)} %fusion.3), channel_id=1, source_target_pairs={{0,4},{4,0},{1,5},{5,1},{2,6},{6,2},{3,7},{7,3},{8,12},{12,8},{9,1... | collective-permute-start | bytes 147464 | tf_op jit(solution)/shard_map/ppermute | solution.py:356
  73.7 27.4 %collective-permute-start.11 = (f32[32,1536]{1,0:T(8,128)S(1)}, f32[32,1536]{1,0:T(8,128)S(1)}, u32[]{:S(2)}, u32[]{:S(2)}) collective-permute-start(f32[32,1536]{1,0:T(8,128)S(1)} %get-tuple-element.56), channel_id=1, source_target_pairs={{0,8},{8,0},{1,9},{9,1},{2,10},{10,2},{3,11},{11,3},{4,12},{12,4},... | collective-permute-start | bytes 589832 | tf_op jit(solution)/shard_map/ppermute | solution.py:356
  82.5 12.1 %all-to-all-start.2 = ((bf16[8,56,128]{2,1,0:T(8,128)(2,1)}), bf16[8,56,128]{2,1,0:T(8,128)(2,1)S(1)}, u32[]{:S(2)}, u32[]{:S(2)}) async-start(bf16[8,56,128]{2,1,0:T(8,128)(2,1)} %plane_sum.1), calls=%async_computation.2 | async-start | bytes 229376 | tf_op jit(solution)/shard_map/all_to_all | solution.py:360
  95.4 16.4 %all-to-all-start.3 = ((bf16[32,56,128]{2,1,0:T(8,128)(2,1)}), bf16[32,56,128]{2,1,0:T(8,128)(2,1)S(1)}, u32[]{:S(2)}, u32[]{:S(2)}) async-start(bf16[32,56,128]{2,1,0:T(8,128)(2,1)} %column_sum.1.after), calls=%async_computation.3 | async-start | bytes 917504 | tf_op jit(solution)/shard_map/all_to_all | solution.py:360
  101.2 10.6 %copy-start.2 = (bf16[128,512]{1,0:T(8,128)(2,1)S(1)}, bf16[128,512]{1,0:T(8,128)(2,1)}, u32[]{:S(2)}) copy-start(bf16[128,512]{1,0:T(8,128)(2,1)} %gate_w.5) | copy-start | bytes 393220
  101.2 10.6 %copy-start.4 = (bf16[128,512]{1,0:T(8,128)(2,1)S(1)}, bf16[128,512]{1,0:T(8,128)(2,1)}, u32[]{:S(2)}) copy-start(bf16[128,512]{1,0:T(8,128)(2,1)} %up_w.5) | copy-start | bytes 393220
  101.2 10.6 %copy-start.11 = (f32[128]{0:T(128)S(1)}, f32[128]{0:T(128)}, u32[]{:S(2)}) copy-start(f32[128]{0:T(128)} %param.16) | copy-start | bytes 1540

commit v5 on v4

--- a/solution.py
+++ b/solution.py
@@ -19,7 +19,7 @@
 SCALE = HEAD_DIM**-0.5
 CHUNK_ROWS = 56
 CHUNKS = 32
-GROUP = 4
+GROUP = 2
 F32 = jnp.float32
 BF16 = jnp.bfloat16
 NOISE = ("zl", "x")
@@ -44,6 +44,18 @@
 
 def layer_norm(values):
     center = values - jnp.mean(values, axis=1, keepdims=True)
+    inverse = lax.rsqrt(jnp.mean(center * center, axis=1, keepdims=True) + EPSILON)
+    return center * inverse, inverse
+
+
+def centering_matrix():
+    row = lax.broadcasted_iota(jnp.int32, (PAIR, PAIR), 0)
+    column = lax.broadcasted_iota(jnp.int32, (PAIR, PAIR), 1)
+    return (jnp.where(row == column, 1.0, 0.0) - 1.0 / PAIR).astype(BF16)
+
+
+def centered_norm(cells, centering):
+    center = dot(cells, centering, NN)
     inverse = lax.rsqrt(jnp.mean(center * center, axis=1, keepdims=True) + EPSILON)
     return center * inverse, inverse
 
@@ -88,30 +100,46 @@
         ),
         sems,
     )
-    for copy in copies[:4]:
+    for copy in copies:
         copy.wait()
-    for start in range(0, 4, GROUP):
-        blocks = range(start, start + GROUP)
+    centering = centering_matrix()
+    groups = [range(start, start + GROUP) for start in range(0, 4, GROUP)]
+
+    def normed_cells(blocks):
         cells = jnp.concatenate(
             [block_cells(lambda r: cells_v[k, r].reshape(KEYS, PAIR)) for k in blocks], axis=0
-        ).astype(F32)
-        normed, _ = layer_norm(cells)
-        if start == 0:
-            for copy in copies[4:]:
-                copy.wait()
+        )
+        return cells.astype(F32), centered_norm(cells, centering)[0]
+
+    def project(cells, normed):
         lowered = (normed * gain1[...]).astype(BF16)
-        half = dot(lowered, gate_w[...] * 0.5, NN)
-        up = dot(lowered, up_w[...], NN)
-        hidden = (silu_parts(half)[0] * up).astype(BF16)
-        updated = cells + dot(hidden, down_w[...], NN)
-        post, _ = layer_norm(updated)
-        post_low = (post * gain2[...]).astype(BF16)
-        bias = dot(head_t[...], post_low, NT)
-        for place_k, k in enumerate(blocks):
-            for step in range(8):
-                lane = place_k * 1024 + step * 128
-                rows[k, pl.ds(step, HEADS, stride=8), :] = bias[:, lane : lane + 128]
-            out[k] = rows[k].astype(BF16)
+        return cells, dot(lowered, gate_w[...] * 0.5, NN), dot(lowered, up_w[...], NN)
+
+    def activate(cells, half, up):
+        return cells, (silu_parts(half)[0] * up).astype(BF16)
+
+    def update(cells, hidden):
+        return (cells + dot(hidden, down_w[...], NN),)
+
+    def lower(updated):
+        return ((layer_norm(updated)[0] * gain2[...]).astype(BF16),)
+
+    stages = (project, activate, update, lower)
+    held = [None] * len(groups)
+    for step in range(len(groups) + len(stages)):
+        for index, blocks in enumerate(groups):
+            stage = step - index
+            if stage == 0:
+                held[index] = normed_cells(blocks)
+            elif 0 < stage <= len(stages):
+                held[index] = stages[stage - 1](*held[index])
+            if stage == len(stages):
+                bias = dot(head_t[...], held[index][0], NT)
+                for order, k in enumerate(blocks):
+                    for row in range(8):
+                        lane = order * 1024 + row * 128
+                        rows[k, pl.ds(row, HEADS, stride=8), :] = bias[:, lane : lane + 128]
+                    out[k] = rows[k].astype(BF16)
 
 
 def head_mask(shape, head):
@@ -237,8 +265,9 @@
 ):
     for copy in fetch((pair.at[pl.ds(place[0] * SUB, SUB)],), (cells_v,), sems):
         copy.wait()
-    cells = block_cells(lambda r: cells_v[r].reshape(KEYS, PAIR)).astype(F32)
-    normed, _ = layer_norm(cells)
+    low_cells = block_cells(lambda r: cells_v[r].reshape(KEYS, PAIR))
+    cells = low_cells.astype(F32)
+    normed, _ = centered_norm(low_cells, centering_matrix())
     scaled = normed * gain1[...]
     pre_t[...] = scaled.T.astype(BF16)
     lowered = scaled.astype(BF16)
@@ -267,18 +296,29 @@
     low = jnp.concatenate(
         [rows[pl.ds(step, HEADS, stride=8), :] for step in range(8)], axis=1
     ).astype(BF16)
-    post_scaled = dot(low, head_t[...], TN)
+    spans = [slice(start, start + 512) for start in (0, 512)]
+    post_scaled = [dot(low[:, span], head_t[...], TN) for span in spans]
     copies[0].wait()
     copies[1].wait()
-    updated_grad = norm_backward(post_scaled * gain2[...], post_normed[...], post_inverse[...])
-    updated_v[...] = updated_grad
+    updated_grads = [
+        norm_backward(scaled * gain2[...], post_normed[span, :], post_inverse[span, :])
+        for scaled, span in zip(post_scaled, spans)
+    ]
+    for grad, span in zip(updated_grads, spans):
+        updated_v[span, :] = grad
     outs = fetch((updated_v,), (updated_out,), out_sems)
-    updated_low = updated_grad.astype(BF16)
-    hidden_grad = dot(updated_low, down_w[...], NT)
+    updated_lows = [grad.astype(BF16) for grad in updated_grads]
+    hidden_grads = [dot(grad, down_w[...], NT) for grad in updated_lows]
     for copy in copies[2:]:
         copy.wait()
-    gate_low = (hidden_grad * gate_slope[...]).astype(BF16)
-    up_low = (hidden_grad * up_slope[...]).astype(BF16)
+    gate_low = jnp.concatenate(
+        [(g * gate_slope[span, :]).astype(BF16) for g, span in zip(hidden_grads, spans)], axis=0
+    )
+    up_low = jnp.concatenate(
+        [(g * up_slope[span, :]).astype(BF16) for g, span in zip(hidden_grads, spans)], axis=0
+    )
+    updated_low = jnp.concatenate(updated_lows, axis=0)
+
     def give(first, rows_of, k):
         part = pl.ds(first, rows_of)
         outs.extend(fetch((weights_v.at[part],), (weights.at[part],), out_sems.at[pl.ds(k, 1)]))

time: 113 us -> 113 us (level)
  no operation moved by 1% of the time
where the time goes in v5:
time: 113 us; the launch traced here: 112 us
  starting transfers between devices  44.3 us (39%)
  waiting for transfers between devices  35 us (31%)
  Pallas kernels  30.3 us (27%)
    pallas_call x12, Pallas kernels, call(): pl.pallas_call(kernel, in_specs=[spec for spec, _ in ins], out_specs=[spe...  30.3 us
    all_to_all x4, starting transfers between devices, all_to_all(): return lax.all_to_all(value, axes, 0, 0, tiled=True)  22.2 us
    ppermute x12, starting transfers between devices, shifted(): lax.ppermute(value, axis, [(i, (i + shift) % size) for i in range(size)])  22.1 us
    all_to_all x4, waiting for transfers between devices, all_to_all(): return lax.all_to_all(value, axes, 0, 0, tiled=True)  20.2 us
    ppermute x12, waiting for transfers between devices, shifted(): lax.ppermute(value, axis, [(i, (i + shift) % size) for i in range(size)])  14.8 us
  transfers between devices with their start and end apart: 16, of which 12 were waited for; matrix products, arithmetic and copies ran while one was open for 1% of the time, Pallas kernels for 15%

profile of v5, /device:TPU:1, one launch (start us, length us, event | category | flops | bytes accessed | tf_op | source)
XLA Modules:
  0.0 112.0 jit_solution(17668614669835936042)
XLA Ops:
  0.6 0.0 copy-start.6
  0.7 0.0 copy-start.8
  0.7 0.0 copy-start.7
  0.7 0.0 copy-start.5
  0.7 0.0 copy-start
  0.7 0.0 copy-start.1
  0.7 0.0 copy-start.3
  0.7 0.0 copy-start.9
  0.7 0.0 copy-start.10
  0.7 0.0 copy-start.12
  0.8 0.1 stack.23.place
  0.8 6.5 %pair_bias.1.own = bf16[4,128,128]{2,1,0:T(8,128)(2,1)S(1)} custom-call(s32[5]{0:T(128)S(1)} %stack.23.place, bf16[256,2,32,128]{3,2,1,0:T(8,128)(2,1)} %pair.5, f32[1,128]{1,0:T(1,128)} %bitcast.43, bf16[128,512]{1,0:T(8,128)(2,1)} %gate_w.5, bf16[128,512]{1,0:T(8,128)(2,1)} %up_w.5, bf16[512,128]{1,0:T(8,128)(2,1)} %down_w.5, f32[1,128]{1,0:T(1,128)} %bitcast.47, ...), custom_call_target="tpu_custom_call" | custom-call | tf_op jit(solution)/shard_map/pair_bias/pallas_call | solution.py:415
  7.4 3.4 %collective-permute-start.2 = (bf16[4,128,128]{2,1,0:T(8,128)(2,1)S(1)}, bf16[4,128,128]{2,1,0:T(8,128)(2,1)S(1)}, u32[]{:S(2)}, u32[]{:S(2)}) collective-permute-start(bf16[4,128,128]{2,1,0:T(8,128)(2,1)S(1)} %pair_bias.1.own), channel_id=1, source_target_pairs={{0,48},{16,0},{32,16},{48,32},{1,49},{17,1},{33,17},{49,33},{2,50}... | collective-permute-start | bytes 393224 | tf_op jit(solution)/shard_map/ppermute | solution.py:396
  10.8 0.5 collective-permute-start.1
  11.3 0.6 collective-permute-start
  11.9 0.0 copy-done.6
  11.9 0.0 copy-done.8
  11.9 0.0 copy-done.7
  11.9 0.0 copy-done.5
  11.9 2.2 %products.1 = (f32[1024,256]{1,0:T(8,128)S(1)}, f32[1024,256]{1,0:T(8,128)S(1)}, bf16[256,768]{1,0:T(8,128)(2,1)}, bf16[256,768]{1,0:T(8,128)(2,1)}, bf16[1024,768]{1,0:T(8,128)(2,1)}) custom-call(bf16[256,768]{1,0:T(8,128)(2,1)S(1)} %bitcast.35, bf16[256,768]{1,0:T(8,128)(2,1)S(1)} %bitcast.36, bf16[2,32,768]{2,1,0:T(8,128)(2,1)S(1)} %bitcast.37, ...), custom_call_target="tpu_custom_call" | custom-call | tf_op jit(solution)/shard_map/products/pallas_call | solution.py:415
  14.1 0.2 collective-permute-done.2.third
  14.3 1.9 %collective-permute-done.1.second = bf16[4,128,128]{2,1,0:T(8,128)(2,1)S(1)} collective-permute-done((bf16[4,128,128]{2,1,0:T(8,128)(2,1)S(1)}, bf16[4,128,128]{2,1,0:T(8,128)(2,1)S(1)}, u32[]{:S(2)}, u32[]{:S(2)}) %collective-permute-start.1) | collective-permute-done | bytes 131104 | tf_op jit(solution)/shard_map/ppermute | solution.py:396
  16.2 4.1 %collective-permute-done.first = bf16[4,128,128]{2,1,0:T(8,128)(2,1)S(1)} collective-permute-done((bf16[4,128,128]{2,1,0:T(8,128)(2,1)S(1)}, bf16[4,128,128]{2,1,0:T(8,128)(2,1)S(1)}, u32[]{:S(2)}, u32[]{:S(2)}) %collective-permute-start) | collective-permute-done | bytes 131104 | tf_op jit(solution)/shard_map/ppermute | solution.py:396
  20.3 1.1 %softmax_stats.1 = (f32[1024,256]{1,0:T(8,128)S(1)}, f32[32,256]{1,0:T(8,128)S(1)}) custom-call(s32[5]{0:T(128)S(1)} %stack.23.place, f32[1024,256]{1,0:T(8,128)S(1)} %get-tuple-element.41.scores, f32[1024,256]{1,0:T(8,128)S(1)} %get-tuple-element.42.attend, bf16[4,128,128]{2,1,0:T(8,128)(2,1)S(1)} %pair_bias.1.own, ...), custom_call_target="tpu_custom_call" | custom-call | tf_op jit(solution)/shard_map/softmax_stats/pallas_call | solution.py:415
  21.4 7.0 %collective-permute-start.3 = (f32[32,256]{1,0:T(8,128)S(1)}, f32[32,256]{1,0:T(8,128)S(1)}, u32[]{:S(2)}, u32[]{:S(2)}) collective-permute-start(f32[32,256]{1,0:T(8,128)S(1)} %get-tuple-element.43.own), channel_id=1, source_target_pairs={{0,4},{4,0},{1,5},{5,1},{2,6},{6,2},{3,7},{7,3},{8,12},{12,8},{9,1... | collective-permute-start | bytes 98312 | tf_op jit(solution)/shard_map/ppermute | solution.py:396
  28.5 0.0 copy-done.3
  28.5 4.7 %pair_states.1 = (f32[1024,128]{1,0:T(8,128)}, f32[1024,128]{1,0:T(8,128)}, bf16[1024,512]{1,0:T(8,128)(2,1)}, bf16[1024,512]{1,0:T(8,128)(2,1)}, bf16[128,1024]...) custom-call(s32[5]{0:T(128)S(1)} %stack.23.place, ...), custom_call_target="tpu_custom_call" | custom-call | tf_op jit(solution)/shard_map/pair_states/pallas_call | solution.py:415
  33.2 0.0 collective-permute-done.3.received
  33.2 3.0 %collective-permute-start.6 = (f32[32,256]{1,0:T(8,128)S(1)}, f32[32,256]{1,0:T(8,128)S(1)}, u32[]{:S(2)}, u32[]{:S(2)}) collective-permute-start(f32[32,256]{1,0:T(8,128)S(1)} %merge_stats.1.own), channel_id=1, source_target_pairs={{0,2},{1,3},{2,0},{3,1},{4,6},{5,7},{6,4},{7,5},{8,10},{9,11},{10,... | collective-permute-start | bytes 98312 | tf_op jit(solution)/shard_map/ppermute | solution.py:396
  36.2 0.8 collective-permute-start.5
  37.0 0.7 collective-permute-start.4
  37.7 0.0 collective-permute-done.6.third
  37.7 1.6 %collective-permute-done.5.second = f32[32,256]{1,0:T(8,128)S(1)} collective-permute-done((f32[32,256]{1,0:T(8,128)S(1)}, f32[32,256]{1,0:T(8,128)S(1)}, u32[]{:S(2)}, u32[]{:S(2)}) %collective-permute-start.5) | collective-permute-done | bytes 32800 | tf_op jit(solution)/shard_map/ppermute | solution.py:396
  39.3 1.7 %collective-permute-done.4.first = f32[32,256]{1,0:T(8,128)S(1)} collective-permute-done((f32[32,256]{1,0:T(8,128)S(1)}, f32[32,256]{1,0:T(8,128)S(1)}, u32[]{:S(2)}, u32[]{:S(2)}) %collective-permute-start.4) | collective-permute-done | bytes 32800 | tf_op jit(solution)/shard_map/ppermute | solution.py:396
  40.9 1.5 %score_grads.1 = (bf16[16,128,128]{2,1,0:T(8,128)(2,1)}, bf16[1024,256]{1,0:T(8,128)(2,1)}, bf16[1024,256]{1,0:T(8,128)(2,1)}) custom-call(f32[32,256]{1,0:T(8,128)S(1)} %merge_stats.1.own, f32[32,256]{1,0:T(8,128)S(1)} %collective-permute-done.4.first, f32[32,256]{1,0:T(8,128)S(1)} %collective-permute-done.5.second, ...), custom_call_target="tpu_custom_call" | custom-call | tf_op jit(solution)/shard_map/score_grads/pallas_call | solution.py:415
  42.4 3.6 %all-to-all-start = ((bf16[16,128,128]{2,1,0:T(8,128)(2,1)}), bf16[16,128,128]{2,1,0:T(8,128)(2,1)S(1)}, u32[]{:S(2)}, u32[]{:S(2)}) async-start(bf16[16,128,128]{2,1,0:T(8,128)(2,1)} %get-tuple-element.57), calls=%async_computation | async-start | bytes 1048576 | tf_op jit(solution)/shard_map/all_to_all | solution.py:400
  46.0 3.4 %row_grads.1 = (bf16[2,32,768]{2,1,0:T(8,128)(2,1)S(1)}, bf16[2,32,768]{2,1,0:T(8,128)(2,1)S(1)}, bf16[2,32,768]{2,1,0:T(8,128)(2,1)S(1)}, bf16[2,32,768]{2,1,0:...) custom-call(s32[5]{0:T(128)S(1)} %stack.23.place, bf16[1024,256]{1,0:T(8,128)(2,1)} %get-tuple-element.46.score_low, ...), custom_call_target="tpu_custom_call" | custom-call | tf_op jit(solution)/shard_map/row_grads/pallas_call | solution.py:415
  49.4 0.2 collective-permute-start.7
  49.6 2.6 %collective-permute-start.8 = (bf16[2,32,768]{2,1,0:T(8,128)(2,1)S(1)}, bf16[2,32,768]{2,1,0:T(8,128)(2,1)S(1)}, u32[]{:S(2)}, u32[]{:S(2)}) collective-permute-start(bf16[2,32,768]{2,1,0:T(8,128)(2,1)S(1)} %get-tuple-element.53), channel_id=1, source_target_pairs={{0,3},{1,0},{2,1},{3,2},{4,7},{5,4},{6,5},{7,6},{8,11},{9,8},{10,9... | collective-permute-start | bytes 294920 | tf_op jit(solution)/shard_map/ppermute | solution.py:396
  52.2 0.0 collective-permute-start.9
  52.2 2.3 %collective-permute-done.7 = bf16[2,32,768]{2,1,0:T(8,128)(2,1)S(1)} collective-permute-done((bf16[2,32,768]{2,1,0:T(8,128)(2,1)S(1)}, bf16[2,32,768]{2,1,0:T(8,128)(2,1)S(1)}, u32[]{:S(2)}, u32[]{:S(2)}) %collective-permute-start.7) | collective-permute-done | bytes 98336 | tf_op jit(solution)/shard_map/ppermute | solution.py:396
  54.5 0.3 collective-permute-done.8
  54.8 2.7 %collective-permute-done.9 = bf16[2,32,768]{2,1,0:T(8,128)(2,1)S(1)} collective-permute-done((bf16[2,32,768]{2,1,0:T(8,128)(2,1)S(1)}, bf16[2,32,768]{2,1,0:T(8,128)(2,1)S(1)}, u32[]{:S(2)}, u32[]{:S(2)}) %collective-permute-start.9) | collective-permute-done | bytes 98336 | tf_op jit(solution)/shard_map/ppermute | solution.py:396
  57.5 0.6 all-to-all-done.received
  58.1 3.8 %pair_weights.1 = (bf16[1792,128]{1,0:T(8,128)(2,1)}, f32[1024,128]{1,0:T(8,128)}) custom-call(bf16[16,128,128]{2,1,0:T(8,128)(2,1)S(1)} %all-to-all-done.received, bf16[512,128]{1,0:T(8,128)(2,1)S(1)} %copy-done, f32[1,128]{1,0:T(1,128)S(1)} %bitcast.49, bf16[16,128]{1,0:T(8,128)(2,1)S(1)} %bitcast.41, f32[2,32,768]{2,1,0:T(8,128)S(1)} %convert_add_fusion.after, ...), custom_call_target="tpu_custom_call" | custom-call | tf_op jit(solution)/shard_map/pair_weights/pallas_call | solution.py:415
  61.9 8.6 %all-to-all-start.1 = ((bf16[32,56,128]{2,1,0:T(8,128)(2,1)}), bf16[32,56,128]{2,1,0:T(8,128)(2,1)S(1)}, u32[]{:S(2)}, u32[]{:S(2)}) async-start(bf16[32,56,128]{2,1,0:T(8,128)(2,1)} %bitcast.51), calls=%async_computation.1 | async-start | bytes 917504 | tf_op jit(solution)/shard_map/all_to_all | solution.py:400
  70.5 2.9 %collective-permute-start.10 = (bf16[32,768]{1,0:T(8,128)(2,1)S(1)}, bf16[32,768]{1,0:T(8,128)(2,1)S(1)}, u32[]{:S(2)}, u32[]{:S(2)}) collective-permute-start(bf16[32,768]{1,0:T(8,128)(2,1)S(1)} %fusion.3), channel_id=1, source_target_pairs={{0,4},{4,0},{1,5},{5,1},{2,6},{6,2},{3,7},{7,3},{8,12},{12,8},{9,1... | collective-permute-start | bytes 147464 | tf_op jit(solution)/shard_map/ppermute | solution.py:396
  73.4 0.5 collective-permute-start.11
  73.9 7.1 %all-to-all-done.1.parts = bf16[32,56,128]{2,1,0:T(8,128)(2,1)S(1)} async-done(((bf16[32,56,128]{2,1,0:T(8,128)(2,1)}), bf16[32,56,128]{2,1,0:T(8,128)(2,1)S(1)}, u32[]{:S(2)}, u32[]{:S(2)}) %all-to-all-start.1) | async-done | bytes 458784 | tf_op jit(solution)/shard_map/all_to_all | solution.py:400
  81.0 0.7 plane_sum.1
  81.7 4.3 %all-to-all-start.2 = ((bf16[8,56,128]{2,1,0:T(8,128)(2,1)}), bf16[8,56,128]{2,1,0:T(8,128)(2,1)S(1)}, u32[]{:S(2)}, u32[]{:S(2)}) async-start(bf16[8,56,128]{2,1,0:T(8,128)(2,1)} %plane_sum.1), calls=%async_computation.2 | async-start | bytes 229376 | tf_op jit(solution)/shard_map/all_to_all | solution.py:400
  86.0 0.0 collective-permute-done.10
  86.0 0.6 fusion.2
  86.6 7.2 %all-to-all-done.2.parts = bf16[8,56,128]{2,1,0:T(8,128)(2,1)S(1)} async-done(((bf16[8,56,128]{2,1,0:T(8,128)(2,1)}), bf16[8,56,128]{2,1,0:T(8,128)(2,1)S(1)}, u32[]{:S(2)}, u32[]{:S(2)}) %all-to-all-start.2) | async-done | bytes 114720 | tf_op jit(solution)/shard_map/all_to_all | solution.py:400
  93.8 0.8 column_sum.1.after
  94.6 5.8 %all-to-all-start.3 = ((bf16[32,56,128]{2,1,0:T(8,128)(2,1)}), bf16[32,56,128]{2,1,0:T(8,128)(2,1)S(1)}, u32[]{:S(2)}, u32[]{:S(2)}) async-start(bf16[32,56,128]{2,1,0:T(8,128)(2,1)} %column_sum.1.after), calls=%async_computation.3 | async-start | bytes 917504 | tf_op jit(solution)/shard_map/all_to_all | solution.py:400
  100.4 0.0 collective-permute-done.11
  100.4 0.0 copy-start.2
  100.4 0.0 copy-start.4
  100.4 0.0 copy-start.11
  100.5 0.6 slice_bitcast_fusion.1
  101.1 4.5 %pair_inputs.1 = bf16[16,2,32,128]{3,2,1,0:T(8,128)(2,1)} custom-call(s32[5]{0:T(128)S(1)} %stack.23.place, bf16[32,56,128]{2,1,0:T(8,128)(2,1)} %column_sum.1.after, bf16[256,2,32,128]{3,2,1,0:T(8,128)(2,1)} %pair.5, f32[1024,128]{1,0:T(8,128)} %get-tuple-element.65.updated_grad, bf16[1024,512]{1,0:T(8,128)(2,1)} %get-tuple-element.59.h2.gate_slope, ...), custom_call_target="tpu_custom_call" | custom-call | tf_op jit(solution)/shard_map/pair_inputs/pallas_call | solution.py:415
  105.6 5.4 %all-to-all-done.3 = bf16[32,56,128]{2,1,0:T(8,128)(2,1)S(1)} async-done(((bf16[32,56,128]{2,1,0:T(8,128)(2,1)}), bf16[32,56,128]{2,1,0:T(8,128)(2,1)S(1)}, u32[]{:S(2)}, u32[]{:S(2)}) %all-to-all-start.3) | async-done | bytes 458784 | tf_op jit(solution)/shard_map/all_to_all | solution.py:400
  111.0 1.0 unpack.1
  (12 shorter events, 0.1 us)
Async XLA Ops:
  0.6 11.3 %copy-start.6 = (bf16[1,256,768]{2,1,0:T(8,128)(2,1)S(1)}, bf16[1,256,768]{2,1,0:T(8,128)(2,1)}, u32[]{:S(2)}) copy-start(bf16[1,256,768]{2,1,0:T(8,128)(2,1)} %param.15) | copy-start | bytes 1179652
  0.7 11.3 %copy-start.8 = (bf16[1,2,32,768]{3,2,1,0:T(8,128)(2,1)S(1)}, bf16[1,2,32,768]{3,2,1,0:T(8,128)(2,1)}, u32[]{:S(2)}) copy-start(bf16[1,2,32,768]{3,2,1,0:T(8,128)(2,1)} %param.14) | copy-start | bytes 294916
  0.7 11.2 %copy-start.7 = (bf16[1,2,32,768]{3,2,1,0:T(8,128)(2,1)S(1)}, bf16[1,2,32,768]{3,2,1,0:T(8,128)(2,1)}, u32[]{:S(2)}) copy-start(bf16[1,2,32,768]{3,2,1,0:T(8,128)(2,1)} %param.13) | copy-start | bytes 294916
  0.7 11.2 %copy-start.5 = (bf16[1,256,768]{2,1,0:T(8,128)(2,1)S(1)}, bf16[1,256,768]{2,1,0:T(8,128)(2,1)}, u32[]{:S(2)}) copy-start(bf16[1,256,768]{2,1,0:T(8,128)(2,1)} %param.12) | copy-start | bytes 1179652
  0.7 27.8 %copy-start = (bf16[512,128]{1,0:T(8,128)(2,1)S(1)}, bf16[512,128]{1,0:T(8,128)(2,1)}, u32[]{:S(2)}) copy-start(bf16[512,128]{1,0:T(8,128)(2,1)} %down_w.5) | copy-start | bytes 393220
  0.7 27.8 %copy-start.1 = (bf16[128,512]{1,0:T(8,128)(2,1)S(1)}, bf16[128,512]{1,0:T(8,128)(2,1)}, u32[]{:S(2)}) copy-start(bf16[128,512]{1,0:T(8,128)(2,1)} %gate_w.5) | copy-start | bytes 393220
  0.7 27.7 %copy-start.3 = (bf16[128,512]{1,0:T(8,128)(2,1)S(1)}, bf16[128,512]{1,0:T(8,128)(2,1)}, u32[]{:S(2)}) copy-start(bf16[128,512]{1,0:T(8,128)(2,1)} %up_w.5) | copy-start | bytes 393220
  0.7 27.7 %copy-start.9 = (bf16[128,16]{0,1:T(8,128)(2,1)S(1)}, bf16[128,16]{0,1:T(8,128)(2,1)}, u32[]{:S(2)}) copy-start(bf16[128,16]{0,1:T(8,128)(2,1)} %param.21) | copy-start | bytes 12292
  0.7 27.7 %copy-start.10 = (f32[128]{0:T(128)S(1)}, f32[128]{0:T(128)}, u32[]{:S(2)}) copy-start(f32[128]{0:T(128)} %param.16) | copy-start | bytes 1540
  0.7 27.7 %copy-start.12 = (f32[128]{0:T(128)S(1)}, f32[128]{0:T(128)}, u32[]{:S(2)}) copy-start(f32[128]{0:T(128)} %param.20) | copy-start | bytes 1540
  7.4 6.9 %collective-permute-start.2 = (bf16[4,128,128]{2,1,0:T(8,128)(2,1)S(1)}, bf16[4,128,128]{2,1,0:T(8,128)(2,1)S(1)}, u32[]{:S(2)}, u32[]{:S(2)}) collective-permute-start(bf16[4,128,128]{2,1,0:T(8,128)(2,1)S(1)} %pair_bias.1.own), channel_id=1, source_target_pairs={{0,48},{16,0},{32,16},{48,32},{1,49},{17,1},{33,17},{49,33},{2,50}... | collective-permute-start | bytes 393224 | tf_op jit(solution)/shard_map/ppermute | solution.py:396
  10.8 5.4 %collective-permute-start.1 = (bf16[4,128,128]{2,1,0:T(8,128)(2,1)S(1)}, bf16[4,128,128]{2,1,0:T(8,128)(2,1)S(1)}, u32[]{:S(2)}, u32[]{:S(2)}) collective-permute-start(bf16[4,128,128]{2,1,0:T(8,128)(2,1)S(1)} %pair_bias.1.own), channel_id=1, source_target_pairs={{0,32},{16,48},{32,0},{48,16},{1,33},{17,49},{33,1},{49,17},{2,34}... | collective-permute-start | bytes 393224 | tf_op jit(solution)/shard_map/ppermute | solution.py:396
  11.3 9.0 %collective-permute-start = (bf16[4,128,128]{2,1,0:T(8,128)(2,1)S(1)}, bf16[4,128,128]{2,1,0:T(8,128)(2,1)S(1)}, u32[]{:S(2)}, u32[]{:S(2)}) collective-permute-start(bf16[4,128,128]{2,1,0:T(8,128)(2,1)S(1)} %pair_bias.1.own), channel_id=1, source_target_pairs={{0,16},{16,32},{32,48},{48,0},{1,17},{17,33},{33,49},{49,1},{2,18}... | collective-permute-start | bytes 393224 | tf_op jit(solution)/shard_map/ppermute | solution.py:396
  21.4 11.7 %collective-permute-start.3 = (f32[32,256]{1,0:T(8,128)S(1)}, f32[32,256]{1,0:T(8,128)S(1)}, u32[]{:S(2)}, u32[]{:S(2)}) collective-permute-start(f32[32,256]{1,0:T(8,128)S(1)} %get-tuple-element.43.own), channel_id=1, source_target_pairs={{0,4},{4,0},{1,5},{5,1},{2,6},{6,2},{3,7},{7,3},{8,12},{12,8},{9,1... | collective-permute-start | bytes 98312 | tf_op jit(solution)/shard_map/ppermute | solution.py:396
  33.2 4.5 %collective-permute-start.6 = (f32[32,256]{1,0:T(8,128)S(1)}, f32[32,256]{1,0:T(8,128)S(1)}, u32[]{:S(2)}, u32[]{:S(2)}) collective-permute-start(f32[32,256]{1,0:T(8,128)S(1)} %merge_stats.1.own), channel_id=1, source_target_pairs={{0,2},{1,3},{2,0},{3,1},{4,6},{5,7},{6,4},{7,5},{8,10},{9,11},{10,... | collective-permute-start | bytes 98312 | tf_op jit(solution)/shard_map/ppermute | solution.py:396
  36.2 3.1 %collective-permute-start.5 = (f32[32,256]{1,0:T(8,128)S(1)}, f32[32,256]{1,0:T(8,128)S(1)}, u32[]{:S(2)}, u32[]{:S(2)}) collective-permute-start(f32[32,256]{1,0:T(8,128)S(1)} %merge_stats.1.own), channel_id=1, source_target_pairs={{0,3},{1,0},{2,1},{3,2},{4,7},{5,4},{6,5},{7,6},{8,11},{9,8},{10,9... | collective-permute-start | bytes 98312 | tf_op jit(solution)/shard_map/ppermute | solution.py:396
  37.0 4.0 %collective-permute-start.4 = (f32[32,256]{1,0:T(8,128)S(1)}, f32[32,256]{1,0:T(8,128)S(1)}, u32[]{:S(2)}, u32[]{:S(2)}) collective-permute-start(f32[32,256]{1,0:T(8,128)S(1)} %merge_stats.1.own), channel_id=1, source_target_pairs={{0,1},{1,2},{2,3},{3,0},{4,5},{5,6},{6,7},{7,4},{8,9},{9,10},{10,1... | collective-permute-start | bytes 98312 | tf_op jit(solution)/shard_map/ppermute | solution.py:396
  42.4 15.7 %all-to-all-start = ((bf16[16,128,128]{2,1,0:T(8,128)(2,1)}), bf16[16,128,128]{2,1,0:T(8,128)(2,1)S(1)}, u32[]{:S(2)}, u32[]{:S(2)}) async-start(bf16[16,128,128]{2,1,0:T(8,128)(2,1)} %get-tuple-element.57), calls=%async_computation | async-start | bytes 1048576 | tf_op jit(solution)/shard_map/all_to_all | solution.py:400
  49.4 5.0 %collective-permute-start.7 = (bf16[2,32,768]{2,1,0:T(8,128)(2,1)S(1)}, bf16[2,32,768]{2,1,0:T(8,128)(2,1)S(1)}, u32[]{:S(2)}, u32[]{:S(2)}) collective-permute-start(bf16[2,32,768]{2,1,0:T(8,128)(2,1)S(1)} %get-tuple-element.52), channel_id=1, source_target_pairs={{0,1},{1,2},{2,3},{3,0},{4,5},{5,6},{6,7},{7,4},{8,9},{9,10},{10,1... | collective-permute-start | bytes 294920 | tf_op jit(solution)/shard_map/ppermute | solution.py:396
  49.6 5.2 %collective-permute-start.8 = (bf16[2,32,768]{2,1,0:T(8,128)(2,1)S(1)}, bf16[2,32,768]{2,1,0:T(8,128)(2,1)S(1)}, u32[]{:S(2)}, u32[]{:S(2)}) collective-permute-start(bf16[2,32,768]{2,1,0:T(8,128)(2,1)S(1)} %get-tuple-element.53), channel_id=1, source_target_pairs={{0,3},{1,0},{2,1},{3,2},{4,7},{5,4},{6,5},{7,6},{8,11},{9,8},{10,9... | collective-permute-start | bytes 294920 | tf_op jit(solution)/shard_map/ppermute | solution.py:396
  52.2 5.3 %collective-permute-start.9 = (bf16[2,32,768]{2,1,0:T(8,128)(2,1)S(1)}, bf16[2,32,768]{2,1,0:T(8,128)(2,1)S(1)}, u32[]{:S(2)}, u32[]{:S(2)}) collective-permute-start(bf16[2,32,768]{2,1,0:T(8,128)(2,1)S(1)} %get-tuple-element.54), channel_id=1, source_target_pairs={{0,2},{1,3},{2,0},{3,1},{4,6},{5,7},{6,4},{7,5},{8,10},{9,11},{10,... | collective-permute-start | bytes 294920 | tf_op jit(solution)/shard_map/ppermute | solution.py:396
  61.9 19.1 %all-to-all-start.1 = ((bf16[32,56,128]{2,1,0:T(8,128)(2,1)}), bf16[32,56,128]{2,1,0:T(8,128)(2,1)S(1)}, u32[]{:S(2)}, u32[]{:S(2)}) async-start(bf16[32,56,128]{2,1,0:T(8,128)(2,1)} %bitcast.51), calls=%async_computation.1 | async-start | bytes 917504 | tf_op jit(solution)/shard_map/all_to_all | solution.py:400
  70.5 15.5 %collective-permute-start.10 = (bf16[32,768]{1,0:T(8,128)(2,1)S(1)}, bf16[32,768]{1,0:T(8,128)(2,1)S(1)}, u32[]{:S(2)}, u32[]{:S(2)}) collective-permute-start(bf16[32,768]{1,0:T(8,128)(2,1)S(1)} %fusion.3), channel_id=1, source_target_pairs={{0,4},{4,0},{1,5},{5,1},{2,6},{6,2},{3,7},{7,3},{8,12},{12,8},{9,1... | collective-permute-start | bytes 147464 | tf_op jit(solution)/shard_map/ppermute | solution.py:396
  73.4 27.0 %collective-permute-start.11 = (f32[32,1536]{1,0:T(8,128)S(1)}, f32[32,1536]{1,0:T(8,128)S(1)}, u32[]{:S(2)}, u32[]{:S(2)}) collective-permute-start(f32[32,1536]{1,0:T(8,128)S(1)} %get-tuple-element.56), channel_id=1, source_target_pairs={{0,8},{8,0},{1,9},{9,1},{2,10},{10,2},{3,11},{11,3},{4,12},{12,4},... | collective-permute-start | bytes 589832 | tf_op jit(solution)/shard_map/ppermute | solution.py:396
  81.7 12.1 %all-to-all-start.2 = ((bf16[8,56,128]{2,1,0:T(8,128)(2,1)}), bf16[8,56,128]{2,1,0:T(8,128)(2,1)S(1)}, u32[]{:S(2)}, u32[]{:S(2)}) async-start(bf16[8,56,128]{2,1,0:T(8,128)(2,1)} %plane_sum.1), calls=%async_computation.2 | async-start | bytes 229376 | tf_op jit(solution)/shard_map/all_to_all | solution.py:400
  94.6 16.4 %all-to-all-start.3 = ((bf16[32,56,128]{2,1,0:T(8,128)(2,1)}), bf16[32,56,128]{2,1,0:T(8,128)(2,1)S(1)}, u32[]{:S(2)}, u32[]{:S(2)}) async-start(bf16[32,56,128]{2,1,0:T(8,128)(2,1)} %column_sum.1.after), calls=%async_computation.3 | async-start | bytes 917504 | tf_op jit(solution)/shard_map/all_to_all | solution.py:400
  100.4 10.6 %copy-start.2 = (bf16[128,512]{1,0:T(8,128)(2,1)S(1)}, bf16[128,512]{1,0:T(8,128)(2,1)}, u32[]{:S(2)}) copy-start(bf16[128,512]{1,0:T(8,128)(2,1)} %gate_w.5) | copy-start | bytes 393220
  100.4 10.6 %copy-start.4 = (bf16[128,512]{1,0:T(8,128)(2,1)S(1)}, bf16[128,512]{1,0:T(8,128)(2,1)}, u32[]{:S(2)}) copy-start(bf16[128,512]{1,0:T(8,128)(2,1)} %up_w.5) | copy-start | bytes 393220
  100.4 10.6 %copy-start.11 = (f32[128]{0:T(128)S(1)}, f32[128]{0:T(128)}, u32[]{:S(2)}) copy-start(f32[128]{0:T(128)} %param.16) | copy-start | bytes 1540

commit v6 on v5

--- a/solution.py
+++ b/solution.py
@@ -23,8 +23,8 @@
 F32 = jnp.float32
 BF16 = jnp.bfloat16
 NOISE = ("zl", "x")
-PLANE = ("x", "qi", "y")
-COLUMN = ("zh", "zl")
+PLANE = ("qi", "x", "y")
+COLUMN = ("zl", "zh")
 
 VMEM = pl.BlockSpec(memory_space=pltpu.VMEM)
 SMEM = pl.BlockSpec(memory_space=pltpu.SMEM)

time: 113 us -> 112 us (level)
  no operation moved by 1% of the time
where the time goes in v6:
time: 112 us; the launch traced here: 111 us
  starting transfers between devices  44.6 us (40%)
  waiting for transfers between devices  33.9 us (30%)
  Pallas kernels  30.3 us (27%)
    pallas_call x12, Pallas kernels, call(): pl.pallas_call(kernel, in_specs=[spec for spec, _ in ins], out_specs=[spe...  30.3 us
    all_to_all x4, starting transfers between devices, all_to_all(): return lax.all_to_all(value, axes, 0, 0, tiled=True)  22.4 us
    ppermute x12, starting transfers between devices, shifted(): lax.ppermute(value, axis, [(i, (i + shift) % size) for i in range(size)])  22.1 us
    all_to_all x4, waiting for transfers between devices, all_to_all(): return lax.all_to_all(value, axes, 0, 0, tiled=True)  19.2 us
    ppermute x12, waiting for transfers between devices, shifted(): lax.ppermute(value, axis, [(i, (i + shift) % size) for i in range(size)])  14.8 us
  transfers between devices with their start and end apart: 16, of which 12 were waited for; matrix products, arithmetic and copies ran while one was open for 1% of the time, Pallas kernels for 15%

profile of v6, /device:TPU:1, one launch (start us, length us, event | category | flops | bytes accessed | tf_op | source)
XLA Modules:
  0.0 111.2 jit_solution(16063813941916048310)
XLA Ops:
  0.6 0.0 copy-start.6
  0.7 0.0 copy-start.8
  0.7 0.0 copy-start.7
  0.7 0.0 copy-start.5
  0.7 0.0 copy-start
  0.7 0.0 copy-start.1
  0.7 0.0 copy-start.3
  0.7 0.0 copy-start.9
  0.7 0.0 copy-start.10
  0.7 0.0 copy-start.12
  0.8 0.1 stack.23.place
  0.8 6.5 %pair_bias.1.own = bf16[4,128,128]{2,1,0:T(8,128)(2,1)S(1)} custom-call(s32[5]{0:T(128)S(1)} %stack.23.place, bf16[256,2,32,128]{3,2,1,0:T(8,128)(2,1)} %pair.5, f32[1,128]{1,0:T(1,128)} %bitcast.43, bf16[128,512]{1,0:T(8,128)(2,1)} %gate_w.5, bf16[128,512]{1,0:T(8,128)(2,1)} %up_w.5, bf16[512,128]{1,0:T(8,128)(2,1)} %down_w.5, f32[1,128]{1,0:T(1,128)} %bitcast.47, ...), custom_call_target="tpu_custom_call" | custom-call | tf_op jit(solution)/shard_map/pair_bias/pallas_call | solution.py:415
  7.4 3.4 %collective-permute-start.2 = (bf16[4,128,128]{2,1,0:T(8,128)(2,1)S(1)}, bf16[4,128,128]{2,1,0:T(8,128)(2,1)S(1)}, u32[]{:S(2)}, u32[]{:S(2)}) collective-permute-start(bf16[4,128,128]{2,1,0:T(8,128)(2,1)S(1)} %pair_bias.1.own), channel_id=1, source_target_pairs={{0,48},{16,0},{32,16},{48,32},{1,49},{17,1},{33,17},{49,33},{2,50}... | collective-permute-start | bytes 393224 | tf_op jit(solution)/shard_map/ppermute | solution.py:396
  10.8 0.5 collective-permute-start.1
  11.3 0.6 collective-permute-start
  11.9 0.0 copy-done.6
  11.9 0.0 copy-done.8
  11.9 0.0 copy-done.7
  11.9 0.0 copy-done.5
  11.9 2.2 %products.1 = (f32[1024,256]{1,0:T(8,128)S(1)}, f32[1024,256]{1,0:T(8,128)S(1)}, bf16[256,768]{1,0:T(8,128)(2,1)}, bf16[256,768]{1,0:T(8,128)(2,1)}, bf16[1024,768]{1,0:T(8,128)(2,1)}) custom-call(bf16[256,768]{1,0:T(8,128)(2,1)S(1)} %bitcast.35, bf16[256,768]{1,0:T(8,128)(2,1)S(1)} %bitcast.36, bf16[2,32,768]{2,1,0:T(8,128)(2,1)S(1)} %bitcast.37, ...), custom_call_target="tpu_custom_call" | custom-call | tf_op jit(solution)/shard_map/products/pallas_call | solution.py:415
  14.1 0.2 collective-permute-done.2.third
  14.3 1.9 %collective-permute-done.1.second = bf16[4,128,128]{2,1,0:T(8,128)(2,1)S(1)} collective-permute-done((bf16[4,128,128]{2,1,0:T(8,128)(2,1)S(1)}, bf16[4,128,128]{2,1,0:T(8,128)(2,1)S(1)}, u32[]{:S(2)}, u32[]{:S(2)}) %collective-permute-start.1) | collective-permute-done | bytes 131104 | tf_op jit(solution)/shard_map/ppermute | solution.py:396
  16.2 4.1 %collective-permute-done.first = bf16[4,128,128]{2,1,0:T(8,128)(2,1)S(1)} collective-permute-done((bf16[4,128,128]{2,1,0:T(8,128)(2,1)S(1)}, bf16[4,128,128]{2,1,0:T(8,128)(2,1)S(1)}, u32[]{:S(2)}, u32[]{:S(2)}) %collective-permute-start) | collective-permute-done | bytes 131104 | tf_op jit(solution)/shard_map/ppermute | solution.py:396
  20.3 1.1 %softmax_stats.1 = (f32[1024,256]{1,0:T(8,128)S(1)}, f32[32,256]{1,0:T(8,128)S(1)}) custom-call(s32[5]{0:T(128)S(1)} %stack.23.place, f32[1024,256]{1,0:T(8,128)S(1)} %get-tuple-element.41.scores, f32[1024,256]{1,0:T(8,128)S(1)} %get-tuple-element.42.attend, bf16[4,128,128]{2,1,0:T(8,128)(2,1)S(1)} %pair_bias.1.own, ...), custom_call_target="tpu_custom_call" | custom-call | tf_op jit(solution)/shard_map/softmax_stats/pallas_call | solution.py:415
  21.4 7.0 %collective-permute-start.3 = (f32[32,256]{1,0:T(8,128)S(1)}, f32[32,256]{1,0:T(8,128)S(1)}, u32[]{:S(2)}, u32[]{:S(2)}) collective-permute-start(f32[32,256]{1,0:T(8,128)S(1)} %get-tuple-element.43.own), channel_id=1, source_target_pairs={{0,4},{4,0},{1,5},{5,1},{2,6},{6,2},{3,7},{7,3},{8,12},{12,8},{9,1... | collective-permute-start | bytes 98312 | tf_op jit(solution)/shard_map/ppermute | solution.py:396
  28.5 0.0 copy-done.9
  28.5 4.7 %pair_states.1 = (f32[1024,128]{1,0:T(8,128)}, f32[1024,128]{1,0:T(8,128)}, bf16[1024,512]{1,0:T(8,128)(2,1)}, bf16[1024,512]{1,0:T(8,128)(2,1)}, bf16[128,1024]...) custom-call(s32[5]{0:T(128)S(1)} %stack.23.place, ...), custom_call_target="tpu_custom_call" | custom-call | tf_op jit(solution)/shard_map/pair_states/pallas_call | solution.py:415
  33.2 0.0 collective-permute-done.3.received
  33.2 3.0 %collective-permute-start.6 = (f32[32,256]{1,0:T(8,128)S(1)}, f32[32,256]{1,0:T(8,128)S(1)}, u32[]{:S(2)}, u32[]{:S(2)}) collective-permute-start(f32[32,256]{1,0:T(8,128)S(1)} %merge_stats.1.own), channel_id=1, source_target_pairs={{0,2},{1,3},{2,0},{3,1},{4,6},{5,7},{6,4},{7,5},{8,10},{9,11},{10,... | collective-permute-start | bytes 98312 | tf_op jit(solution)/shard_map/ppermute | solution.py:396
  36.2 0.8 collective-permute-start.5
  37.0 0.7 collective-permute-start.4
  37.7 0.0 collective-permute-done.6.third
  37.7 1.6 %collective-permute-done.5.second = f32[32,256]{1,0:T(8,128)S(1)} collective-permute-done((f32[32,256]{1,0:T(8,128)S(1)}, f32[32,256]{1,0:T(8,128)S(1)}, u32[]{:S(2)}, u32[]{:S(2)}) %collective-permute-start.5) | collective-permute-done | bytes 32800 | tf_op jit(solution)/shard_map/ppermute | solution.py:396
  39.3 1.7 %collective-permute-done.4.first = f32[32,256]{1,0:T(8,128)S(1)} collective-permute-done((f32[32,256]{1,0:T(8,128)S(1)}, f32[32,256]{1,0:T(8,128)S(1)}, u32[]{:S(2)}, u32[]{:S(2)}) %collective-permute-start.4) | collective-permute-done | bytes 32800 | tf_op jit(solution)/shard_map/ppermute | solution.py:396
  40.9 1.5 %score_grads.1 = (bf16[16,128,128]{2,1,0:T(8,128)(2,1)}, bf16[1024,256]{1,0:T(8,128)(2,1)}, bf16[1024,256]{1,0:T(8,128)(2,1)}) custom-call(f32[32,256]{1,0:T(8,128)S(1)} %merge_stats.1.own, f32[32,256]{1,0:T(8,128)S(1)} %collective-permute-done.4.first, f32[32,256]{1,0:T(8,128)S(1)} %collective-permute-done.5.second, ...), custom_call_target="tpu_custom_call" | custom-call | tf_op jit(solution)/shard_map/score_grads/pallas_call | solution.py:415
  42.4 3.6 %all-to-all-start = ((bf16[16,128,128]{2,1,0:T(8,128)(2,1)}), bf16[16,128,128]{2,1,0:T(8,128)(2,1)S(1)}, u32[]{:S(2)}, u32[]{:S(2)}) async-start(bf16[16,128,128]{2,1,0:T(8,128)(2,1)} %get-tuple-element.57), calls=%async_computation | async-start | bytes 1048576 | tf_op jit(solution)/shard_map/all_to_all | solution.py:400
  46.0 3.4 %row_grads.1 = (bf16[2,32,768]{2,1,0:T(8,128)(2,1)S(1)}, bf16[2,32,768]{2,1,0:T(8,128)(2,1)S(1)}, bf16[2,32,768]{2,1,0:T(8,128)(2,1)S(1)}, bf16[2,32,768]{2,1,0:...) custom-call(s32[5]{0:T(128)S(1)} %stack.23.place, bf16[1024,256]{1,0:T(8,128)(2,1)} %get-tuple-element.46.score_low, ...), custom_call_target="tpu_custom_call" | custom-call | tf_op jit(solution)/shard_map/row_grads/pallas_call | solution.py:415
  49.4 0.2 collective-permute-start.7
  49.6 2.6 %collective-permute-start.8 = (bf16[2,32,768]{2,1,0:T(8,128)(2,1)S(1)}, bf16[2,32,768]{2,1,0:T(8,128)(2,1)S(1)}, u32[]{:S(2)}, u32[]{:S(2)}) collective-permute-start(bf16[2,32,768]{2,1,0:T(8,128)(2,1)S(1)} %get-tuple-element.53), channel_id=1, source_target_pairs={{0,3},{1,0},{2,1},{3,2},{4,7},{5,4},{6,5},{7,6},{8,11},{9,8},{10,9... | collective-permute-start | bytes 294920 | tf_op jit(solution)/shard_map/ppermute | solution.py:396
  52.2 0.0 collective-permute-start.9
  52.2 2.3 %collective-permute-done.7 = bf16[2,32,768]{2,1,0:T(8,128)(2,1)S(1)} collective-permute-done((bf16[2,32,768]{2,1,0:T(8,128)(2,1)S(1)}, bf16[2,32,768]{2,1,0:T(8,128)(2,1)S(1)}, u32[]{:S(2)}, u32[]{:S(2)}) %collective-permute-start.7) | collective-permute-done | bytes 98336 | tf_op jit(solution)/shard_map/ppermute | solution.py:396
  54.5 0.3 collective-permute-done.8
  54.8 2.7 %collective-permute-done.9 = bf16[2,32,768]{2,1,0:T(8,128)(2,1)S(1)} collective-permute-done((bf16[2,32,768]{2,1,0:T(8,128)(2,1)S(1)}, bf16[2,32,768]{2,1,0:T(8,128)(2,1)S(1)}, u32[]{:S(2)}, u32[]{:S(2)}) %collective-permute-start.9) | collective-permute-done | bytes 98336 | tf_op jit(solution)/shard_map/ppermute | solution.py:396
  57.5 0.6 all-to-all-done.received
  58.1 3.8 %pair_weights.1 = (bf16[1792,128]{1,0:T(8,128)(2,1)}, f32[1024,128]{1,0:T(8,128)}) custom-call(bf16[16,128,128]{2,1,0:T(8,128)(2,1)S(1)} %all-to-all-done.received, bf16[512,128]{1,0:T(8,128)(2,1)S(1)} %copy-done, f32[1,128]{1,0:T(1,128)S(1)} %bitcast.49, bf16[16,128]{1,0:T(8,128)(2,1)S(1)} %bitcast.41, f32[2,32,768]{2,1,0:T(8,128)S(1)} %convert_add_fusion.after, ...), custom_call_target="tpu_custom_call" | custom-call | tf_op jit(solution)/shard_map/pair_weights/pallas_call | solution.py:415
  61.9 8.6 %all-to-all-start.1 = ((bf16[32,56,128]{2,1,0:T(8,128)(2,1)}), bf16[32,56,128]{2,1,0:T(8,128)(2,1)S(1)}, u32[]{:S(2)}, u32[]{:S(2)}) async-start(bf16[32,56,128]{2,1,0:T(8,128)(2,1)} %bitcast.51), calls=%async_computation.1 | async-start | bytes 917504 | tf_op jit(solution)/shard_map/all_to_all | solution.py:400
  70.5 2.9 %collective-permute-start.10 = (bf16[32,768]{1,0:T(8,128)(2,1)S(1)}, bf16[32,768]{1,0:T(8,128)(2,1)S(1)}, u32[]{:S(2)}, u32[]{:S(2)}) collective-permute-start(bf16[32,768]{1,0:T(8,128)(2,1)S(1)} %fusion.3), channel_id=1, source_target_pairs={{0,4},{4,0},{1,5},{5,1},{2,6},{6,2},{3,7},{7,3},{8,12},{12,8},{9,1... | collective-permute-start | bytes 147464 | tf_op jit(solution)/shard_map/ppermute | solution.py:396
  73.4 0.5 collective-permute-start.11
  73.9 7.1 %all-to-all-done.1.parts = bf16[32,56,128]{2,1,0:T(8,128)(2,1)S(1)} async-done(((bf16[32,56,128]{2,1,0:T(8,128)(2,1)}), bf16[32,56,128]{2,1,0:T(8,128)(2,1)S(1)}, u32[]{:S(2)}, u32[]{:S(2)}) %all-to-all-start.1) | async-done | bytes 458784 | tf_op jit(solution)/shard_map/all_to_all | solution.py:400
  81.0 0.7 plane_sum.1
  81.7 4.3 %all-to-all-start.2 = ((bf16[8,56,128]{2,1,0:T(8,128)(2,1)}), bf16[8,56,128]{2,1,0:T(8,128)(2,1)S(1)}, u32[]{:S(2)}, u32[]{:S(2)}) async-start(bf16[8,56,128]{2,1,0:T(8,128)(2,1)} %plane_sum.1), calls=%async_computation.2 | async-start | bytes 229376 | tf_op jit(solution)/shard_map/all_to_all | solution.py:400
  86.0 0.0 collective-permute-done.10
  86.0 0.6 fusion.2
  86.6 6.1 %all-to-all-done.2.parts = bf16[8,56,128]{2,1,0:T(8,128)(2,1)S(1)} async-done(((bf16[8,56,128]{2,1,0:T(8,128)(2,1)}), bf16[8,56,128]{2,1,0:T(8,128)(2,1)S(1)}, u32[]{:S(2)}, u32[]{:S(2)}) %all-to-all-start.2) | async-done | bytes 114720 | tf_op jit(solution)/shard_map/all_to_all | solution.py:400
  92.8 0.8 column_sum.1.after
  93.6 6.0 %all-to-all-start.3 = ((bf16[32,56,128]{2,1,0:T(8,128)(2,1)}), bf16[32,56,128]{2,1,0:T(8,128)(2,1)S(1)}, u32[]{:S(2)}, u32[]{:S(2)}) async-start(bf16[32,56,128]{2,1,0:T(8,128)(2,1)} %column_sum.1.after), calls=%async_computation.3 | async-start | bytes 917504 | tf_op jit(solution)/shard_map/all_to_all | solution.py:400
  99.6 0.0 collective-permute-done.11
  99.7 0.0 copy-start.2
  99.7 0.0 copy-start.4
  99.7 0.0 copy-start.11
  99.7 0.6 slice_bitcast_fusion.1
  100.4 4.5 %pair_inputs.1 = bf16[16,2,32,128]{3,2,1,0:T(8,128)(2,1)} custom-call(s32[5]{0:T(128)S(1)} %stack.23.place, bf16[32,56,128]{2,1,0:T(8,128)(2,1)} %column_sum.1.after, bf16[256,2,32,128]{3,2,1,0:T(8,128)(2,1)} %pair.5, f32[1024,128]{1,0:T(8,128)} %get-tuple-element.65.updated_grad, bf16[1024,512]{1,0:T(8,128)(2,1)} %get-tuple-element.59.h2.gate_slope, ...), custom_call_target="tpu_custom_call" | custom-call | tf_op jit(solution)/shard_map/pair_inputs/pallas_call | solution.py:415
  104.9 5.4 %all-to-all-done.3 = bf16[32,56,128]{2,1,0:T(8,128)(2,1)S(1)} async-done(((bf16[32,56,128]{2,1,0:T(8,128)(2,1)}), bf16[32,56,128]{2,1,0:T(8,128)(2,1)S(1)}, u32[]{:S(2)}, u32[]{:S(2)}) %all-to-all-start.3) | async-done | bytes 458784 | tf_op jit(solution)/shard_map/all_to_all | solution.py:400
  110.3 1.0 unpack.1
  (12 shorter events, 0.1 us)
Async XLA Ops:
  0.6 11.3 %copy-start.6 = (bf16[1,256,768]{2,1,0:T(8,128)(2,1)S(1)}, bf16[1,256,768]{2,1,0:T(8,128)(2,1)}, u32[]{:S(2)}) copy-start(bf16[1,256,768]{2,1,0:T(8,128)(2,1)} %param.15) | copy-start | bytes 1179652
  0.7 11.3 %copy-start.8 = (bf16[1,2,32,768]{3,2,1,0:T(8,128)(2,1)S(1)}, bf16[1,2,32,768]{3,2,1,0:T(8,128)(2,1)}, u32[]{:S(2)}) copy-start(bf16[1,2,32,768]{3,2,1,0:T(8,128)(2,1)} %param.14) | copy-start | bytes 294916
  0.7 11.2 %copy-start.7 = (bf16[1,2,32,768]{3,2,1,0:T(8,128)(2,1)S(1)}, bf16[1,2,32,768]{3,2,1,0:T(8,128)(2,1)}, u32[]{:S(2)}) copy-start(bf16[1,2,32,768]{3,2,1,0:T(8,128)(2,1)} %param.13) | copy-start | bytes 294916
  0.7 11.2 %copy-start.5 = (bf16[1,256,768]{2,1,0:T(8,128)(2,1)S(1)}, bf16[1,256,768]{2,1,0:T(8,128)(2,1)}, u32[]{:S(2)}) copy-start(bf16[1,256,768]{2,1,0:T(8,128)(2,1)} %param.12) | copy-start | bytes 1179652
  0.7 27.8 %copy-start = (bf16[512,128]{1,0:T(8,128)(2,1)S(1)}, bf16[512,128]{1,0:T(8,128)(2,1)}, u32[]{:S(2)}) copy-start(bf16[512,128]{1,0:T(8,128)(2,1)} %down_w.5) | copy-start | bytes 393220
  0.7 27.8 %copy-start.1 = (bf16[128,512]{1,0:T(8,128)(2,1)S(1)}, bf16[128,512]{1,0:T(8,128)(2,1)}, u32[]{:S(2)}) copy-start(bf16[128,512]{1,0:T(8,128)(2,1)} %gate_w.5) | copy-start | bytes 393220
  0.7 27.7 %copy-start.3 = (bf16[128,512]{1,0:T(8,128)(2,1)S(1)}, bf16[128,512]{1,0:T(8,128)(2,1)}, u32[]{:S(2)}) copy-start(bf16[128,512]{1,0:T(8,128)(2,1)} %up_w.5) | copy-start | bytes 393220
  0.7 27.7 %copy-start.9 = (bf16[128,16]{0,1:T(8,128)(2,1)S(1)}, bf16[128,16]{0,1:T(8,128)(2,1)}, u32[]{:S(2)}) copy-start(bf16[128,16]{0,1:T(8,128)(2,1)} %param.21) | copy-start | bytes 12292
  0.7 27.7 %copy-start.10 = (f32[128]{0:T(128)S(1)}, f32[128]{0:T(128)}, u32[]{:S(2)}) copy-start(f32[128]{0:T(128)} %param.16) | copy-start | bytes 1540
  0.7 27.7 %copy-start.12 = (f32[128]{0:T(128)S(1)}, f32[128]{0:T(128)}, u32[]{:S(2)}) copy-start(f32[128]{0:T(128)} %param.20) | copy-start | bytes 1540
  7.4 6.9 %collective-permute-start.2 = (bf16[4,128,128]{2,1,0:T(8,128)(2,1)S(1)}, bf16[4,128,128]{2,1,0:T(8,128)(2,1)S(1)}, u32[]{:S(2)}, u32[]{:S(2)}) collective-permute-start(bf16[4,128,128]{2,1,0:T(8,128)(2,1)S(1)} %pair_bias.1.own), channel_id=1, source_target_pairs={{0,48},{16,0},{32,16},{48,32},{1,49},{17,1},{33,17},{49,33},{2,50}... | collective-permute-start | bytes 393224 | tf_op jit(solution)/shard_map/ppermute | solution.py:396
  10.8 5.4 %collective-permute-start.1 = (bf16[4,128,128]{2,1,0:T(8,128)(2,1)S(1)}, bf16[4,128,128]{2,1,0:T(8,128)(2,1)S(1)}, u32[]{:S(2)}, u32[]{:S(2)}) collective-permute-start(bf16[4,128,128]{2,1,0:T(8,128)(2,1)S(1)} %pair_bias.1.own), channel_id=1, source_target_pairs={{0,32},{16,48},{32,0},{48,16},{1,33},{17,49},{33,1},{49,17},{2,34}... | collective-permute-start | bytes 393224 | tf_op jit(solution)/shard_map/ppermute | solution.py:396
  11.3 9.0 %collective-permute-start = (bf16[4,128,128]{2,1,0:T(8,128)(2,1)S(1)}, bf16[4,128,128]{2,1,0:T(8,128)(2,1)S(1)}, u32[]{:S(2)}, u32[]{:S(2)}) collective-permute-start(bf16[4,128,128]{2,1,0:T(8,128)(2,1)S(1)} %pair_bias.1.own), channel_id=1, source_target_pairs={{0,16},{16,32},{32,48},{48,0},{1,17},{17,33},{33,49},{49,1},{2,18}... | collective-permute-start | bytes 393224 | tf_op jit(solution)/shard_map/ppermute | solution.py:396
  21.4 11.7 %collective-permute-start.3 = (f32[32,256]{1,0:T(8,128)S(1)}, f32[32,256]{1,0:T(8,128)S(1)}, u32[]{:S(2)}, u32[]{:S(2)}) collective-permute-start(f32[32,256]{1,0:T(8,128)S(1)} %get-tuple-element.43.own), channel_id=1, source_target_pairs={{0,4},{4,0},{1,5},{5,1},{2,6},{6,2},{3,7},{7,3},{8,12},{12,8},{9,1... | collective-permute-start | bytes 98312 | tf_op jit(solution)/shard_map/ppermute | solution.py:396
  33.2 4.5 %collective-permute-start.6 = (f32[32,256]{1,0:T(8,128)S(1)}, f32[32,256]{1,0:T(8,128)S(1)}, u32[]{:S(2)}, u32[]{:S(2)}) collective-permute-start(f32[32,256]{1,0:T(8,128)S(1)} %merge_stats.1.own), channel_id=1, source_target_pairs={{0,2},{1,3},{2,0},{3,1},{4,6},{5,7},{6,4},{7,5},{8,10},{9,11},{10,... | collective-permute-start | bytes 98312 | tf_op jit(solution)/shard_map/ppermute | solution.py:396
  36.2 3.1 %collective-permute-start.5 = (f32[32,256]{1,0:T(8,128)S(1)}, f32[32,256]{1,0:T(8,128)S(1)}, u32[]{:S(2)}, u32[]{:S(2)}) collective-permute-start(f32[32,256]{1,0:T(8,128)S(1)} %merge_stats.1.own), channel_id=1, source_target_pairs={{0,3},{1,0},{2,1},{3,2},{4,7},{5,4},{6,5},{7,6},{8,11},{9,8},{10,9... | collective-permute-start | bytes 98312 | tf_op jit(solution)/shard_map/ppermute | solution.py:396
  37.0 4.0 %collective-permute-start.4 = (f32[32,256]{1,0:T(8,128)S(1)}, f32[32,256]{1,0:T(8,128)S(1)}, u32[]{:S(2)}, u32[]{:S(2)}) collective-permute-start(f32[32,256]{1,0:T(8,128)S(1)} %merge_stats.1.own), channel_id=1, source_target_pairs={{0,1},{1,2},{2,3},{3,0},{4,5},{5,6},{6,7},{7,4},{8,9},{9,10},{10,1... | collective-permute-start | bytes 98312 | tf_op jit(solution)/shard_map/ppermute | solution.py:396
  42.4 15.7 %all-to-all-start = ((bf16[16,128,128]{2,1,0:T(8,128)(2,1)}), bf16[16,128,128]{2,1,0:T(8,128)(2,1)S(1)}, u32[]{:S(2)}, u32[]{:S(2)}) async-start(bf16[16,128,128]{2,1,0:T(8,128)(2,1)} %get-tuple-element.57), calls=%async_computation | async-start | bytes 1048576 | tf_op jit(solution)/shard_map/all_to_all | solution.py:400
  49.4 5.0 %collective-permute-start.7 = (bf16[2,32,768]{2,1,0:T(8,128)(2,1)S(1)}, bf16[2,32,768]{2,1,0:T(8,128)(2,1)S(1)}, u32[]{:S(2)}, u32[]{:S(2)}) collective-permute-start(bf16[2,32,768]{2,1,0:T(8,128)(2,1)S(1)} %get-tuple-element.52), channel_id=1, source_target_pairs={{0,1},{1,2},{2,3},{3,0},{4,5},{5,6},{6,7},{7,4},{8,9},{9,10},{10,1... | collective-permute-start | bytes 294920 | tf_op jit(solution)/shard_map/ppermute | solution.py:396
  49.6 5.2 %collective-permute-start.8 = (bf16[2,32,768]{2,1,0:T(8,128)(2,1)S(1)}, bf16[2,32,768]{2,1,0:T(8,128)(2,1)S(1)}, u32[]{:S(2)}, u32[]{:S(2)}) collective-permute-start(bf16[2,32,768]{2,1,0:T(8,128)(2,1)S(1)} %get-tuple-element.53), channel_id=1, source_target_pairs={{0,3},{1,0},{2,1},{3,2},{4,7},{5,4},{6,5},{7,6},{8,11},{9,8},{10,9... | collective-permute-start | bytes 294920 | tf_op jit(solution)/shard_map/ppermute | solution.py:396
  52.2 5.3 %collective-permute-start.9 = (bf16[2,32,768]{2,1,0:T(8,128)(2,1)S(1)}, bf16[2,32,768]{2,1,0:T(8,128)(2,1)S(1)}, u32[]{:S(2)}, u32[]{:S(2)}) collective-permute-start(bf16[2,32,768]{2,1,0:T(8,128)(2,1)S(1)} %get-tuple-element.54), channel_id=1, source_target_pairs={{0,2},{1,3},{2,0},{3,1},{4,6},{5,7},{6,4},{7,5},{8,10},{9,11},{10,... | collective-permute-start | bytes 294920 | tf_op jit(solution)/shard_map/ppermute | solution.py:396
  61.9 19.1 %all-to-all-start.1 = ((bf16[32,56,128]{2,1,0:T(8,128)(2,1)}), bf16[32,56,128]{2,1,0:T(8,128)(2,1)S(1)}, u32[]{:S(2)}, u32[]{:S(2)}) async-start(bf16[32,56,128]{2,1,0:T(8,128)(2,1)} %bitcast.51), calls=%async_computation.1 | async-start | bytes 917504 | tf_op jit(solution)/shard_map/all_to_all | solution.py:400
  70.5 15.5 %collective-permute-start.10 = (bf16[32,768]{1,0:T(8,128)(2,1)S(1)}, bf16[32,768]{1,0:T(8,128)(2,1)S(1)}, u32[]{:S(2)}, u32[]{:S(2)}) collective-permute-start(bf16[32,768]{1,0:T(8,128)(2,1)S(1)} %fusion.3), channel_id=1, source_target_pairs={{0,4},{4,0},{1,5},{5,1},{2,6},{6,2},{3,7},{7,3},{8,12},{12,8},{9,1... | collective-permute-start | bytes 147464 | tf_op jit(solution)/shard_map/ppermute | solution.py:396
  73.4 26.2 %collective-permute-start.11 = (f32[32,1536]{1,0:T(8,128)S(1)}, f32[32,1536]{1,0:T(8,128)S(1)}, u32[]{:S(2)}, u32[]{:S(2)}) collective-permute-start(f32[32,1536]{1,0:T(8,128)S(1)} %get-tuple-element.56), channel_id=1, source_target_pairs={{0,8},{8,0},{1,9},{9,1},{2,10},{10,2},{3,11},{11,3},{4,12},{12,4},... | collective-permute-start | bytes 589832 | tf_op jit(solution)/shard_map/ppermute | solution.py:396
  81.7 11.0 %all-to-all-start.2 = ((bf16[8,56,128]{2,1,0:T(8,128)(2,1)}), bf16[8,56,128]{2,1,0:T(8,128)(2,1)S(1)}, u32[]{:S(2)}, u32[]{:S(2)}) async-start(bf16[8,56,128]{2,1,0:T(8,128)(2,1)} %plane_sum.1), calls=%async_computation.2 | async-start | bytes 229376 | tf_op jit(solution)/shard_map/all_to_all | solution.py:400
  93.6 16.6 %all-to-all-start.3 = ((bf16[32,56,128]{2,1,0:T(8,128)(2,1)}), bf16[32,56,128]{2,1,0:T(8,128)(2,1)S(1)}, u32[]{:S(2)}, u32[]{:S(2)}) async-start(bf16[32,56,128]{2,1,0:T(8,128)(2,1)} %column_sum.1.after), calls=%async_computation.3 | async-start | bytes 917504 | tf_op jit(solution)/shard_map/all_to_all | solution.py:400
  99.7 10.6 %copy-start.2 = (bf16[128,512]{1,0:T(8,128)(2,1)S(1)}, bf16[128,512]{1,0:T(8,128)(2,1)}, u32[]{:S(2)}) copy-start(bf16[128,512]{1,0:T(8,128)(2,1)} %gate_w.5) | copy-start | bytes 393220
  99.7 10.6 %copy-start.4 = (bf16[128,512]{1,0:T(8,128)(2,1)S(1)}, bf16[128,512]{1,0:T(8,128)(2,1)}, u32[]{:S(2)}) copy-start(bf16[128,512]{1,0:T(8,128)(2,1)} %up_w.5) | copy-start | bytes 393220
  99.7 10.6 %copy-start.11 = (f32[128]{0:T(128)S(1)}, f32[128]{0:T(128)}, u32[]{:S(2)}) copy-start(f32[128]{0:T(128)} %param.16) | copy-start | bytes 1540

commit v7 on v6

--- a/solution.py
+++ b/solution.py
@@ -526,7 +526,7 @@
     weights, updated_grad = call(
         weight_kernel,
         [
-            *vmem(received, *params[3:], half),
+            *vmem(received, *params[3:], query_parts[1]),
             *[in_hbm(v) for v in states[:7]],
         ],
         [

time: 112 us -> 111 us (level)
  starting transfers between devices: 44.6 us -> 41.9 us
  waiting for transfers between devices: 33.9 us -> 35.3 us
    all_to_all x4, waiting for transfers between devices: 19.2 us -> 25.8 us  [all_to_all(): return lax.all_to_all(value, axes, 0, 0, tiled=True)]
    ppermute x12, waiting for transfers between devices: 14.8 us -> 9.5 us  [shifted(): lax.ppermute(value, axis, [(i, (i + shift) % size) for i in range(size)])]
    all_to_all x4, starting transfers between devices: 22.4 us -> 21.1 us  [all_to_all(): return lax.all_to_all(value, axes, 0, 0, tiled=True)]
    ppermute x12, starting transfers between devices: 22.1 us -> 20.8 us  [shifted(): lax.ppermute(value, axis, [(i, (i + shift) % size) for i in range(size)])]
  transfers between devices with their start and end apart: 16 -> 16, of which waited for: 12 -> 9; matrix products, arithmetic and copies ran while one was open for 1% -> 1% of each run, Pallas kernels for 15% -> 18%
where the time goes in v7:
time: 111 us; the launch traced here: 110 us
  starting transfers between devices  41.9 us (38%)
  waiting for transfers between devices  35.3 us (32%)
  Pallas kernels  30.3 us (27%)
    pallas_call x12, Pallas kernels, call(): pl.pallas_call(kernel, in_specs=[spec for spec, _ in ins], out_specs=[spe...  30.3 us
    all_to_all x4, waiting for transfers between devices, all_to_all(): return lax.all_to_all(value, axes, 0, 0, tiled=True)  25.8 us
    all_to_all x4, starting transfers between devices, all_to_all(): return lax.all_to_all(value, axes, 0, 0, tiled=True)  21.1 us
    ppermute x12, starting transfers between devices, shifted(): lax.ppermute(value, axis, [(i, (i + shift) % size) for i in range(size)])  20.8 us
    ppermute x12, waiting for transfers between devices, shifted(): lax.ppermute(value, axis, [(i, (i + shift) % size) for i in range(size)])  9.5 us
  transfers between devices with their start and end apart: 16, of which 9 were waited for; matrix products, arithmetic and copies ran while one was open for 1% of the time, Pallas kernels for 18%

profile of v7, /device:TPU:1, one launch (start us, length us, event | category | flops | bytes accessed | tf_op | source)
XLA Modules:
  0.0 110.0 jit_solution(3905430690823513466)
XLA Ops:
  0.6 0.0 copy-start.6
  0.7 0.0 copy-start.8
  0.7 0.0 copy-start.7
  0.7 0.0 copy-start.5
  0.7 0.0 copy-start
  0.7 0.0 copy-start.1
  0.7 0.0 copy-start.3
  0.7 0.0 copy-start.9
  0.7 0.0 copy-start.10
  0.7 0.0 copy-start.12
  0.8 0.1 stack.23.place
  0.8 6.5 %pair_bias.1.own = bf16[4,128,128]{2,1,0:T(8,128)(2,1)S(1)} custom-call(s32[5]{0:T(128)S(1)} %stack.23.place, bf16[256,2,32,128]{3,2,1,0:T(8,128)(2,1)} %pair.5, f32[1,128]{1,0:T(1,128)} %bitcast.43, bf16[128,512]{1,0:T(8,128)(2,1)} %gate_w.5, bf16[128,512]{1,0:T(8,128)(2,1)} %up_w.5, bf16[512,128]{1,0:T(8,128)(2,1)} %down_w.5, f32[1,128]{1,0:T(1,128)} %bitcast.47, ...), custom_call_target="tpu_custom_call" | custom-call | tf_op jit(solution)/shard_map/pair_bias/pallas_call | solution.py:415
  7.4 3.4 %collective-permute-start.2 = (bf16[4,128,128]{2,1,0:T(8,128)(2,1)S(1)}, bf16[4,128,128]{2,1,0:T(8,128)(2,1)S(1)}, u32[]{:S(2)}, u32[]{:S(2)}) collective-permute-start(bf16[4,128,128]{2,1,0:T(8,128)(2,1)S(1)} %pair_bias.1.own), channel_id=1, source_target_pairs={{0,48},{16,0},{32,16},{48,32},{1,49},{17,1},{33,17},{49,33},{2,50}... | collective-permute-start | bytes 393224 | tf_op jit(solution)/shard_map/ppermute | solution.py:396
  10.8 0.5 collective-permute-start.1
  11.3 0.6 collective-permute-start
  11.9 0.0 copy-done.6
  11.9 0.0 copy-done.7
  11.9 2.2 %products.1 = (f32[1024,256]{1,0:T(8,128)S(1)}, f32[1024,256]{1,0:T(8,128)S(1)}, bf16[256,768]{1,0:T(8,128)(2,1)}, bf16[256,768]{1,0:T(8,128)(2,1)}, bf16[1024,768]{1,0:T(8,128)(2,1)}) custom-call(bf16[256,768]{1,0:T(8,128)(2,1)S(1)} %bitcast.35, bf16[256,768]{1,0:T(8,128)(2,1)S(1)} %bitcast.36, bf16[2,32,768]{2,1,0:T(8,128)(2,1)S(1)} %bitcast.37, ...), custom_call_target="tpu_custom_call" | custom-call | tf_op jit(solution)/shard_map/products/pallas_call | solution.py:415
  14.1 0.2 collective-permute-done.2.third
  14.3 1.9 %collective-permute-done.1.second = bf16[4,128,128]{2,1,0:T(8,128)(2,1)S(1)} collective-permute-done((bf16[4,128,128]{2,1,0:T(8,128)(2,1)S(1)}, bf16[4,128,128]{2,1,0:T(8,128)(2,1)S(1)}, u32[]{:S(2)}, u32[]{:S(2)}) %collective-permute-start.1) | collective-permute-done | bytes 131104 | tf_op jit(solution)/shard_map/ppermute | solution.py:396
  16.2 4.1 %collective-permute-done.first = bf16[4,128,128]{2,1,0:T(8,128)(2,1)S(1)} collective-permute-done((bf16[4,128,128]{2,1,0:T(8,128)(2,1)S(1)}, bf16[4,128,128]{2,1,0:T(8,128)(2,1)S(1)}, u32[]{:S(2)}, u32[]{:S(2)}) %collective-permute-start) | collective-permute-done | bytes 131104 | tf_op jit(solution)/shard_map/ppermute | solution.py:396
  20.3 1.1 %softmax_stats.1 = (f32[1024,256]{1,0:T(8,128)S(1)}, f32[32,256]{1,0:T(8,128)S(1)}) custom-call(s32[5]{0:T(128)S(1)} %stack.23.place, f32[1024,256]{1,0:T(8,128)S(1)} %get-tuple-element.41.scores, f32[1024,256]{1,0:T(8,128)S(1)} %get-tuple-element.42.attend, bf16[4,128,128]{2,1,0:T(8,128)(2,1)S(1)} %pair_bias.1.own, ...), custom_call_target="tpu_custom_call" | custom-call | tf_op jit(solution)/shard_map/softmax_stats/pallas_call | solution.py:415
  21.4 7.0 %collective-permute-start.3 = (f32[32,256]{1,0:T(8,128)S(1)}, f32[32,256]{1,0:T(8,128)S(1)}, u32[]{:S(2)}, u32[]{:S(2)}) collective-permute-start(f32[32,256]{1,0:T(8,128)S(1)} %get-tuple-element.43.own), channel_id=1, source_target_pairs={{0,4},{4,0},{1,5},{5,1},{2,6},{6,2},{3,7},{7,3},{8,12},{12,8},{9,1... | collective-permute-start | bytes 98312 | tf_op jit(solution)/shard_map/ppermute | solution.py:396
  28.5 0.0 copy-done.9
  28.5 4.7 %pair_states.1 = (f32[1024,128]{1,0:T(8,128)}, f32[1024,128]{1,0:T(8,128)}, bf16[1024,512]{1,0:T(8,128)(2,1)}, bf16[1024,512]{1,0:T(8,128)(2,1)}, bf16[128,1024]...) custom-call(s32[5]{0:T(128)S(1)} %stack.23.place, ...), custom_call_target="tpu_custom_call" | custom-call | tf_op jit(solution)/shard_map/pair_states/pallas_call | solution.py:415
  33.2 0.0 collective-permute-done.3.received
  33.2 3.0 %collective-permute-start.6 = (f32[32,256]{1,0:T(8,128)S(1)}, f32[32,256]{1,0:T(8,128)S(1)}, u32[]{:S(2)}, u32[]{:S(2)}) collective-permute-start(f32[32,256]{1,0:T(8,128)S(1)} %merge_stats.1.own), channel_id=1, source_target_pairs={{0,2},{1,3},{2,0},{3,1},{4,6},{5,7},{6,4},{7,5},{8,10},{9,11},{10,... | collective-permute-start | bytes 98312 | tf_op jit(solution)/shard_map/ppermute | solution.py:396
  36.2 0.8 collective-permute-start.5
  37.0 0.7 collective-permute-start.4
  37.7 0.0 collective-permute-done.6.third
  37.7 1.6 %collective-permute-done.5.second = f32[32,256]{1,0:T(8,128)S(1)} collective-permute-done((f32[32,256]{1,0:T(8,128)S(1)}, f32[32,256]{1,0:T(8,128)S(1)}, u32[]{:S(2)}, u32[]{:S(2)}) %collective-permute-start.5) | collective-permute-done | bytes 32800 | tf_op jit(solution)/shard_map/ppermute | solution.py:396
  39.3 1.7 %collective-permute-done.4.first = f32[32,256]{1,0:T(8,128)S(1)} collective-permute-done((f32[32,256]{1,0:T(8,128)S(1)}, f32[32,256]{1,0:T(8,128)S(1)}, u32[]{:S(2)}, u32[]{:S(2)}) %collective-permute-start.4) | collective-permute-done | bytes 32800 | tf_op jit(solution)/shard_map/ppermute | solution.py:396
  40.9 1.5 %score_grads.1 = (bf16[16,128,128]{2,1,0:T(8,128)(2,1)}, bf16[1024,256]{1,0:T(8,128)(2,1)}, bf16[1024,256]{1,0:T(8,128)(2,1)}) custom-call(f32[32,256]{1,0:T(8,128)S(1)} %merge_stats.1.own, f32[32,256]{1,0:T(8,128)S(1)} %collective-permute-done.4.first, f32[32,256]{1,0:T(8,128)S(1)} %collective-permute-done.5.second, ...), custom_call_target="tpu_custom_call" | custom-call | tf_op jit(solution)/shard_map/score_grads/pallas_call | solution.py:415
  42.4 3.6 %all-to-all-start = ((bf16[16,128,128]{2,1,0:T(8,128)(2,1)}), bf16[16,128,128]{2,1,0:T(8,128)(2,1)S(1)}, u32[]{:S(2)}, u32[]{:S(2)}) async-start(bf16[16,128,128]{2,1,0:T(8,128)(2,1)} %get-tuple-element.57), calls=%async_computation | async-start | bytes 1048576 | tf_op jit(solution)/shard_map/all_to_all | solution.py:400
  46.0 3.4 %row_grads.1 = (bf16[2,32,768]{2,1,0:T(8,128)(2,1)S(1)}, bf16[2,32,768]{2,1,0:T(8,128)(2,1)S(1)}, bf16[2,32,768]{2,1,0:T(8,128)(2,1)S(1)}, bf16[2,32,768]{2,1,0:...) custom-call(s32[5]{0:T(128)S(1)} %stack.23.place, bf16[1024,256]{1,0:T(8,128)(2,1)} %get-tuple-element.46.score_low, ...), custom_call_target="tpu_custom_call" | custom-call | tf_op jit(solution)/shard_map/row_grads/pallas_call | solution.py:415
  49.4 0.1 collective-permute-start.8
  49.5 1.9 %collective-permute-start.9 = (bf16[2,32,768]{2,1,0:T(8,128)(2,1)S(1)}, bf16[2,32,768]{2,1,0:T(8,128)(2,1)S(1)}, u32[]{:S(2)}, u32[]{:S(2)}) collective-permute-start(bf16[2,32,768]{2,1,0:T(8,128)(2,1)S(1)} %get-tuple-element.54), channel_id=1, source_target_pairs={{0,2},{1,3},{2,0},{3,1},{4,6},{5,7},{6,4},{7,5},{8,10},{9,11},{10,... | collective-permute-start | bytes 294920 | tf_op jit(solution)/shard_map/ppermute | solution.py:396
  51.4 0.0 collective-permute-start.7
  51.4 6.7 %all-to-all-done.received = bf16[16,128,128]{2,1,0:T(8,128)(2,1)S(1)} async-done(((bf16[16,128,128]{2,1,0:T(8,128)(2,1)}), bf16[16,128,128]{2,1,0:T(8,128)(2,1)S(1)}, u32[]{:S(2)}, u32[]{:S(2)}) %all-to-all-start) | async-done | bytes 524320 | tf_op jit(solution)/shard_map/all_to_all | solution.py:400
  58.1 3.8 %pair_weights.1 = (bf16[1792,128]{1,0:T(8,128)(2,1)}, f32[1024,128]{1,0:T(8,128)}) custom-call(bf16[16,128,128]{2,1,0:T(8,128)(2,1)S(1)} %all-to-all-done.received, bf16[512,128]{1,0:T(8,128)(2,1)S(1)} %copy-done, f32[1,128]{1,0:T(1,128)S(1)} %bitcast.49, bf16[16,128]{1,0:T(8,128)(2,1)S(1)} %bitcast.41, bf16[2,32,768]{2,1,0:T(8,128)(2,1)S(1)} %get-tuple-element.52.after, ...), custom_call_target="tpu_custom_call" | custom-call | tf_op jit(solution)/shard_map/pair_weights/pallas_call | solution.py:415
  61.9 8.0 %all-to-all-start.1 = ((bf16[32,56,128]{2,1,0:T(8,128)(2,1)}), bf16[32,56,128]{2,1,0:T(8,128)(2,1)S(1)}, u32[]{:S(2)}, u32[]{:S(2)}) async-start(bf16[32,56,128]{2,1,0:T(8,128)(2,1)} %bitcast.51), calls=%async_computation.1 | async-start | bytes 917504 | tf_op jit(solution)/shard_map/all_to_all | solution.py:400
  69.9 0.0 collective-permute-done.8
  69.9 0.0 collective-permute-done.9
  69.9 0.0 collective-permute-done.7
  69.9 0.1 convert_add_fusion
  70.0 2.4 %collective-permute-start.10 = (bf16[32,768]{1,0:T(8,128)(2,1)S(1)}, bf16[32,768]{1,0:T(8,128)(2,1)S(1)}, u32[]{:S(2)}, u32[]{:S(2)}) collective-permute-start(bf16[32,768]{1,0:T(8,128)(2,1)S(1)} %fusion.3), channel_id=1, source_target_pairs={{0,4},{4,0},{1,5},{5,1},{2,6},{6,2},{3,7},{7,3},{8,12},{12,8},{9,1... | collective-permute-start | bytes 147464 | tf_op jit(solution)/shard_map/ppermute | solution.py:396
  72.4 0.5 collective-permute-start.11
  72.9 7.6 %all-to-all-done.1.parts = bf16[32,56,128]{2,1,0:T(8,128)(2,1)S(1)} async-done(((bf16[32,56,128]{2,1,0:T(8,128)(2,1)}), bf16[32,56,128]{2,1,0:T(8,128)(2,1)S(1)}, u32[]{:S(2)}, u32[]{:S(2)}) %all-to-all-start.1) | async-done | bytes 458784 | tf_op jit(solution)/shard_map/all_to_all | solution.py:400
  80.5 0.7 plane_sum.1
  81.2 3.6 %all-to-all-start.2 = ((bf16[8,56,128]{2,1,0:T(8,128)(2,1)}), bf16[8,56,128]{2,1,0:T(8,128)(2,1)S(1)}, u32[]{:S(2)}, u32[]{:S(2)}) async-start(bf16[8,56,128]{2,1,0:T(8,128)(2,1)} %plane_sum.1), calls=%async_computation.2 | async-start | bytes 229376 | tf_op jit(solution)/shard_map/all_to_all | solution.py:400
  84.8 0.0 collective-permute-done.10
  84.8 0.6 fusion.2
  85.4 6.1 %all-to-all-done.2.parts = bf16[8,56,128]{2,1,0:T(8,128)(2,1)S(1)} async-done(((bf16[8,56,128]{2,1,0:T(8,128)(2,1)}), bf16[8,56,128]{2,1,0:T(8,128)(2,1)S(1)}, u32[]{:S(2)}, u32[]{:S(2)}) %all-to-all-start.2) | async-done | bytes 114720 | tf_op jit(solution)/shard_map/all_to_all | solution.py:400
  91.6 0.8 column_sum.1.after
  92.4 6.0 %all-to-all-start.3 = ((bf16[32,56,128]{2,1,0:T(8,128)(2,1)}), bf16[32,56,128]{2,1,0:T(8,128)(2,1)S(1)}, u32[]{:S(2)}, u32[]{:S(2)}) async-start(bf16[32,56,128]{2,1,0:T(8,128)(2,1)} %column_sum.1.after), calls=%async_computation.3 | async-start | bytes 917504 | tf_op jit(solution)/shard_map/all_to_all | solution.py:400
  98.4 0.0 collective-permute-done.11
  98.4 0.0 copy-start.2
  98.4 0.0 copy-start.4
  98.4 0.0 copy-start.11
  98.4 0.6 slice_bitcast_fusion.1
  99.1 4.5 %pair_inputs.1 = bf16[16,2,32,128]{3,2,1,0:T(8,128)(2,1)} custom-call(s32[5]{0:T(128)S(1)} %stack.23.place, bf16[32,56,128]{2,1,0:T(8,128)(2,1)} %column_sum.1.after, bf16[256,2,32,128]{3,2,1,0:T(8,128)(2,1)} %pair.5, f32[1024,128]{1,0:T(8,128)} %get-tuple-element.65.updated_grad, bf16[1024,512]{1,0:T(8,128)(2,1)} %get-tuple-element.59.h2.gate_slope, ...), custom_call_target="tpu_custom_call" | custom-call | tf_op jit(solution)/shard_map/pair_inputs/pallas_call | solution.py:415
  103.6 5.4 %all-to-all-done.3 = bf16[32,56,128]{2,1,0:T(8,128)(2,1)S(1)} async-done(((bf16[32,56,128]{2,1,0:T(8,128)(2,1)}), bf16[32,56,128]{2,1,0:T(8,128)(2,1)S(1)}, u32[]{:S(2)}, u32[]{:S(2)}) %all-to-all-start.3) | async-done | bytes 458784 | tf_op jit(solution)/shard_map/all_to_all | solution.py:400
  109.0 0.0 copy-done.2
  109.0 1.0 unpack.1
  (12 shorter events, 0.1 us)
Async XLA Ops:
  0.6 11.3 %copy-start.6 = (bf16[1,256,768]{2,1,0:T(8,128)(2,1)S(1)}, bf16[1,256,768]{2,1,0:T(8,128)(2,1)}, u32[]{:S(2)}) copy-start(bf16[1,256,768]{2,1,0:T(8,128)(2,1)} %param.15) | copy-start | bytes 1179652
  0.7 11.3 %copy-start.8 = (bf16[1,2,32,768]{3,2,1,0:T(8,128)(2,1)S(1)}, bf16[1,2,32,768]{3,2,1,0:T(8,128)(2,1)}, u32[]{:S(2)}) copy-start(bf16[1,2,32,768]{3,2,1,0:T(8,128)(2,1)} %param.14) | copy-start | bytes 294916
  0.7 11.2 %copy-start.7 = (bf16[1,2,32,768]{3,2,1,0:T(8,128)(2,1)S(1)}, bf16[1,2,32,768]{3,2,1,0:T(8,128)(2,1)}, u32[]{:S(2)}) copy-start(bf16[1,2,32,768]{3,2,1,0:T(8,128)(2,1)} %param.13) | copy-start | bytes 294916
  0.7 11.2 %copy-start.5 = (bf16[1,256,768]{2,1,0:T(8,128)(2,1)S(1)}, bf16[1,256,768]{2,1,0:T(8,128)(2,1)}, u32[]{:S(2)}) copy-start(bf16[1,256,768]{2,1,0:T(8,128)(2,1)} %param.12) | copy-start | bytes 1179652
  0.7 27.8 %copy-start = (bf16[512,128]{1,0:T(8,128)(2,1)S(1)}, bf16[512,128]{1,0:T(8,128)(2,1)}, u32[]{:S(2)}) copy-start(bf16[512,128]{1,0:T(8,128)(2,1)} %down_w.5) | copy-start | bytes 393220
  0.7 27.8 %copy-start.1 = (bf16[128,512]{1,0:T(8,128)(2,1)S(1)}, bf16[128,512]{1,0:T(8,128)(2,1)}, u32[]{:S(2)}) copy-start(bf16[128,512]{1,0:T(8,128)(2,1)} %gate_w.5) | copy-start | bytes 393220
  0.7 27.7 %copy-start.3 = (bf16[128,512]{1,0:T(8,128)(2,1)S(1)}, bf16[128,512]{1,0:T(8,128)(2,1)}, u32[]{:S(2)}) copy-start(bf16[128,512]{1,0:T(8,128)(2,1)} %up_w.5) | copy-start | bytes 393220
  0.7 27.7 %copy-start.9 = (bf16[128,16]{0,1:T(8,128)(2,1)S(1)}, bf16[128,16]{0,1:T(8,128)(2,1)}, u32[]{:S(2)}) copy-start(bf16[128,16]{0,1:T(8,128)(2,1)} %param.21) | copy-start | bytes 12292
  0.7 27.7 %copy-start.10 = (f32[128]{0:T(128)S(1)}, f32[128]{0:T(128)}, u32[]{:S(2)}) copy-start(f32[128]{0:T(128)} %param.16) | copy-start | bytes 1540
  0.7 27.7 %copy-start.12 = (f32[128]{0:T(128)S(1)}, f32[128]{0:T(128)}, u32[]{:S(2)}) copy-start(f32[128]{0:T(128)} %param.20) | copy-start | bytes 1540
  7.4 6.9 %collective-permute-start.2 = (bf16[4,128,128]{2,1,0:T(8,128)(2,1)S(1)}, bf16[4,128,128]{2,1,0:T(8,128)(2,1)S(1)}, u32[]{:S(2)}, u32[]{:S(2)}) collective-permute-start(bf16[4,128,128]{2,1,0:T(8,128)(2,1)S(1)} %pair_bias.1.own), channel_id=1, source_target_pairs={{0,48},{16,0},{32,16},{48,32},{1,49},{17,1},{33,17},{49,33},{2,50}... | collective-permute-start | bytes 393224 | tf_op jit(solution)/shard_map/ppermute | solution.py:396
  10.8 5.4 %collective-permute-start.1 = (bf16[4,128,128]{2,1,0:T(8,128)(2,1)S(1)}, bf16[4,128,128]{2,1,0:T(8,128)(2,1)S(1)}, u32[]{:S(2)}, u32[]{:S(2)}) collective-permute-start(bf16[4,128,128]{2,1,0:T(8,128)(2,1)S(1)} %pair_bias.1.own), channel_id=1, source_target_pairs={{0,32},{16,48},{32,0},{48,16},{1,33},{17,49},{33,1},{49,17},{2,34}... | collective-permute-start | bytes 393224 | tf_op jit(solution)/shard_map/ppermute | solution.py:396
  11.3 9.0 %collective-permute-start = (bf16[4,128,128]{2,1,0:T(8,128)(2,1)S(1)}, bf16[4,128,128]{2,1,0:T(8,128)(2,1)S(1)}, u32[]{:S(2)}, u32[]{:S(2)}) collective-permute-start(bf16[4,128,128]{2,1,0:T(8,128)(2,1)S(1)} %pair_bias.1.own), channel_id=1, source_target_pairs={{0,16},{16,32},{32,48},{48,0},{1,17},{17,33},{33,49},{49,1},{2,18}... | collective-permute-start | bytes 393224 | tf_op jit(solution)/shard_map/ppermute | solution.py:396
  21.4 11.7 %collective-permute-start.3 = (f32[32,256]{1,0:T(8,128)S(1)}, f32[32,256]{1,0:T(8,128)S(1)}, u32[]{:S(2)}, u32[]{:S(2)}) collective-permute-start(f32[32,256]{1,0:T(8,128)S(1)} %get-tuple-element.43.own), channel_id=1, source_target_pairs={{0,4},{4,0},{1,5},{5,1},{2,6},{6,2},{3,7},{7,3},{8,12},{12,8},{9,1... | collective-permute-start | bytes 98312 | tf_op jit(solution)/shard_map/ppermute | solution.py:396
  33.2 4.5 %collective-permute-start.6 = (f32[32,256]{1,0:T(8,128)S(1)}, f32[32,256]{1,0:T(8,128)S(1)}, u32[]{:S(2)}, u32[]{:S(2)}) collective-permute-start(f32[32,256]{1,0:T(8,128)S(1)} %merge_stats.1.own), channel_id=1, source_target_pairs={{0,2},{1,3},{2,0},{3,1},{4,6},{5,7},{6,4},{7,5},{8,10},{9,11},{10,... | collective-permute-start | bytes 98312 | tf_op jit(solution)/shard_map/ppermute | solution.py:396
  36.2 3.1 %collective-permute-start.5 = (f32[32,256]{1,0:T(8,128)S(1)}, f32[32,256]{1,0:T(8,128)S(1)}, u32[]{:S(2)}, u32[]{:S(2)}) collective-permute-start(f32[32,256]{1,0:T(8,128)S(1)} %merge_stats.1.own), channel_id=1, source_target_pairs={{0,3},{1,0},{2,1},{3,2},{4,7},{5,4},{6,5},{7,6},{8,11},{9,8},{10,9... | collective-permute-start | bytes 98312 | tf_op jit(solution)/shard_map/ppermute | solution.py:396
  37.0 4.0 %collective-permute-start.4 = (f32[32,256]{1,0:T(8,128)S(1)}, f32[32,256]{1,0:T(8,128)S(1)}, u32[]{:S(2)}, u32[]{:S(2)}) collective-permute-start(f32[32,256]{1,0:T(8,128)S(1)} %merge_stats.1.own), channel_id=1, source_target_pairs={{0,1},{1,2},{2,3},{3,0},{4,5},{5,6},{6,7},{7,4},{8,9},{9,10},{10,1... | collective-permute-start | bytes 98312 | tf_op jit(solution)/shard_map/ppermute | solution.py:396
  42.4 15.7 %all-to-all-start = ((bf16[16,128,128]{2,1,0:T(8,128)(2,1)}), bf16[16,128,128]{2,1,0:T(8,128)(2,1)S(1)}, u32[]{:S(2)}, u32[]{:S(2)}) async-start(bf16[16,128,128]{2,1,0:T(8,128)(2,1)} %get-tuple-element.57), calls=%async_computation | async-start | bytes 1048576 | tf_op jit(solution)/shard_map/all_to_all | solution.py:400
  49.4 20.5 %collective-permute-start.8 = (bf16[2,32,768]{2,1,0:T(8,128)(2,1)S(1)}, bf16[2,32,768]{2,1,0:T(8,128)(2,1)S(1)}, u32[]{:S(2)}, u32[]{:S(2)}) collective-permute-start(bf16[2,32,768]{2,1,0:T(8,128)(2,1)S(1)} %get-tuple-element.53), channel_id=1, source_target_pairs={{0,3},{1,0},{2,1},{3,2},{4,7},{5,4},{6,5},{7,6},{8,11},{9,8},{10,9... | collective-permute-start | bytes 294920 | tf_op jit(solution)/shard_map/ppermute | solution.py:396
  49.5 20.4 %collective-permute-start.9 = (bf16[2,32,768]{2,1,0:T(8,128)(2,1)S(1)}, bf16[2,32,768]{2,1,0:T(8,128)(2,1)S(1)}, u32[]{:S(2)}, u32[]{:S(2)}) collective-permute-start(bf16[2,32,768]{2,1,0:T(8,128)(2,1)S(1)} %get-tuple-element.54), channel_id=1, source_target_pairs={{0,2},{1,3},{2,0},{3,1},{4,6},{5,7},{6,4},{7,5},{8,10},{9,11},{10,... | collective-permute-start | bytes 294920 | tf_op jit(solution)/shard_map/ppermute | solution.py:396
  51.4 18.6 %collective-permute-start.7 = (bf16[2,32,768]{2,1,0:T(8,128)(2,1)S(1)}, bf16[2,32,768]{2,1,0:T(8,128)(2,1)S(1)}, u32[]{:S(2)}, u32[]{:S(2)}) collective-permute-start(bf16[2,32,768]{2,1,0:T(8,128)(2,1)S(1)} %get-tuple-element.52.after), channel_id=1, source_target_pairs={{0,1},{1,2},{2,3},{3,0},{4,5},{5,6},{6,7},{7,4},{8,9},{9,10},{10,1... | collective-permute-start | bytes 294920 | tf_op jit(solution)/shard_map/ppermute | solution.py:396
  61.9 18.6 %all-to-all-start.1 = ((bf16[32,56,128]{2,1,0:T(8,128)(2,1)}), bf16[32,56,128]{2,1,0:T(8,128)(2,1)S(1)}, u32[]{:S(2)}, u32[]{:S(2)}) async-start(bf16[32,56,128]{2,1,0:T(8,128)(2,1)} %bitcast.51), calls=%async_computation.1 | async-start | bytes 917504 | tf_op jit(solution)/shard_map/all_to_all | solution.py:400
  70.0 14.8 %collective-permute-start.10 = (bf16[32,768]{1,0:T(8,128)(2,1)S(1)}, bf16[32,768]{1,0:T(8,128)(2,1)S(1)}, u32[]{:S(2)}, u32[]{:S(2)}) collective-permute-start(bf16[32,768]{1,0:T(8,128)(2,1)S(1)} %fusion.3), channel_id=1, source_target_pairs={{0,4},{4,0},{1,5},{5,1},{2,6},{6,2},{3,7},{7,3},{8,12},{12,8},{9,1... | collective-permute-start | bytes 147464 | tf_op jit(solution)/shard_map/ppermute | solution.py:396
  72.4 26.0 %collective-permute-start.11 = (f32[32,1536]{1,0:T(8,128)S(1)}, f32[32,1536]{1,0:T(8,128)S(1)}, u32[]{:S(2)}, u32[]{:S(2)}) collective-permute-start(f32[32,1536]{1,0:T(8,128)S(1)} %get-tuple-element.56), channel_id=1, source_target_pairs={{0,8},{8,0},{1,9},{9,1},{2,10},{10,2},{3,11},{11,3},{4,12},{12,4},... | collective-permute-start | bytes 589832 | tf_op jit(solution)/shard_map/ppermute | solution.py:396
  81.2 10.3 %all-to-all-start.2 = ((bf16[8,56,128]{2,1,0:T(8,128)(2,1)}), bf16[8,56,128]{2,1,0:T(8,128)(2,1)S(1)}, u32[]{:S(2)}, u32[]{:S(2)}) async-start(bf16[8,56,128]{2,1,0:T(8,128)(2,1)} %plane_sum.1), calls=%async_computation.2 | async-start | bytes 229376 | tf_op jit(solution)/shard_map/all_to_all | solution.py:400
  92.4 16.6 %all-to-all-start.3 = ((bf16[32,56,128]{2,1,0:T(8,128)(2,1)}), bf16[32,56,128]{2,1,0:T(8,128)(2,1)S(1)}, u32[]{:S(2)}, u32[]{:S(2)}) async-start(bf16[32,56,128]{2,1,0:T(8,128)(2,1)} %column_sum.1.after), calls=%async_computation.3 | async-start | bytes 917504 | tf_op jit(solution)/shard_map/all_to_all | solution.py:400
  98.4 10.6 %copy-start.2 = (bf16[128,512]{1,0:T(8,128)(2,1)S(1)}, bf16[128,512]{1,0:T(8,128)(2,1)}, u32[]{:S(2)}) copy-start(bf16[128,512]{1,0:T(8,128)(2,1)} %gate_w.5) | copy-start | bytes 393220
  98.4 10.6 %copy-start.4 = (bf16[128,512]{1,0:T(8,128)(2,1)S(1)}, bf16[128,512]{1,0:T(8,128)(2,1)}, u32[]{:S(2)}) copy-start(bf16[128,512]{1,0:T(8,128)(2,1)} %up_w.5) | copy-start | bytes 393220
  98.4 10.6 %copy-start.11 = (f32[128]{0:T(128)S(1)}, f32[128]{0:T(128)}, u32[]{:S(2)}) copy-start(f32[128]{0:T(128)} %param.16) | copy-start | bytes 1540
